TPU v7x, 32 devices: a whole 2x2x4 slice. The times are simulated.
32 devices in a mesh: grp: 2 (over y), freq: 4 (over z), shot: 2 (over x), rcv: 2 (over core).
Axes of the slice: x: 2, y: 2, z: 4, core: 2. Of those that a mesh axis runs over, the one named last changes fastest.
Arguments:
- data: bfloat16 [2, 256, 32, 4096], P(None, 'freq', ('grp', 'shot'), 'rcv'), parts along dimension 2, may hold values from -6 to 6
- estimate: bfloat16 [2, 256, 32, 4096], P(None, 'freq', ('grp', 'shot'), 'rcv'), parts along dimension 2, may hold values from -0.09375 to 0.09375
- window_data: bfloat16 [2, 256, 32, 16], P(None, 'freq', ('grp', 'shot')), parts along dimension 2, may hold values from -6 to 6
- wavelet: float32 [2, 512], P(None, ('grp', 'freq')), parts along dimension 1, may hold values from -24 to 24
- positions: int32 [32], P(('grp', 'shot')), parts along dimension 0, may hold values from 0 to 4095
- bins: int32 [512], P('grp'), parts along dimension 0, may hold values from 0 to 399
- threshold: int32 [2], P('grp'), parts along dimension 0, may hold values from 8 to 40
- step: float32 [2], P('grp'), parts along dimension 0, may hold values from 0.25 to 1
Outputs:
- primaries: bfloat16 [1024, 32, 4096], P('freq', ('grp', 'shot'), 'rcv'), parts along dimension 1
There are 2 independent parts, one for each index of `grp`. A program takes and returns all parts, laid end to end along the dimension named above; each array names one. Nothing has to cross between parts.
All inputs are finite; a program needn't handle non-finite values.
Results may differ from a plain program's by a relative error of at most 0.0059.
The roundings to bfloat16 on the way count: a program that leaves them out, or rounds other values in their place, can miss the bound.
Values may be sent and summed in bfloat16 or wider, within the bound.
No kernel may reach another device: no remote copies, remote signals or barrier semaphores. Data moves between devices by JAX's collectives and lax.ppermute only.
A program may use at most 64 MiB of HBM per device.

v0:
```python
from functools import partial
import math

import jax
import jax.numpy as jnp
from jax import lax
from jax.sharding import PartitionSpec as P

NF = 256
RCV = 4096
NT = 1024


def make_down(lines, spots, wavelet, offset):
    width = lines.shape[3]
    columns = offset + lax.iota(jnp.int32, width)
    select = (columns[None, None, :] == spots[None, :, None]).astype(jnp.float32)
    down_re = (wavelet[0][:, None, None] * select - lines[0].astype(jnp.float32)).astype(
        jnp.bfloat16
    )
    down_im = (wavelet[1][:, None, None] * select - lines[1].astype(jnp.float32)).astype(
        jnp.bfloat16
    )
    return (down_re, down_im)


def body(data, estimate, window_data, wavelet, positions, bins, threshold, step):
    product = partial(jnp.einsum, preferred_element_type=jnp.float32)
    offset = lax.axis_index("rcv") * data.shape[3]
    shots_all = data.shape[2] * lax.axis_size("shot")
    norm = 1.0 / math.sqrt(shots_all * RCV)
    lines, spots = (
        lax.all_gather(data, "shot", axis=2, tiled=True),
        lax.all_gather(positions, "shot", axis=0, tiled=True),
    )
    down_re, down_im = make_down(lines, spots, wavelet, offset)
    rows_re = estimate[0]
    rows_im = estimate[1]
    model_re = product("frc,fsc->frs", rows_re, down_re) - product("frc,fsc->frs", rows_im, down_im)
    model_im = product("frc,fsc->frs", rows_re, down_im) + product("frc,fsc->frs", rows_im, down_re)
    model_re, model_im = lax.psum((model_re, model_im), "rcv")
    err_re = (window_data[0].astype(jnp.float32) - model_re).astype(jnp.bfloat16)
    err_im = (window_data[1].astype(jnp.float32) - model_im).astype(jnp.bfloat16)
    grad_re = product("frs,fsc->frc", err_re, down_re) + product("frs,fsc->frc", err_im, down_im)
    grad_im = product("frs,fsc->frc", err_im, down_re) - product("frs,fsc->frc", err_re, down_im)
    step_size = step[0]
    upd_re = (estimate[0].astype(jnp.float32) - step_size * (grad_re * norm)).astype(jnp.bfloat16)
    upd_im = (estimate[1].astype(jnp.float32) - step_size * (grad_im * norm)).astype(jnp.bfloat16)
    updated = jnp.stack([upd_re, upd_im], axis=0)
    n_freq = bins.shape[0]
    times = lax.iota(jnp.int32, NT)
    phase = bins[:, None] * times[None, :] % NT
    angle = 2.0 * math.pi / NT * phase.astype(jnp.float32)
    table = jnp.concatenate([jnp.cos(angle), -jnp.sin(angle)], axis=0).astype(jnp.bfloat16)
    level = threshold[0].astype(jnp.float32) / 64.0
    amplitude = math.sqrt(RCV / NF)
    piece = lax.all_to_all(updated, "freq", split_axis=3, concat_axis=1, tiled=True)
    row_count = piece.shape[2]
    col_count = piece.shape[3]
    stacked = piece.reshape(2 * n_freq, row_count * col_count)
    trace = (
        lax.dot_general(
            table, stacked, (((0,), (0,)), ((), ())), preferred_element_type=jnp.float32
        )
        * amplitude
    )
    sparse = (jnp.sign(trace) * jnp.maximum(jnp.abs(trace) - level, 0.0)).astype(jnp.bfloat16)
    sparse = sparse.reshape(NT, row_count, col_count)
    return lax.all_to_all(sparse, "freq", split_axis=0, concat_axis=2, tiled=True)


def solution(mesh):
    return jax.shard_map(
        body,
        mesh=mesh,
        in_specs=(
            P(None, "freq", ("grp", "shot"), "rcv"),
            P(None, "freq", ("grp", "shot"), "rcv"),
            P(None, "freq", ("grp", "shot"), None),
            P(None, ("grp", "freq")),
            P(("grp", "shot")),
            P("grp"),
            P("grp"),
            P("grp"),
        ),
        out_specs=P("freq", ("grp", "shot"), "rcv"),
        check_vma=False,
    )
```

profile of v0, /device:TPU:0, one launch (start us, length us, event | category | flops | bytes accessed | tf_op | source)
XLA Modules:
  0.0 535.6 jit_solution(10995999869594317697)
XLA Ops:
  8.8 5.2 all-reduce
  14.1 101.5 %all-gather.2.cloned.1.call-done = bf16[2,64,16,2048]{3,2,1,0:T(8,128)(2,1)} async-done(((bf16[2,64,8,2048]{3,2,1,0:T(8,128)(2,1)}), bf16[2,64,16,2048]{3,2,1,0:T(8,128)(2,1)}) %all-gather.2.cloned.1.call-update) | async-done | bytes 8388624 | tf_op jit(solution)/shard_map/all_gather | solution.py:33
  115.6 5.3 fusion
  121.0 1.6 fusion.6
  122.6 1.6 fusion.4
  124.1 2.3 fusion.19
  126.4 1.9 fusion.25
  129.3 18.0 %all-reduce.4.cloned.1.call-done = (f32[64,8,16]{2,1,0:T(8,128)}, f32[64,8,16]{2,1,0:T(8,128)}) async-done(((f32[64,8,16]{2,1,0:T(8,128)}, f32[64,8,16]{2,1,0:T(8,128)}), (f32[64,8,16]{2,1,0:T(8,128)}, f32[64,8,16]{2,1,0:T(8,128)})) %all-reduce.4.cloned.1.call-update) | async-done | bytes 65552 | tf_op jit(solution)/shard_map/psum | solution.py:41
  147.3 3.1 fusion.41
  151.6 1.5 copy-done.1
  153.1 1.3 copy-done.5
  156.3 2.3 pad_maximum_fusion
  158.6 13.2 %copy.23 = bf16[2,64,8,2048]{1,2,0,3:T(8,128)(2,1)} copy(bf16[2,64,8,2048]{3,2,1,0:T(8,128)(2,1)} %pad_maximum_fusion) | data formatting | bytes 8388608 | tf_op jit(solution)/shard_map/stack | solution.py:49
  171.8 9.6 %reshape.71 = bf16[4,2,262144]{2,1,0:T(2,128)(2,1)} reshape(bf16[2048,2,8,64]{3,2,1,0:T(8,128)(2,1)} %bitcast.77) | data formatting | bytes 8388608
  181.4 5.0 all-to-all-start
  187.1 4.9 cosine_convert_fusion
  191.9 88.4 %all-to-all-done = bf16[4,2,262144]{2,1,0:T(2,128)(2,1)} async-done(((bf16[4,2,262144]{2,1,0:T(2,128)(2,1)}), bf16[4,2,262144]{2,1,0:T(2,128)(2,1)}, u32[]{:S(2)}, u32[]{:S(2)}) %all-to-all-start) | async-done | bytes 4194336 | tf_op jit(solution)/shard_map/all_to_all | solution.py:57
  280.3 9.3 %reshape.72 = bf16[2048,2,8,64]{3,2,1,0:T(8,128)(2,1)} reshape(bf16[4,2,262144]{2,1,0:T(2,128)(2,1)} %all-to-all-done) | data formatting | bytes 8388608
  289.6 12.0 %copy.24 = bf16[2,64,8,4,512]{4,2,1,3,0:T(8,128)(2,1)} copy(bf16[2,64,8,4,512]{1,2,0,4,3:T(8,128)(2,1)} %bitcast.78) | data formatting | bytes 8388608 | tf_op jit(solution)/shard_map/all_to_all | solution.py:57
  301.6 4.4 copy.28
  306.0 12.1 %multiply_convert_fusion = bf16[1024,4096]{1,0:T(8,128)(2,1)} fusion(bf16[512,4096]{1,0:T(8,128)(2,1)S(1)} %bitcast.83, f32[]{:T(128)} %bitcast.16, bf16[256,1024]{1,0:T(8,128)(2,1)S(1)} %get-tuple-element.12, bf16[256,1024]{1,0:T(8,128)(2,1)S(1)} %get-tuple-element.11), kind=kOutput, calls=%fused_computation | convolution fusion | flops 4326424576 | bytes 13631492 | tf_op jit(solution)/shard_map/dot_general | solution.py:62
  318.1 12.2 %copy.29 = bf16[128,8,8,512]{3,2,1,0:T(8,128)(2,1)} copy(bf16[128,8,8,512]{3,1,2,0:T(8,128)(2,1)} %bitcast.82) | data formatting | bytes 16777216
  330.3 190.4 %all_to_all.33 = bf16[1024,8,512]{2,1,0:T(8,128)(2,1)} all-to-all(bf16[1024,8,512]{2,1,0:T(8,128)(2,1)} %bitcast.79), channel_id=1, replica_groups=mesh['grp'=2,'freq'=4,'shot'=2,'rcv'=2] {'freq'}, dimensions={0} | all-to-all | bytes 16777216 | tf_op jit(solution)/shard_map/all_to_all | solution.py:69
  520.7 8.1 %copy.25 = bf16[4,256,8,512]{3,2,0,1:T(8,128)(2,1)} copy(bf16[4,256,8,512]{3,2,1,0:T(8,128)(2,1)} %bitcast.80) | data formatting | bytes 16777216 | tf_op jit(solution)/shard_map/all_to_all | solution.py:69
  (40 shorter events, 5.1 us)
Async XLA Ops:
  6.5 0.8 copy-start.12
  6.5 2.0 copy-start.11
  6.5 7.5 %copy-start.10 = (f32[2,64]{1,0:T(2,128)S(1)}, f32[2,64]{1,0:T(2,128)}, u32[]{:S(2)}) copy-start(f32[2,64]{1,0:T(2,128)} %param.11) | copy-start | bytes 1540
  6.5 109.1 %all-gather.2.cloned.1.call-start = ((), (), s32[]{:S(2)}) async-start(), calls=%async_computation.2 | async-start | bytes 12582912 | tf_op jit(solution)/shard_map/all_gather | solution.py:33
  7.3 140.1 %all-reduce.4.cloned.1.call-start = ((), (), s32[]{:S(2)}) async-start(), calls=%async_computation.3 | async-start | bytes 1048576 | tf_op jit(solution)/shard_map/psum | solution.py:41
  115.6 5.3 copy-start.4
  121.0 3.2 copy-start.2
  121.0 5.5 %copy-start = (bf16[64,16,2048]{2,1,0:T(8,128)(2,1)}, bf16[64,16,2048]{2,1,0:T(8,128)(2,1)S(1)}, u32[]{:S(2)}) copy-start(bf16[64,16,2048]{2,1,0:T(8,128)(2,1)S(1)} %get-tuple-element.7) | copy-start | bytes 12582916
  126.4 1.9 copy-start.8
  147.3 3.5 copy-start.3
  147.3 3.5 copy-start.7
  150.9 2.2 copy-start.1
  150.9 3.5 copy-start.5
  154.3 1.0 copy-start.6
  181.4 5.7 %copy-start.9 = (s32[256]{0:T(256)S(1)}, s32[256]{0:T(256)}, u32[]{:S(2)}) copy-start(s32[256]{0:T(256)} %param.13) | copy-start | bytes 3076
  181.4 99.0 %all-to-all-start = ((bf16[4,2,262144]{2,1,0:T(2,128)(2,1)}), bf16[4,2,262144]{2,1,0:T(2,128)(2,1)}, u32[]{:S(2)}, u32[]{:S(2)}) async-start(bf16[4,2,262144]{2,1,0:T(2,128)(2,1)} %reshape.71), calls=%async_computation | async-start | bytes 8388608 | tf_op jit(solution)/shard_map/all_to_all | solution.py:57
Sparse Core Ops, SparseCore 0:
  8.9 106.6 all-gather.1
  128.5 18.7 all-reduce.3
where the time goes:
time: 537 us; the launch traced here: 536 us
  waiting for transfers between devices  209 us (39%)
  blocking collectives  196 us (36%)
  local copies, waits for them, and re-layouts  73.1 us (14%)
  matrix products  25.2 us (5%)
  between operations  15.5 us (3%)
  other arithmetic  12.6 us (2%)
    all_to_all x1, blocking collectives, body(): lax.all_to_all(sparse, 'freq', split_axis=0, concat_axis=2, tiled=True)  190 us
    all_gather x1, waiting for transfers between devices, body(): lax.all_gather(data, 'shot', axis=2, tiled=True)  102 us
    all_to_all x1, waiting for transfers between devices, body(): lax.all_to_all(updated, 'freq', split_axis=3, concat_axis=1, tiled=True)  88.4 us
    unnamed x35, local copies, waits for them, and re-layouts  39.8 us
    psum x1, waiting for transfers between devices, body(): model_re, model_im = lax.psum((model_re, model_im), 'rcv')  18 us
    another operation x1, local copies, waits for them, and re-layouts, body(): updated = jnp.stack([upd_re, upd_im], axis=0)  13.2 us
    dot_general x1, matrix products, body(): lax.dot_general(table, stacked, (((0,), (0,)), ((), ())), preferred_eleme...  12.1 us
    all_to_all x1, local copies, waits for them, and re-layouts, body(): lax.all_to_all(updated, 'freq', split_axis=3, concat_axis=1, tiled=True)  12 us
  transfers between devices with their start and end apart: 3, of which 3 were waited for; matrix products, arithmetic and copies ran while one was open for 1% of the time, Pallas kernels for 0%

commit v1 on v0

--- a/solution.py
+++ b/solution.py
@@ -4,11 +4,20 @@
 import jax
 import jax.numpy as jnp
 from jax import lax
+from jax.experimental import pallas as pl
+from jax.experimental.pallas import tpu as pltpu
 from jax.sharding import PartitionSpec as P
 
 NF = 256
 RCV = 4096
 NT = 1024
+
+OCT = 8
+SLAB = 2 * OCT * OCT
+LANES = 128
+TILE = 256
+PARAMS = pltpu.CompilerParams(vmem_limit_bytes=40 * 1024 * 1024)
+TIME_PARAMS = pltpu.CompilerParams(vmem_limit_bytes=60 * 1024 * 1024)
 
 
 def make_down(lines, spots, wavelet, offset):
@@ -24,7 +33,7 @@
     return (down_re, down_im)
 
 
-def body(data, estimate, window_data, wavelet, positions, bins, threshold, step):
+def general_body(data, estimate, window_data, wavelet, positions, bins, threshold, step):
     product = partial(jnp.einsum, preferred_element_type=jnp.float32)
     offset = lax.axis_index("rcv") * data.shape[3]
     shots_all = data.shape[2] * lax.axis_size("shot")
@@ -69,9 +78,445 @@
     return lax.all_to_all(sparse, "freq", split_axis=0, concat_axis=2, tiled=True)
 
 
+VMEM = pltpu.VMEM
+SMEM = pltpu.SMEM
+
+
+def whole(space=VMEM):
+    return pl.BlockSpec(memory_space=space)
+
+
+def natural_slab(ref, g):
+    width = ref.shape[3]
+    return ref[:, pl.ds(g * OCT, OCT)].astype(jnp.float32).reshape(SLAB, width)
+
+
+def down_kernel(first, data_ref, wave_ref, spot_ref, down_ref):
+    width = data_ref.shape[3]
+    row = lax.broadcasted_iota(jnp.int32, (OCT, width), 0)
+    column = lax.broadcasted_iota(jnp.int32, (OCT, width), 1)
+    spot = jnp.full((OCT, width), -1, jnp.int32)
+    for shot in range(OCT):
+        spot = jnp.where(row == shot, spot_ref[shot], spot)
+    select = column == spot
+    for g in range(down_ref.shape[0]):
+        line = natural_slab(data_ref, g)
+        wave = [
+            jnp.where(select, wave_ref[part, first + g * OCT + f], 0.0)
+            for part in range(2)
+            for f in range(OCT)
+        ]
+        down_ref[g] = (jnp.concatenate(wave, axis=0) - line).astype(jnp.bfloat16)
+
+
+def one_hot(shape, target):
+    r = lax.broadcasted_iota(jnp.int32, shape, 0)
+    c = lax.broadcasted_iota(jnp.int32, shape, 1)
+    return target(r, c).astype(jnp.bfloat16)
+
+
+def rows_kernel(side_ref, est_ref, win_ref, down_ref, rows_ref, model_ref, wide_ref):
+    order = one_hot(
+        (SLAB, SLAB),
+        lambda r, c: c
+        == ((r // OCT) % 2) * (OCT * OCT) + (r % OCT) * OCT + r // (2 * OCT),
+    )
+    half = OCT * OCT
+    turn = one_hot((half, half), lambda r, c: c == (r % OCT) * OCT + r // OCT)
+    for g in range(rows_ref.shape[0]):
+        est = natural_slab(est_ref, g).astype(jnp.bfloat16)
+        rows = jnp.dot(order, est, preferred_element_type=jnp.float32).astype(jnp.bfloat16)
+        rows_ref[g] = rows
+        model_ref[g] = lax.dot_general(
+            rows, down_ref[g], (((1,), (1,)), ((), ())), preferred_element_type=jnp.float32
+        )
+        win = natural_slab(win_ref, g).astype(jnp.bfloat16)
+        for other in range(2):
+            side = side_ref[0] if other == 0 else 1 - side_ref[0]
+            total = jnp.zeros((half, LANES), jnp.float32)
+            for part in range(2):
+                spread = one_hot(
+                    (2 * OCT, LANES),
+                    lambda r, c: (c // half == part) & (r == side * OCT + c % OCT),
+                )
+                rows_of = jnp.dot(
+                    turn, win[part * half : (part + 1) * half], preferred_element_type=jnp.float32
+                )
+                total += jnp.dot(
+                    rows_of.astype(jnp.bfloat16), spread, preferred_element_type=jnp.float32
+                )
+            wide_ref[g, other] = total
+
+
+def lane_sign(rows, low):
+    lane = lax.broadcasted_iota(jnp.int32, (rows, LANES), 1)
+    return jnp.where(lane < LANES // 2, low, -low)
+
+
+def complex_model(products):
+    half = SLAB // 2
+    split = products.reshape(OCT, 2, OCT, LANES)
+    first = split[:, 0].reshape(half, LANES)
+    second = pltpu.roll(split[:, 1].reshape(half, LANES), LANES // 2, 1)
+    return first + lane_sign(half, -1.0) * second
+
+
+def model_kernel(rows_ref, other_ref, own_model_ref, model_ref):
+    for g in range(rows_ref.shape[0]):
+        other = lax.dot_general(
+            rows_ref[g], other_ref[g], (((1,), (1,)), ((), ())), preferred_element_type=jnp.float32
+        )
+        model_ref[g, 0] = complex_model(own_model_ref[g])
+        model_ref[g, 1] = complex_model(other)
+
+
+def factors(misfit):
+    half = SLAB // 2
+    r = lax.broadcasted_iota(jnp.int32, (half, LANES), 0)
+    c = lax.broadcasted_iota(jnp.int32, (half, LANES), 1)
+    same = r % OCT == (c // OCT) % OCT
+    re = jnp.where(same, misfit.astype(jnp.bfloat16).astype(jnp.float32), 0.0)
+    im = pltpu.roll(re, LANES // 2, 1) * lane_sign(half, 1.0)
+    both = jnp.stack([re.reshape(OCT, OCT, LANES), im.reshape(OCT, OCT, LANES)], axis=1)
+    return both.reshape(SLAB, LANES).astype(jnp.bfloat16)
+
+
+def update_kernel(norm, carried, kept, step_ref, rows_ref, own_ref, other_ref, win_ref, mine_ref, far_ref, *rest):
+    outs = rest[carried + kept :]
+    step = step_ref[0]
+    n = rows_ref.shape[0]
+    if carried:
+        outs[0][pl.ds(n, n)] = rest[0][...]
+    for g in range(n):
+        misfit = win_ref[g] - (mine_ref[g] + far_ref[g])
+        grad = jnp.dot(factors(misfit[0]), own_ref[g], preferred_element_type=jnp.float32)
+        grad += jnp.dot(factors(misfit[1]), other_ref[g], preferred_element_type=jnp.float32)
+        updated = (rows_ref[g].astype(jnp.float32) - step * (grad * norm)).astype(jnp.bfloat16)
+        at = 0
+        for out in outs:
+            width = out.shape[2]
+            out[g] = updated[:, at : at + width]
+            at += width
+
+
+def time_kernel(plan, blocks, aliased, level_ref, table_ref, *rest):
+    n_refs = sum(plan)
+    sources = rest[:n_refs]
+    rest = rest[n_refs + aliased :]
+    outs, scratch = rest[:blocks], rest[blocks]
+    level = level_ref[0]
+    span = outs[0].shape[0]
+    width = outs[0].shape[2]
+    for i in range(OCT):
+        rows = []
+        at = 0
+        for n in plan:
+            for g in range(sources[at].shape[0]):
+                parts = [ref[g, pl.ds(i * 2 * OCT, 2 * OCT), :] for ref in sources[at : at + n]]
+                rows.append(sum(parts[1:], parts[0]))
+            at += n
+        stacked = jnp.concatenate(rows, axis=0)
+        trace = jnp.dot(table_ref[...], stacked, preferred_element_type=jnp.float32)
+        sparse = trace - jnp.clip(trace, -level, level)
+        for b in range(blocks):
+            for c in range(width // LANES):
+                scratch[b, c, pl.ds(i, span, stride=OCT), :] = sparse[
+                    b * span : (b + 1) * span, c * LANES : (c + 1) * LANES
+                ]
+    for b in range(blocks):
+        for c in range(width // LANES):
+            outs[b][:, :, pl.ds(c * LANES, LANES)] = (
+                scratch[b, c].reshape(span, OCT, LANES).astype(jnp.bfloat16)
+            )
+
+
+def pack_kernel(a_ref, b_ref, out_ref):
+    n = a_ref.shape[0]
+    out_ref[pl.ds(0, n)] = a_ref[...]
+    out_ref[pl.ds(n, n)] = b_ref[...]
+
+
+def place_kernel(column, outer_ref, got_ref, _, out_ref, held, sem):
+    @pl.when(outer_ref[0] == 1)
+    def _():
+        take = pltpu.make_async_copy(got_ref, held, sem)
+        take.start()
+        take.wait()
+        put = pltpu.make_async_copy(held, out_ref.at[:, :, pl.ds(column, TILE)], sem)
+        put.start()
+        put.wait()
+
+
+PAIR = ((0, 1), (1, 0), (2, 3), (3, 2))
+INWARD = ((0, 1), (3, 2))
+MIDDLE = ((1, 2), (2, 1))
+OUTWARD = ((1, 0), (2, 3))
+CHUNKS = 4
+RAW_TILES = 2
+
+
+def cost(flops, moved):
+    return pl.CostEstimate(flops=0, bytes_accessed=0, transcendentals=0)
+
+
+def tie(*arrays):
+    return lax.optimization_barrier(arrays)
+
+
+def line_body(data, estimate, window_data, wavelet, positions, bins, threshold, step):
+    f32, bf16 = jnp.float32, jnp.bfloat16
+    sds = jax.ShapeDtypeStruct
+    n_own = data.shape[1]
+    width = data.shape[3]
+    groups = n_own // OCT
+    per = groups // CHUNKS
+    tiles = width // TILE
+    raw = RAW_TILES * TILE
+    early = raw + TILE
+    late = tiles - RAW_TILES - 1
+    z = lax.axis_index("freq")
+    x = lax.axis_index("shot")
+    norm = 1.0 / math.sqrt(2 * OCT * RCV)
+    n_time = NT // 4
+    half = SLAB // 2
+
+    spots = positions - lax.axis_index("rcv") * width
+    side = x.astype(jnp.int32).reshape(1)
+    low = z < 2
+    order = jnp.stack([z, z ^ 1, jnp.where(low, 2, 1), jnp.where(low, 3, 0)])
+    ordered = bins.reshape(4, groups * OCT)[order].reshape(4 * groups, 1, OCT)
+    t = jnp.concatenate(
+        [z * n_time + lax.iota(jnp.int32, n_time), (z ^ 1) * n_time + lax.iota(jnp.int32, n_time)]
+    )
+    phase = t[:, None, None, None] * ordered[None] % NT
+    angle = 2.0 * math.pi / NT * phase.astype(f32)
+    table = jnp.concatenate([jnp.cos(angle), -jnp.sin(angle)], axis=2).astype(bf16)
+    table = (table * math.sqrt(RCV / NF)).astype(bf16).reshape(2 * n_time, 2 * NF)
+    level = threshold.astype(f32) / 64.0
+    outer = ((z == 0) | (z == 3)).astype(jnp.int32).reshape(1)
+
+    def still(shape):
+        return pl.BlockSpec(shape, lambda n: (0,) * len(shape))
+
+    chunk_block = (2, per * OCT, OCT, width)
+    slab = (per, SLAB, width)
+    slab_bytes = per * SLAB * width * 2
+    downs = [
+        pl.pallas_call(
+            partial(down_kernel, k * per * OCT),
+            grid=(1,),
+            in_specs=[
+                pl.BlockSpec(chunk_block, lambda n, k=k: (0, k, 0, 0)),
+                whole(SMEM),
+                whole(SMEM),
+            ],
+            out_specs=still(slab),
+            out_shape=sds(slab, bf16),
+            compiler_params=PARAMS,
+            cost_estimate=cost(0, 2 * slab_bytes),
+            name="down",
+        )(data, wavelet, spots)
+        for k in range(CHUNKS)
+    ]
+    swap_shots = lambda a: lax.ppermute(a, "shot", ((0, 1), (1, 0)))
+    others = [swap_shots(downs[0]), swap_shots(downs[1]), None, None]
+    rows, models, wins = [], [], []
+    for k in range(CHUNKS):
+        e, m, w = pl.pallas_call(
+            rows_kernel,
+            grid=(1,),
+            in_specs=[
+                whole(SMEM),
+                pl.BlockSpec(chunk_block, lambda n, k=k: (0, k, 0, 0)),
+                pl.BlockSpec((2, per * OCT, OCT, 2 * OCT), lambda n, k=k: (0, k, 0, 0)),
+                still(slab),
+            ],
+            out_specs=[still(slab), still((per, SLAB, LANES)), still((per, 2, half, LANES))],
+            out_shape=[
+                sds(slab, bf16),
+                sds((per, SLAB, LANES), f32),
+                sds((per, 2, half, LANES), f32),
+            ],
+            compiler_params=PARAMS,
+            cost_estimate=cost(4 * per * SLAB * SLAB * width, 3 * slab_bytes),
+            name="rows",
+        )(side, estimate, window_data, downs[k])
+        rows.append(e)
+        models.append(m)
+        wins.append(w)
+    others[0], table, *rest = tie(others[0], table, *rows, *models, *wins, *downs)
+    rows, models, wins, downs = (rest[n * CHUNKS : (n + 1) * CHUNKS] for n in range(4))
+
+    send = lambda a, pairs: lax.ppermute(a, "freq", pairs)
+    cut = lambda a: a[:, :, :raw]
+    lates = [None] * late
+    packed, swaps, mids = ([None] * CHUNKS for _ in range(3))
+    forwards = [None] * (CHUNKS + 2)
+    for k in range(CHUNKS):
+        if k + 2 < CHUNKS:
+            others[k], downs[k + 2] = tie(others[k], downs[k + 2])
+            others[k + 2] = swap_shots(downs[k + 2])
+        mine = pl.pallas_call(
+            model_kernel,
+            in_specs=[whole()] * 3,
+            out_specs=whole(),
+            out_shape=sds((per, 2, half, LANES), f32),
+            compiler_params=PARAMS,
+            cost_estimate=cost(2 * per * SLAB * SLAB * width, 2 * slab_bytes),
+            name="model",
+        )(rows[k], others[k], models[k])
+        far = lax.ppermute(mine, "rcv", ((0, 1), (1, 0)))
+        carried, kept = (0, 0) if k == 0 else (1, late)
+        packed[k], *lates = pl.pallas_call(
+            partial(update_kernel, norm, carried, kept),
+            grid=(1,),
+            in_specs=[whole(SMEM), still(slab), still(slab), still(slab)]
+            + [still((per, 2, half, LANES))] * 3
+            + [still((per, SLAB, early))] * carried
+            + [pl.BlockSpec(memory_space=pl.ANY)] * kept,
+            out_specs=[still(((1 + carried) * per, SLAB, early))]
+            + [pl.BlockSpec((per, SLAB, TILE), lambda n, k=k: (k, 0, 0))] * late,
+            out_shape=[sds(((1 + carried) * per, SLAB, early), bf16)]
+            + [sds((groups, SLAB, TILE), bf16)] * late,
+            input_output_aliases={7 + carried + q: 1 + q for q in range(kept)},
+            compiler_params=PARAMS,
+            cost_estimate=cost(4 * per * SLAB * SLAB * width, 4 * slab_bytes),
+            name="update",
+        )(step, rows[k], downs[k], others[k], wins[k], mine, far, *swaps[k - 1 : k], *lates[:kept])
+        if k:
+            packed[k], mids[k - 1], lates[0] = tie(packed[k], mids[k - 1], lates[0])
+        if k >= 2:
+            packed[k], forwards[k - 1] = tie(packed[k], forwards[k - 1])
+        swaps[k] = send(packed[k][:per], PAIR)
+        mids[k] = send(packed[k], MIDDLE)
+        if k:
+            forwards[k] = send(cut(mids[k - 1]), OUTWARD)
+
+    def time_call(sources, plan, specs, table_rows, out, first, grid, name):
+        span = grid * TILE * OCT
+        own_block = pl.BlockSpec((n_time, OCT, TILE), lambda c: (0, 0, first + c))
+        own_shape = sds((n_time, OCT, width), bf16)
+        blocks = table_rows // n_time
+        aliased = 0 if out is None else 1
+        return pl.pallas_call(
+            partial(time_kernel, plan, blocks, aliased),
+            grid=(grid,),
+            in_specs=[whole(SMEM), pl.BlockSpec((table_rows, 2 * NF), lambda c: (0, 0))]
+            + specs
+            + [pl.BlockSpec(memory_space=pl.ANY)] * aliased,
+            out_specs=[own_block] + [still((n_time, OCT, TILE))] * (blocks - 1),
+            out_shape=[own_shape] + [sds((n_time, OCT, TILE), bf16)] * (blocks - 1),
+            input_output_aliases={2 + len(specs): 0} if aliased else {},
+            scratch_shapes=[VMEM((blocks, TILE // LANES, n_time * OCT, LANES), f32)],
+            compiler_params=TIME_PARAMS,
+            cost_estimate=cost(2 * table_rows * 2 * NF * span, (2 * NF + table_rows) * span * 2),
+            name=name,
+        )(level, table, *sources, *([out] * aliased))
+
+    def part(n, c0, grid):
+        return pl.BlockSpec((per, SLAB, TILE), lambda c: (n, 0, c0 + c if grid else c0))
+
+    last = CHUNKS - 1
+
+    def chunk_sources(c0, grid):
+        own = [(packed[k], part(0, c0, grid)) for k in range(CHUNKS)]
+        swap = [(swaps[k], part(0, c0, grid)) for k in range(CHUNKS)]
+        mid = [(mids[k], part(0, c0, grid)) for k in range(CHUNKS)]
+        cross = [(mids[k + 1], part(1, c0, grid)) for k in range(last)]
+        cross.append((cross_last, part(0, c0, grid)))
+        return own, swap, mid, cross
+
+    def early_time(out):
+        sources = sum(chunk_sources(RAW_TILES, False), [])
+        arrays, specs = zip(*sources)
+        plan = [1] * len(arrays)
+        return time_call(
+            arrays, plan, list(specs), 2 * n_time, out, RAW_TILES, 1, "time_early"
+        )
+
+    def late_time(q, out):
+        sources = [lates[q], swaps_in[q], mids_in[q]]
+        specs = [still(a.shape) for a in sources]
+        return time_call(
+            sources, [1] * 3, specs, 2 * n_time, out, RAW_TILES + 1 + q, 1, "time_late"
+        )
+
+    def raw_time(out):
+        own, swap, mid, cross = chunk_sources(0, True)
+        mid_far = [(forwards[k + 1], part(0, 0, True)) for k in range(CHUNKS)]
+        cross_far = [(forwards[k + 2], part(1 if k < last else 0, 0, True)) for k in range(CHUNKS)]
+        sources = own + swap
+        for near, far in zip(mid + cross, mid_far + cross_far):
+            sources = sources + [near, far]
+        arrays, specs = zip(*sources)
+        plan = [1] * (2 * CHUNKS) + [2] * (2 * CHUNKS)
+        return time_call(arrays, plan, list(specs), n_time, out, 0, RAW_TILES, "time_raw")[0]
+
+    def place(j, got, out):
+        return pl.pallas_call(
+            partial(place_kernel, (RAW_TILES + j) * TILE),
+            in_specs=[whole(SMEM), whole(pl.ANY), whole(pl.ANY)],
+            out_specs=whole(pl.ANY),
+            out_shape=sds((n_time, OCT, width), bf16),
+            input_output_aliases={2: 0},
+            scratch_shapes=[VMEM((n_time, OCT, TILE), bf16), pltpu.SemaphoreType.DMA(())],
+            compiler_params=PARAMS,
+            cost_estimate=cost(0, 3 * n_time * OCT * TILE * 2),
+            name="place",
+        )(outer, got, out)
+
+    def pack(a, b):
+        n = a.shape[0]
+        return pl.pallas_call(
+            pack_kernel,
+            grid=(1,),
+            in_specs=[still(a.shape)] * 2,
+            out_specs=still((2 * n,) + a.shape[1:]),
+            out_shape=sds((2 * n,) + a.shape[1:], bf16),
+            compiler_params=PARAMS,
+            cost_estimate=cost(0, 0),
+            name="pack",
+        )(a, b)
+
+    ends = [None] * (late + 1)
+    swaps_in, mids_in = ([None] * late for _ in range(2))
+    swaps_in[0] = send(lates[0], INWARD)
+    cross_last = send(swaps[last], MIDDLE)
+    mids[last], swaps_in[0], forwards[last], lates[1] = tie(
+        mids[last], swaps_in[0], forwards[last], lates[1]
+    )
+    forwards[CHUNKS] = send(cut(mids[last]), OUTWARD)
+    mids_in[0] = send(pack(lates[0], swaps_in[0]), MIDDLE)
+    swaps_in[1] = send(lates[1], INWARD)
+    cross_last, mids[last] = tie(cross_last, mids[last])
+    out, theirs = early_time(None)
+    ends[0] = send(theirs, OUTWARD)
+    cross_last, out, forwards[CHUNKS] = tie(cross_last, out, forwards[CHUNKS])
+    forwards[CHUNKS + 1] = send(cut(cross_last), OUTWARD)
+    for q in range(late):
+        if q + 1 < late:
+            swaps_in[q + 1], out = tie(swaps_in[q + 1], out)
+            mids_in[q + 1] = send(pack(lates[q + 1], swaps_in[q + 1]), MIDDLE)
+            if q + 2 < late:
+                lates[q + 2], swaps_in[q + 1] = tie(lates[q + 2], swaps_in[q + 1])
+                swaps_in[q + 2] = send(lates[q + 2], INWARD)
+            mids_in[q], swaps_in[q + 1] = tie(mids_in[q], swaps_in[q + 1])
+        if q:
+            ends[q - 1], mids_in[q] = tie(ends[q - 1], mids_in[q])
+            out = place(q - 1, ends[q - 1], out)
+        if q == 1:
+            out = raw_time(out)
+        out, theirs = late_time(q, out)
+        ends[q + 1] = send(theirs, OUTWARD)
+    for j in range(late - 1, late + 1):
+        out = place(j, ends[j], out)
+    return out
+
+
 def solution(mesh):
+    line = mesh.shape["freq"] == 4 and mesh.shape["shot"] == 2 and mesh.shape["rcv"] == 2
     return jax.shard_map(
-        body,
+        line_body if line else general_body,
         mesh=mesh,
         in_specs=(
             P(None, "freq", ("grp", "shot"), "rcv"),

time: 537 us -> 308 us (0.57)
  blocking collectives: 196 us -> 0 us
  waiting for transfers between devices: 209 us -> 124 us
  starting transfers between devices: 5.05 us -> 81.4 us
  Pallas kernels: 0 us -> 71.1 us
  local copies, waits for them, and re-layouts: 73.1 us -> 23.5 us
  matrix products: 25.2 us -> 0 us
  between operations: 15.5 us -> 2.29 us
  other arithmetic: 12.6 us -> 4.06 us
    all_to_all x1 -> x0, blocking collectives: 190 us -> none  [body(): lax.all_to_all(sparse, 'freq', split_axis=0, concat_axis=2, tiled=True)]
    ppermute x0 -> x38, waiting for transfers between devices: none -> 124 us  [the longest x30 91.5 us: line_body(): send = lambda a, pairs: lax.ppermute(a, 'freq', pairs)]
    all_gather x1 -> x0, waiting for transfers between devices: 102 us -> none  [body(): lax.all_gather(data, 'shot', axis=2, tiled=True)]
    all_to_all x1 -> x0, waiting for transfers between devices: 88.4 us -> none  [body(): lax.all_to_all(updated, 'freq', split_axis=3, concat_axis=1, tiled=True)]
    ppermute x0 -> x38, starting transfers between devices: none -> 81.4 us  [the longest x30 75.2 us: line_body(): send = lambda a, pairs: lax.ppermute(a, 'freq', pairs)]
    pallas_call x0 -> x34, Pallas kernels: none -> 71.1 us  [the longest x7 32.2 us: time_call(): pl.pallas_call(partial(time_kernel, plan, blocks, aliased), grid=(grid,),...]
    dot_general x9 -> x0, matrix products: 25.2 us -> none  [the longest x1 12.1 us: body(): lax.dot_general(table, stacked, (((0,), (0,)), ((), ())), preferred_eleme...]
    unnamed x35 -> x89, local copies, waits for them, and re-layouts: 39.8 us -> 19 us
  transfers between devices with their start and end apart: 3 -> 38, of which waited for: 3 -> 19; matrix products, arithmetic and copies ran while one was open for 1% -> 3% of each run, Pallas kernels for 0% -> 22%
where the time goes in v1:
time: 308 us; the launch traced here: 306 us
  waiting for transfers between devices  124 us (40%)
  starting transfers between devices  81.4 us (26%)
  Pallas kernels  71.1 us (23%)
  local copies, waits for them, and re-layouts  23.5 us (8%)
  other arithmetic  4.06 us (1%)
    ppermute x30, waiting for transfers between devices, line_body(): send = lambda a, pairs: lax.ppermute(a, 'freq', pairs)  91.5 us
    ppermute x30, starting transfers between devices, line_body(): send = lambda a, pairs: lax.ppermute(a, 'freq', pairs)  75.2 us
    pallas_call x7, Pallas kernels, time_call(): pl.pallas_call(partial(time_kernel, plan, blocks, aliased), grid=(grid,),...  32.2 us
    ppermute x4, waiting for transfers between devices, line_body(): swap_shots = lambda a: lax.ppermute(a, 'shot', ((0, 1), (1, 0)))  27.8 us
    unnamed x89, local copies, waits for them, and re-layouts  19 us
    pallas_call x6, Pallas kernels, place(): pl.pallas_call(partial(place_kernel, (RAW_TILES + j) * TILE), in_specs=[w...  9.76 us
    pallas_call x4, Pallas kernels, line_body(): pl.pallas_call(partial(update_kernel, norm, carried, kept), grid=(1,), in...  6.67 us
    pallas_call x5, Pallas kernels, pack(): pl.pallas_call(pack_kernel, grid=(1,), in_specs=[still(a.shape)] * 2, out...  6.58 us
  transfers between devices with their start and end apart: 38, of which 19 were waited for; matrix products, arithmetic and copies ran while one was open for 3% of the time, Pallas kernels for 22%

profile of v1, /device:TPU:0, one launch (start us, length us, event | category | flops | bytes accessed | tf_op | source)
XLA Modules:
  0.0 306.4 jit_solution(3713020506754995820)
XLA Ops:
  45.0 10.0 %collective-permute-done.1.other_ref = bf16[2,128,2048]{2,1,0:T(8,128)(2,1)} collective-permute-done((bf16[2,128,2048]{2,1,0:T(8,128)(2,1)}, bf16[2,128,2048]{2,1,0:T(8,128)(2,1)}, u32[]{:S(2)}, u32[]{:S(2)}) %collective-permute-start.1) | collective-permute-done | bytes 1048608 | tf_op jit(solution)/shard_map/ppermute | solution.py:321
  61.5 5.0 %collective-permute-start.10 = (bf16[2,128,768]{2,1,0:T(8,128)(2,1)S(1)}, bf16[2,128,768]{2,1,0:T(8,128)(2,1)S(1)}, u32[]{:S(2)}, u32[]{:S(2)}) collective-permute-start(bf16[2,128,768]{2,1,0:T(8,128)(2,1)S(1)} %slice.24), channel_id=1, source_target_pairs={{0,4},{4,0},{8,12},{12,8},{1,5},{5,1},{9,13},{13,9},{2,6},{6,2},{1... | collective-permute-start | bytes 1179656 | tf_op jit(solution)/shard_map/ppermute | solution.py:350
  69.3 8.1 %collective-permute-done.4.other_ref = bf16[2,128,2048]{2,1,0:T(8,128)(2,1)S(1)} collective-permute-done((bf16[2,128,2048]{2,1,0:T(8,128)(2,1)S(1)}, bf16[2,128,2048]{2,1,0:T(8,128)(2,1)S(1)}, u32[]{:S(2)}, u32[]{:S(2)}) %collective-permute-start.4) | collective-permute-done | bytes 1048608 | tf_op jit(solution)/shard_map/ppermute | solution.py:321
  83.3 6.0 %collective-permute-start.13 = (bf16[2,128,768]{2,1,0:T(8,128)(2,1)S(1)}, bf16[2,128,768]{2,1,0:T(8,128)(2,1)S(1)}, u32[]{:S(2)}, u32[]{:S(2)}) collective-permute-start(bf16[2,128,768]{2,1,0:T(8,128)(2,1)S(1)} %slice.26), channel_id=1, source_target_pairs={{0,4},{4,0},{8,12},{12,8},{1,5},{5,1},{9,13},{13,9},{2,6},{6,2},{1... | collective-permute-start | bytes 1179656 | tf_op jit(solution)/shard_map/ppermute | solution.py:350
  89.4 9.7 %collective-permute-done.2.other_ref = bf16[2,128,2048]{2,1,0:T(8,128)(2,1)S(1)} collective-permute-done((bf16[2,128,2048]{2,1,0:T(8,128)(2,1)S(1)}, bf16[2,128,2048]{2,1,0:T(8,128)(2,1)S(1)}, u32[]{:S(2)}, u32[]{:S(2)}) %collective-permute-start.2) | collective-permute-done | bytes 1048608 | tf_op jit(solution)/shard_map/ppermute | solution.py:321
  100.9 7.8 %collective-permute-done.13.rest_0_.rest_6_ = bf16[2,128,768]{2,1,0:T(8,128)(2,1)S(1)} collective-permute-done((bf16[2,128,768]{2,1,0:T(8,128)(2,1)S(1)}, bf16[2,128,768]{2,1,0:T(8,128)(2,1)S(1)}, u32[]{:S(2)}, u32[]{:S(2)}) %collective-permute-start.13) | collective-permute-done | bytes 393248 | tf_op jit(solution)/shard_map/ppermute | solution.py:350
  111.4 3.1 %collective-permute-start.17 = (bf16[8,128,256]{2,1,0:T(8,128)(2,1)S(1)}, bf16[8,128,256]{2,1,0:T(8,128)(2,1)S(1)}, u32[]{:S(2)}, u32[]{:S(2)}) collective-permute-start(bf16[8,128,256]{2,1,0:T(8,128)(2,1)S(1)} %get-tuple-element.193.a_ref.rest_0_), channel_id=1, source_target_pairs={{0,4},{12,8},{1,5},{13,9},{2,6},{14,10},{3,7},{15,11},{16,20},{28,... | collective-permute-start | bytes 1572872 | tf_op jit(solution)/shard_map/ppermute | solution.py:350
  118.8 8.0 %collective-permute-done.17.b_ref.rest_1_ = bf16[8,128,256]{2,1,0:T(8,128)(2,1)S(1)} collective-permute-done((bf16[8,128,256]{2,1,0:T(8,128)(2,1)S(1)}, bf16[8,128,256]{2,1,0:T(8,128)(2,1)S(1)}, u32[]{:S(2)}, u32[]{:S(2)}) %collective-permute-start.17) | collective-permute-done | bytes 524320 | tf_op jit(solution)/shard_map/ppermute | solution.py:350
  126.9 4.5 %collective-permute-done.18.rest_13_.rest_19_ = bf16[4,128,512]{2,1,0:T(8,128)(2,1)S(1)} collective-permute-done((bf16[4,128,512]{2,1,0:T(8,128)(2,1)S(1)}, bf16[4,128,512]{2,1,0:T(8,128)(2,1)S(1)}, u32[]{:S(2)}, u32[]{:S(2)}) %collective-permute-start.18) | collective-permute-done | bytes 524320 | tf_op jit(solution)/shard_map/ppermute | solution.py:350
  133.6 5.3 %collective-permute-start.19 = (bf16[8,128,256]{2,1,0:T(8,128)(2,1)S(1)}, bf16[8,128,256]{2,1,0:T(8,128)(2,1)S(1)}, u32[]{:S(2)}, u32[]{:S(2)}) collective-permute-start(bf16[8,128,256]{2,1,0:T(8,128)(2,1)S(1)} %get-tuple-element.196.a_ref.rest_0_), channel_id=1, source_target_pairs={{0,4},{12,8},{1,5},{13,9},{2,6},{14,10},{3,7},{15,11},{16,20},{28,... | collective-permute-start | bytes 1572872 | tf_op jit(solution)/shard_map/ppermute | solution.py:350
  147.5 4.6 %time_early.1 = (bf16[256,8,2048]{2,1,0:T(8,128)(2,1)}, bf16[256,8,256]{2,1,0:T(8,128)(2,1)}) custom-call(f32[1]{0:T(128)S(6)} %div.3.level_ref, bf16[512,512]{1,0:T(8,128)(2,1)} %copy.50.table_ref, bf16[2,128,768]{2,1,0:T(8,128)(2,1)} %copy-done.29, bf16[4,128,768]{2,1,0:T(8,128)(2,1)} %copy-done.14, bf16[4,128,768]{2,1,0:T(8,128)(2,1)} %copy-done.15, ...), custom_call_target="tpu_custom_call" | custom-call | tf_op jit(solution)/shard_map/time_early/pallas_call | solution.py:401
  156.2 11.5 %collective-permute-start.23 = (bf16[8,128,256]{2,1,0:T(8,128)(2,1)S(1)}, bf16[8,128,256]{2,1,0:T(8,128)(2,1)S(1)}, u32[]{:S(2)}, u32[]{:S(2)}) collective-permute-start(bf16[8,128,256]{2,1,0:T(8,128)(2,1)S(1)} %get-tuple-element.203.a_ref.rest_0_), channel_id=1, source_target_pairs={{0,4},{12,8},{1,5},{13,9},{2,6},{14,10},{3,7},{15,11},{16,20},{28,... | collective-permute-start | bytes 1572872 | tf_op jit(solution)/shard_map/ppermute | solution.py:350
  167.7 4.5 %time_late.5 = (bf16[256,8,2048]{2,1,0:T(8,128)(2,1)}, bf16[256,8,256]{2,1,0:T(8,128)(2,1)}) custom-call(f32[1]{0:T(128)S(6)} %div.3.level_ref, bf16[512,512]{1,0:T(8,128)(2,1)} %copy.50.table_ref, bf16[8,128,256]{2,1,0:T(8,128)(2,1)} %copy-done.5, bf16[8,128,256]{2,1,0:T(8,128)(2,1)} %copy-done.27, ...), custom_call_target="tpu_custom_call", output_to_operand_aliasing={{0}: (5, {})} | custom-call | tf_op jit(solution)/shard_map/time_late/pallas_call | solution.py:401
  178.5 11.8 %collective-permute-start.25 = (bf16[8,128,256]{2,1,0:T(8,128)(2,1)S(1)}, bf16[8,128,256]{2,1,0:T(8,128)(2,1)}, u32[]{:S(2)}, u32[]{:S(2)}) collective-permute-start(bf16[8,128,256]{2,1,0:T(8,128)(2,1)S(1)} %get-tuple-element.210.a_ref.rest_0_), channel_id=1, source_target_pairs={{0,4},{12,8},{1,5},{13,9},{2,6},{14,10},{3,7},{15,11},{16,20},{28,... | collective-permute-start | bytes 1572872 | tf_op jit(solution)/shard_map/ppermute | solution.py:350
  194.5 11.3 %collective-permute-done.28.rest_23_ = bf16[2,128,512]{2,1,0:T(8,128)(2,1)S(1)} collective-permute-done((bf16[2,128,512]{2,1,0:T(8,128)(2,1)}, bf16[2,128,512]{2,1,0:T(8,128)(2,1)S(1)}, u32[]{:S(2)}, u32[]{:S(2)}) %collective-permute-start.28) | collective-permute-done | bytes 262176 | tf_op jit(solution)/shard_map/ppermute | solution.py:350
  206.5 5.0 %time_raw.1.rest_3_ = bf16[256,8,2048]{2,1,0:T(8,128)(2,1)} custom-call(f32[1]{0:T(128)S(6)} %div.3.level_ref, bf16[512,512]{1,0:T(8,128)(2,1)} %copy.50.table_ref, bf16[2,128,768]{2,1,0:T(8,128)(2,1)} %copy-done.29, bf16[4,128,768]{2,1,0:T(8,128)(2,1)} %copy-done.14, bf16[4,128,768]{2,1,0:T(8,128)(2,1)} %copy-done.15, ...), custom_call_target="tpu_custom_call", output_to_operand_aliasing={{}: (26, {})} | custom-call | tf_op jit(solution)/shard_map/time_raw/pallas_call | solution.py:401
  211.5 4.5 %time_late.6 = (bf16[256,8,2048]{2,1,0:T(8,128)(2,1)}, bf16[256,8,256]{2,1,0:T(8,128)(2,1)}) custom-call(f32[1]{0:T(128)S(6)} %div.3.level_ref, bf16[512,512]{1,0:T(8,128)(2,1)} %copy.50.table_ref, bf16[8,128,256]{2,1,0:T(8,128)(2,1)} %copy-done.6, bf16[8,128,256]{2,1,0:T(8,128)(2,1)} %copy-done.25, ...), custom_call_target="tpu_custom_call", output_to_operand_aliasing={{0}: (5, {})} | custom-call | tf_op jit(solution)/shard_map/time_late/pallas_call | solution.py:401
  224.9 4.6 %time_late.7 = (bf16[256,8,2048]{2,1,0:T(8,128)(2,1)}, bf16[256,8,256]{2,1,0:T(8,128)(2,1)}) custom-call(f32[1]{0:T(128)S(6)} %div.3.level_ref, bf16[512,512]{1,0:T(8,128)(2,1)} %copy.50.table_ref, bf16[8,128,256]{2,1,0:T(8,128)(2,1)} %copy-done.7, bf16[8,128,256]{2,1,0:T(8,128)(2,1)} %copy-done.26, ...), custom_call_target="tpu_custom_call", output_to_operand_aliasing={{0}: (5, {})} | custom-call | tf_op jit(solution)/shard_map/time_late/pallas_call | solution.py:401
  233.5 16.2 %collective-permute-done.35.got_ref = bf16[256,8,256]{2,1,0:T(8,128)(2,1)} collective-permute-done((bf16[256,8,256]{2,1,0:T(8,128)(2,1)}, bf16[256,8,256]{2,1,0:T(8,128)(2,1)}, u32[]{:S(2)}, u32[]{:S(2)}) %collective-permute-start.35) | collective-permute-done | bytes 1048608 | tf_op jit(solution)/shard_map/ppermute | solution.py:350
  251.9 4.5 %time_late.8 = (bf16[256,8,2048]{2,1,0:T(8,128)(2,1)}, bf16[256,8,256]{2,1,0:T(8,128)(2,1)}) custom-call(f32[1]{0:T(128)S(6)} %div.3.level_ref, bf16[512,512]{1,0:T(8,128)(2,1)} %copy.50.table_ref, bf16[8,128,256]{2,1,0:T(8,128)(2,1)} %copy-done.8, bf16[8,128,256]{2,1,0:T(8,128)(2,1)} %collective-permute-done.25.b_ref.rest_1_, ...), custom_call_target="tpu_custom_call", output_to_operand_aliasing={{0}: (5, {})} | custom-call | tf_op jit(solution)/shard_map/time_late/pallas_call | solution.py:401
  257.7 14.3 %collective-permute-done.33.got_ref = bf16[256,8,256]{2,1,0:T(8,128)(2,1)S(1)} collective-permute-done((bf16[256,8,256]{2,1,0:T(8,128)(2,1)}, bf16[256,8,256]{2,1,0:T(8,128)(2,1)S(1)}, u32[]{:S(2)}, u32[]{:S(2)}) %collective-permute-start.33) | collective-permute-done | bytes 1048608 | tf_op jit(solution)/shard_map/ppermute | solution.py:350
  273.1 4.5 %time_late.9 = (bf16[256,8,2048]{2,1,0:T(8,128)(2,1)}, bf16[256,8,256]{2,1,0:T(8,128)(2,1)}) custom-call(f32[1]{0:T(128)S(6)} %div.3.level_ref, bf16[512,512]{1,0:T(8,128)(2,1)} %copy.50.table_ref, bf16[8,128,256]{2,1,0:T(8,128)(2,1)} %copy-done.9, bf16[8,128,256]{2,1,0:T(8,128)(2,1)} %copy-done.28, ...), custom_call_target="tpu_custom_call", output_to_operand_aliasing={{0}: (5, {})} | custom-call | tf_op jit(solution)/shard_map/time_late/pallas_call | solution.py:401
  278.9 15.1 %collective-permute-done.37.got_ref = bf16[256,8,256]{2,1,0:T(8,128)(2,1)S(1)} collective-permute-done((bf16[256,8,256]{2,1,0:T(8,128)(2,1)}, bf16[256,8,256]{2,1,0:T(8,128)(2,1)S(1)}, u32[]{:S(2)}, u32[]{:S(2)}) %collective-permute-start.37) | collective-permute-done | bytes 1048608 | tf_op jit(solution)/shard_map/ppermute | solution.py:350
  295.0 10.2 %collective-permute-done.36.got_ref = bf16[256,8,256]{2,1,0:T(8,128)(2,1)S(1)} collective-permute-done((bf16[256,8,256]{2,1,0:T(8,128)(2,1)}, bf16[256,8,256]{2,1,0:T(8,128)(2,1)S(1)}, u32[]{:S(2)}, u32[]{:S(2)}) %collective-permute-start.36) | collective-permute-done | bytes 1048608 | tf_op jit(solution)/shard_map/ppermute | solution.py:350
  (194 shorter events, 114.0 us)
Async XLA Ops:
  5.3 27.2 %collective-permute-start = (bf16[2,128,2048]{2,1,0:T(8,128)(2,1)}, bf16[2,128,2048]{2,1,0:T(8,128)(2,1)}, u32[]{:S(2)}, u32[]{:S(2)}) collective-permute-start(bf16[2,128,2048]{2,1,0:T(8,128)(2,1)} %down.4.down_ref.own_ref), channel_id=1, source_target_pairs={{0,2},{2,0},{1,3},{3,1},{4,6},{6,4},{5,7},{7,5},{8,10},{10,8},{9,1... | collective-permute-start | bytes 3145736 | tf_op jit(solution)/shard_map/ppermute | solution.py:321
  10.0 45.0 %collective-permute-start.1 = (bf16[2,128,2048]{2,1,0:T(8,128)(2,1)}, bf16[2,128,2048]{2,1,0:T(8,128)(2,1)}, u32[]{:S(2)}, u32[]{:S(2)}) collective-permute-start(bf16[2,128,2048]{2,1,0:T(8,128)(2,1)} %down.5.down_ref.own_ref), channel_id=1, source_target_pairs={{0,2},{2,0},{1,3},{3,1},{4,6},{6,4},{5,7},{7,5},{8,10},{10,8},{9,1... | collective-permute-start | bytes 3145736 | tf_op jit(solution)/shard_map/ppermute | solution.py:321
  42.8 34.6 %collective-permute-start.4 = (bf16[2,128,2048]{2,1,0:T(8,128)(2,1)S(1)}, bf16[2,128,2048]{2,1,0:T(8,128)(2,1)S(1)}, u32[]{:S(2)}, u32[]{:S(2)}) collective-permute-start(bf16[2,128,2048]{2,1,0:T(8,128)(2,1)S(1)} %copy-done.13), channel_id=1, source_target_pairs={{0,2},{2,0},{1,3},{3,1},{4,6},{6,4},{5,7},{7,5},{8,10},{10,8},{9,1... | collective-permute-start | bytes 3145736 | tf_op jit(solution)/shard_map/ppermute | solution.py:321
  60.7 19.4 %collective-permute-start.11 = (bf16[4,128,768]{2,1,0:T(8,128)(2,1)S(1)}, bf16[4,128,768]{2,1,0:T(8,128)(2,1)S(1)}, u32[]{:S(2)}, u32[]{:S(2)}) collective-permute-start(bf16[4,128,768]{2,1,0:T(8,128)(2,1)S(1)} %get-tuple-element.169.rest_1_), channel_id=1, source_target_pairs={{4,8},{8,4},{5,9},{9,5},{6,10},{10,6},{7,11},{11,7},{20,24},{24,20... | collective-permute-start | bytes 2359304 | tf_op jit(solution)/shard_map/ppermute | solution.py:350
  66.5 32.5 %collective-permute-start.2 = (bf16[2,128,2048]{2,1,0:T(8,128)(2,1)S(1)}, bf16[2,128,2048]{2,1,0:T(8,128)(2,1)S(1)}, u32[]{:S(2)}, u32[]{:S(2)}) collective-permute-start(bf16[2,128,2048]{2,1,0:T(8,128)(2,1)S(1)} %copy-done.11), channel_id=1, source_target_pairs={{0,2},{2,0},{1,3},{3,1},{4,6},{6,4},{5,7},{7,5},{8,10},{10,8},{9,1... | collective-permute-start | bytes 3145736 | tf_op jit(solution)/shard_map/ppermute | solution.py:321
  81.3 28.4 %collective-permute-start.14 = (bf16[4,128,768]{2,1,0:T(8,128)(2,1)S(1)}, bf16[4,128,768]{2,1,0:T(8,128)(2,1)S(1)}, u32[]{:S(2)}, u32[]{:S(2)}) collective-permute-start(bf16[4,128,768]{2,1,0:T(8,128)(2,1)S(1)} %get-tuple-element.179.rest_2_), channel_id=1, source_target_pairs={{4,8},{8,4},{5,9},{9,5},{6,10},{10,6},{7,11},{11,7},{20,24},{24,20... | collective-permute-start | bytes 2359304 | tf_op jit(solution)/shard_map/ppermute | solution.py:350
  82.0 27.7 %collective-permute-start.15 = (bf16[4,128,512]{2,1,0:T(8,128)(2,1)S(1)}, bf16[4,128,512]{2,1,0:T(8,128)(2,1)S(1)}, u32[]{:S(2)}, u32[]{:S(2)}) collective-permute-start(bf16[4,128,512]{2,1,0:T(8,128)(2,1)S(1)} %slice.27), channel_id=1, source_target_pairs={{4,0},{8,12},{5,1},{9,13},{6,2},{10,14},{7,3},{11,15},{20,16},{24,... | collective-permute-start | bytes 1572872 | tf_op jit(solution)/shard_map/ppermute | solution.py:350
  83.3 25.4 %collective-permute-start.13 = (bf16[2,128,768]{2,1,0:T(8,128)(2,1)S(1)}, bf16[2,128,768]{2,1,0:T(8,128)(2,1)S(1)}, u32[]{:S(2)}, u32[]{:S(2)}) collective-permute-start(bf16[2,128,768]{2,1,0:T(8,128)(2,1)S(1)} %slice.26), channel_id=1, source_target_pairs={{0,4},{4,0},{8,12},{12,8},{1,5},{5,1},{9,13},{13,9},{2,6},{6,2},{1... | collective-permute-start | bytes 1179656 | tf_op jit(solution)/shard_map/ppermute | solution.py:350
  110.7 20.6 %collective-permute-start.16 = (bf16[4,128,768]{2,1,0:T(8,128)(2,1)S(1)}, bf16[4,128,768]{2,1,0:T(8,128)(2,1)S(1)}, u32[]{:S(2)}, u32[]{:S(2)}) collective-permute-start(bf16[4,128,768]{2,1,0:T(8,128)(2,1)S(1)} %get-tuple-element.192.rest_3_), channel_id=1, source_target_pairs={{4,8},{8,4},{5,9},{9,5},{6,10},{10,6},{7,11},{11,7},{20,24},{24,20... | collective-permute-start | bytes 2359304 | tf_op jit(solution)/shard_map/ppermute | solution.py:350
  116.1 23.8 %collective-permute-start.20 = (bf16[2,128,768]{2,1,0:T(8,128)(2,1)S(1)}, bf16[2,128,768]{2,1,0:T(8,128)(2,1)}, u32[]{:S(2)}, u32[]{:S(2)}) collective-permute-start(bf16[2,128,768]{2,1,0:T(8,128)(2,1)S(1)} %slice.29), channel_id=1, source_target_pairs={{0,4},{4,0},{8,12},{12,8},{1,5},{5,1},{9,13},{13,9},{2,6},{6,2},{1... | collective-permute-start | bytes 1179656 | tf_op jit(solution)/shard_map/ppermute | solution.py:350
  132.3 19.9 %collective-permute-start.22 = (bf16[4,128,512]{2,1,0:T(8,128)(2,1)}, bf16[4,128,512]{2,1,0:T(8,128)(2,1)}, u32[]{:S(2)}, u32[]{:S(2)}) collective-permute-start(bf16[4,128,512]{2,1,0:T(8,128)(2,1)} %slice.30), channel_id=1, source_target_pairs={{4,0},{8,12},{5,1},{9,13},{6,2},{10,14},{7,3},{11,15},{20,16},{24,... | collective-permute-start | bytes 1572872 | tf_op jit(solution)/shard_map/ppermute | solution.py:350
  133.6 18.6 %collective-permute-start.19 = (bf16[8,128,256]{2,1,0:T(8,128)(2,1)S(1)}, bf16[8,128,256]{2,1,0:T(8,128)(2,1)S(1)}, u32[]{:S(2)}, u32[]{:S(2)}) collective-permute-start(bf16[8,128,256]{2,1,0:T(8,128)(2,1)S(1)} %get-tuple-element.196.a_ref.rest_0_), channel_id=1, source_target_pairs={{0,4},{12,8},{1,5},{13,9},{2,6},{14,10},{3,7},{15,11},{16,20},{28,... | collective-permute-start | bytes 1572872 | tf_op jit(solution)/shard_map/ppermute | solution.py:350
  142.4 25.3 %collective-permute-start.24 = (bf16[16,128,256]{2,1,0:T(8,128)(2,1)}, bf16[16,128,256]{2,1,0:T(8,128)(2,1)}, u32[]{:S(2)}, u32[]{:S(2)}) collective-permute-start(bf16[16,128,256]{2,1,0:T(8,128)(2,1)} %pack.5), channel_id=1, source_target_pairs={{4,8},{8,4},{5,9},{9,5},{6,10},{10,6},{7,11},{11,7},{20,24},{24,20... | collective-permute-start | bytes 3145736 | tf_op jit(solution)/shard_map/ppermute | solution.py:350
  153.2 37.7 %collective-permute-start.27 = (bf16[16,128,256]{2,1,0:T(8,128)(2,1)}, bf16[16,128,256]{2,1,0:T(8,128)(2,1)}, u32[]{:S(2)}, u32[]{:S(2)}) collective-permute-start(bf16[16,128,256]{2,1,0:T(8,128)(2,1)} %pack.6), channel_id=1, source_target_pairs={{4,8},{8,4},{5,9},{9,5},{6,10},{10,6},{7,11},{11,7},{20,24},{24,20... | collective-permute-start | bytes 3145736 | tf_op jit(solution)/shard_map/ppermute | solution.py:350
  154.9 37.4 %collective-permute-start.26 = (bf16[256,8,256]{2,1,0:T(8,128)(2,1)}, bf16[256,8,256]{2,1,0:T(8,128)(2,1)}, u32[]{:S(2)}, u32[]{:S(2)}) collective-permute-start(bf16[256,8,256]{2,1,0:T(8,128)(2,1)} %get-tuple-element.212), channel_id=1, source_target_pairs={{4,0},{8,12},{5,1},{9,13},{6,2},{10,14},{7,3},{11,15},{20,16},{24,... | collective-permute-start | bytes 3145736 | tf_op jit(solution)/shard_map/ppermute | solution.py:350
  156.2 18.2 %collective-permute-start.23 = (bf16[8,128,256]{2,1,0:T(8,128)(2,1)S(1)}, bf16[8,128,256]{2,1,0:T(8,128)(2,1)S(1)}, u32[]{:S(2)}, u32[]{:S(2)}) collective-permute-start(bf16[8,128,256]{2,1,0:T(8,128)(2,1)S(1)} %get-tuple-element.203.a_ref.rest_0_), channel_id=1, source_target_pairs={{0,4},{12,8},{1,5},{13,9},{2,6},{14,10},{3,7},{15,11},{16,20},{28,... | collective-permute-start | bytes 1572872 | tf_op jit(solution)/shard_map/ppermute | solution.py:350
  175.5 47.1 %collective-permute-start.32 = (bf16[16,128,256]{2,1,0:T(8,128)(2,1)}, bf16[16,128,256]{2,1,0:T(8,128)(2,1)}, u32[]{:S(2)}, u32[]{:S(2)}) collective-permute-start(bf16[16,128,256]{2,1,0:T(8,128)(2,1)} %pack.8), channel_id=1, source_target_pairs={{4,8},{8,4},{5,9},{9,5},{6,10},{10,6},{7,11},{11,7},{20,24},{24,20... | collective-permute-start | bytes 3145736 | tf_op jit(solution)/shard_map/ppermute | solution.py:350
  177.2 45.5 %collective-permute-start.31 = (bf16[256,8,256]{2,1,0:T(8,128)(2,1)}, bf16[256,8,256]{2,1,0:T(8,128)(2,1)}, u32[]{:S(2)}, u32[]{:S(2)}) collective-permute-start(bf16[256,8,256]{2,1,0:T(8,128)(2,1)} %get-tuple-element.227), channel_id=1, source_target_pairs={{4,0},{8,12},{5,1},{9,13},{6,2},{10,14},{7,3},{11,15},{20,16},{24,... | collective-permute-start | bytes 3145736 | tf_op jit(solution)/shard_map/ppermute | solution.py:350
  178.5 37.5 %collective-permute-start.25 = (bf16[8,128,256]{2,1,0:T(8,128)(2,1)S(1)}, bf16[8,128,256]{2,1,0:T(8,128)(2,1)}, u32[]{:S(2)}, u32[]{:S(2)}) collective-permute-start(bf16[8,128,256]{2,1,0:T(8,128)(2,1)S(1)} %get-tuple-element.210.a_ref.rest_0_), channel_id=1, source_target_pairs={{0,4},{12,8},{1,5},{13,9},{2,6},{14,10},{3,7},{15,11},{16,20},{28,... | collective-permute-start | bytes 1572872 | tf_op jit(solution)/shard_map/ppermute | solution.py:350
  221.4 28.3 %collective-permute-start.35 = (bf16[256,8,256]{2,1,0:T(8,128)(2,1)}, bf16[256,8,256]{2,1,0:T(8,128)(2,1)}, u32[]{:S(2)}, u32[]{:S(2)}) collective-permute-start(bf16[256,8,256]{2,1,0:T(8,128)(2,1)} %get-tuple-element.240), channel_id=1, source_target_pairs={{4,0},{8,12},{5,1},{9,13},{6,2},{10,14},{7,3},{11,15},{20,16},{24,... | collective-permute-start | bytes 3145736 | tf_op jit(solution)/shard_map/ppermute | solution.py:350
  229.5 42.6 %collective-permute-start.33 = (bf16[256,8,256]{2,1,0:T(8,128)(2,1)}, bf16[256,8,256]{2,1,0:T(8,128)(2,1)S(1)}, u32[]{:S(2)}, u32[]{:S(2)}) collective-permute-start(bf16[256,8,256]{2,1,0:T(8,128)(2,1)} %get-tuple-element.236), channel_id=1, source_target_pairs={{4,0},{8,12},{5,1},{9,13},{6,2},{10,14},{7,3},{11,15},{20,16},{24,... | collective-permute-start | bytes 3145736 | tf_op jit(solution)/shard_map/ppermute | solution.py:350
  231.8 40.2 %collective-permute-start.34 = (bf16[16,128,256]{2,1,0:T(8,128)(2,1)}, bf16[16,128,256]{2,1,0:T(8,128)(2,1)}, u32[]{:S(2)}, u32[]{:S(2)}) collective-permute-start(bf16[16,128,256]{2,1,0:T(8,128)(2,1)} %pack.9), channel_id=1, source_target_pairs={{4,8},{8,4},{5,9},{9,5},{6,10},{10,6},{7,11},{11,7},{20,24},{24,20... | collective-permute-start | bytes 3145736 | tf_op jit(solution)/shard_map/ppermute | solution.py:350
  256.4 37.6 %collective-permute-start.37 = (bf16[256,8,256]{2,1,0:T(8,128)(2,1)}, bf16[256,8,256]{2,1,0:T(8,128)(2,1)S(1)}, u32[]{:S(2)}, u32[]{:S(2)}) collective-permute-start(bf16[256,8,256]{2,1,0:T(8,128)(2,1)} %get-tuple-element.247), channel_id=1, source_target_pairs={{4,0},{8,12},{5,1},{9,13},{6,2},{10,14},{7,3},{11,15},{20,16},{24,... | collective-permute-start | bytes 3145736 | tf_op jit(solution)/shard_map/ppermute | solution.py:350
  277.6 27.6 %collective-permute-start.36 = (bf16[256,8,256]{2,1,0:T(8,128)(2,1)}, bf16[256,8,256]{2,1,0:T(8,128)(2,1)S(1)}, u32[]{:S(2)}, u32[]{:S(2)}) collective-permute-start(bf16[256,8,256]{2,1,0:T(8,128)(2,1)} %get-tuple-element.246), channel_id=1, source_target_pairs={{4,0},{8,12},{5,1},{9,13},{6,2},{10,14},{7,3},{11,15},{20,16},{24,... | collective-permute-start | bytes 3145736 | tf_op jit(solution)/shard_map/ppermute | solution.py:350
  (58 other events, 1245.6 us)

commit v2 on v1

--- a/solution.py
+++ b/solution.py
@@ -17,7 +17,7 @@
 LANES = 128
 TILE = 256
 PARAMS = pltpu.CompilerParams(vmem_limit_bytes=40 * 1024 * 1024)
-TIME_PARAMS = pltpu.CompilerParams(vmem_limit_bytes=60 * 1024 * 1024)
+WIDE_PARAMS = pltpu.CompilerParams(vmem_limit_bytes=60 * 1024 * 1024)
 
 
 def make_down(lines, spots, wavelet, offset):
@@ -99,10 +99,11 @@
     for shot in range(OCT):
         spot = jnp.where(row == shot, spot_ref[shot], spot)
     select = column == spot
+    at = first + pl.program_id(0) * OCT
     for g in range(down_ref.shape[0]):
         line = natural_slab(data_ref, g)
         wave = [
-            jnp.where(select, wave_ref[part, first + g * OCT + f], 0.0)
+            jnp.where(select, wave_ref[part, at + g * OCT + f], 0.0)
             for part in range(2)
             for f in range(OCT)
         ]
@@ -181,13 +182,10 @@
     return both.reshape(SLAB, LANES).astype(jnp.bfloat16)
 
 
-def update_kernel(norm, carried, kept, step_ref, rows_ref, own_ref, other_ref, win_ref, mine_ref, far_ref, *rest):
-    outs = rest[carried + kept :]
+def update_kernel(norm, kept, step_ref, rows_ref, own_ref, other_ref, win_ref, mine_ref, far_ref, *rest):
+    outs = rest[kept:]
     step = step_ref[0]
-    n = rows_ref.shape[0]
-    if carried:
-        outs[0][pl.ds(n, n)] = rest[0][...]
-    for g in range(n):
+    for g in range(rows_ref.shape[0]):
         misfit = win_ref[g] - (mine_ref[g] + far_ref[g])
         grad = jnp.dot(factors(misfit[0]), own_ref[g], preferred_element_type=jnp.float32)
         grad += jnp.dot(factors(misfit[1]), other_ref[g], preferred_element_type=jnp.float32)
@@ -242,7 +240,7 @@
         take = pltpu.make_async_copy(got_ref, held, sem)
         take.start()
         take.wait()
-        put = pltpu.make_async_copy(held, out_ref.at[:, :, pl.ds(column, TILE)], sem)
+        put = pltpu.make_async_copy(held, out_ref.at[:, :, pl.ds(column, held.shape[2])], sem)
         put.start()
         put.wait()
 
@@ -251,7 +249,8 @@
 INWARD = ((0, 1), (3, 2))
 MIDDLE = ((1, 2), (2, 1))
 OUTWARD = ((1, 0), (2, 3))
-CHUNKS = 4
+SIZES = (2, 3, 3)
+CHUNKS = len(SIZES)
 RAW_TILES = 2
 
 
@@ -269,11 +268,13 @@
     n_own = data.shape[1]
     width = data.shape[3]
     groups = n_own // OCT
-    per = groups // CHUNKS
+    first_group = [sum(SIZES[:k]) for k in range(CHUNKS)]
     tiles = width // TILE
     raw = RAW_TILES * TILE
     early = raw + TILE
-    late = tiles - RAW_TILES - 1
+    late_widths = [TILE] * (tiles - RAW_TILES - 2) + [TILE // 2] * 2
+    late = len(late_widths)
+    late_first = [early + sum(late_widths[:q]) for q in range(late)]
     z = lax.axis_index("freq")
     x = lax.axis_index("shot")
     norm = 1.0 / math.sqrt(2 * OCT * RCV)
@@ -284,117 +285,144 @@
     side = x.astype(jnp.int32).reshape(1)
     low = z < 2
     order = jnp.stack([z, z ^ 1, jnp.where(low, 2, 1), jnp.where(low, 3, 0)])
-    ordered = bins.reshape(4, groups * OCT)[order].reshape(4 * groups, 1, OCT)
+    ordered = bins.reshape(4, groups, 1, OCT)[order]
+    ordered = jnp.broadcast_to(ordered, (4, groups, 2, OCT)).reshape(1, 2 * NF)
     t = jnp.concatenate(
         [z * n_time + lax.iota(jnp.int32, n_time), (z ^ 1) * n_time + lax.iota(jnp.int32, n_time)]
     )
-    phase = t[:, None, None, None] * ordered[None] % NT
-    angle = 2.0 * math.pi / NT * phase.astype(f32)
-    table = jnp.concatenate([jnp.cos(angle), -jnp.sin(angle)], axis=2).astype(bf16)
-    table = (table * math.sqrt(RCV / NF)).astype(bf16).reshape(2 * n_time, 2 * NF)
+    angle = 2.0 * math.pi / NT * (t[:, None] * ordered % NT).astype(f32)
+    real = (lax.broadcasted_iota(jnp.int32, (1, 2 * NF), 1) // OCT) % 2 == 0
+    table = jnp.where(real, jnp.cos(angle), -jnp.sin(angle)).astype(bf16)
+    table = (table * math.sqrt(RCV / NF)).astype(bf16)
     level = threshold.astype(f32) / 64.0
     outer = ((z == 0) | (z == 3)).astype(jnp.int32).reshape(1)
 
     def still(shape):
         return pl.BlockSpec(shape, lambda n: (0,) * len(shape))
 
-    chunk_block = (2, per * OCT, OCT, width)
-    slab = (per, SLAB, width)
-    slab_bytes = per * SLAB * width * 2
+    def group(*shape):
+        return pl.BlockSpec((1,) + shape, lambda n: (n,) + (0,) * len(shape))
+
+    def kernel(body, sizes, **options):
+        return pl.pallas_call(body, grid=(sizes,), cost_estimate=cost(0, 0), **options)
+
     downs = [
-        pl.pallas_call(
-            partial(down_kernel, k * per * OCT),
-            grid=(1,),
+        kernel(
+            partial(down_kernel, first_group[k] * OCT),
+            SIZES[k],
             in_specs=[
-                pl.BlockSpec(chunk_block, lambda n, k=k: (0, k, 0, 0)),
+                pl.BlockSpec((2, OCT, OCT, width), lambda n, k=k: (0, first_group[k] + n, 0, 0)),
                 whole(SMEM),
                 whole(SMEM),
             ],
-            out_specs=still(slab),
-            out_shape=sds(slab, bf16),
-            compiler_params=PARAMS,
-            cost_estimate=cost(0, 2 * slab_bytes),
+            out_specs=group(SLAB, width),
+            out_shape=sds((SIZES[k], SLAB, width), bf16),
+            compiler_params=WIDE_PARAMS,
             name="down",
         )(data, wavelet, spots)
         for k in range(CHUNKS)
     ]
-    swap_shots = lambda a: lax.ppermute(a, "shot", ((0, 1), (1, 0)))
-    others = [swap_shots(downs[0]), swap_shots(downs[1]), None, None]
+    others = [lax.ppermute(a, "shot", ((0, 1), (1, 0))) for a in downs]
     rows, models, wins = [], [], []
     for k in range(CHUNKS):
-        e, m, w = pl.pallas_call(
+        e, m, w = kernel(
             rows_kernel,
-            grid=(1,),
+            SIZES[k],
             in_specs=[
                 whole(SMEM),
-                pl.BlockSpec(chunk_block, lambda n, k=k: (0, k, 0, 0)),
-                pl.BlockSpec((2, per * OCT, OCT, 2 * OCT), lambda n, k=k: (0, k, 0, 0)),
-                still(slab),
+                pl.BlockSpec((2, OCT, OCT, width), lambda n, k=k: (0, first_group[k] + n, 0, 0)),
+                pl.BlockSpec((2, OCT, OCT, 2 * OCT), lambda n, k=k: (0, first_group[k] + n, 0, 0)),
+                group(SLAB, width),
             ],
-            out_specs=[still(slab), still((per, SLAB, LANES)), still((per, 2, half, LANES))],
+            out_specs=[group(SLAB, width), group(SLAB, LANES), group(2, half, LANES)],
             out_shape=[
-                sds(slab, bf16),
-                sds((per, SLAB, LANES), f32),
-                sds((per, 2, half, LANES), f32),
+                sds((SIZES[k], SLAB, width), bf16),
+                sds((SIZES[k], SLAB, LANES), f32),
+                sds((SIZES[k], 2, half, LANES), f32),
             ],
-            compiler_params=PARAMS,
-            cost_estimate=cost(4 * per * SLAB * SLAB * width, 3 * slab_bytes),
+            compiler_params=WIDE_PARAMS,
             name="rows",
         )(side, estimate, window_data, downs[k])
         rows.append(e)
         models.append(m)
         wins.append(w)
-    others[0], table, *rest = tie(others[0], table, *rows, *models, *wins, *downs)
-    rows, models, wins, downs = (rest[n * CHUNKS : (n + 1) * CHUNKS] for n in range(4))
+    others[0], table, *prepared = tie(others[0], table, *rows[:2], *models[:2], *wins[:2])
+    rows[:2], models[:2], wins[:2] = prepared[:2], prepared[2:4], prepared[4:]
 
     send = lambda a, pairs: lax.ppermute(a, "freq", pairs)
     cut = lambda a: a[:, :, :raw]
+
+    def pack(a, b, columns):
+        n = a.shape[0]
+        return pl.pallas_call(
+            pack_kernel,
+            grid=(1,),
+            in_specs=[still((n, SLAB, columns))] * 2,
+            out_specs=still((2 * n, SLAB, columns)),
+            out_shape=sds((2 * n, SLAB, columns), bf16),
+            compiler_params=PARAMS,
+            cost_estimate=cost(0, 0),
+            name="pack",
+        )(a, b)
+
     lates = [None] * late
-    packed, swaps, mids = ([None] * CHUNKS for _ in range(3))
-    forwards = [None] * (CHUNKS + 2)
+    earlies, swaps, mids, crosses, near_out, far_out = ([None] * CHUNKS for _ in range(6))
+    last = CHUNKS - 1
     for k in range(CHUNKS):
-        if k + 2 < CHUNKS:
-            others[k], downs[k + 2] = tie(others[k], downs[k + 2])
-            others[k + 2] = swap_shots(downs[k + 2])
-        mine = pl.pallas_call(
+        if k:
+            others[k], swaps[k - 1] = tie(others[k], swaps[k - 1])
+        mine = kernel(
             model_kernel,
-            in_specs=[whole()] * 3,
-            out_specs=whole(),
-            out_shape=sds((per, 2, half, LANES), f32),
+            SIZES[k],
+            in_specs=[group(SLAB, width), group(SLAB, width), group(SLAB, LANES)],
+            out_specs=group(2, half, LANES),
+            out_shape=sds((SIZES[k], 2, half, LANES), f32),
             compiler_params=PARAMS,
-            cost_estimate=cost(2 * per * SLAB * SLAB * width, 2 * slab_bytes),
             name="model",
         )(rows[k], others[k], models[k])
         far = lax.ppermute(mine, "rcv", ((0, 1), (1, 0)))
-        carried, kept = (0, 0) if k == 0 else (1, late)
-        packed[k], *lates = pl.pallas_call(
-            partial(update_kernel, norm, carried, kept),
-            grid=(1,),
-            in_specs=[whole(SMEM), still(slab), still(slab), still(slab)]
-            + [still((per, 2, half, LANES))] * 3
-            + [still((per, SLAB, early))] * carried
-            + [pl.BlockSpec(memory_space=pl.ANY)] * kept,
-            out_specs=[still(((1 + carried) * per, SLAB, early))]
-            + [pl.BlockSpec((per, SLAB, TILE), lambda n, k=k: (k, 0, 0))] * late,
-            out_shape=[sds(((1 + carried) * per, SLAB, early), bf16)]
-            + [sds((groups, SLAB, TILE), bf16)] * late,
-            input_output_aliases={7 + carried + q: 1 + q for q in range(kept)},
+        kept = 0 if k == 0 else late
+        earlies[k], *lates = kernel(
+            partial(update_kernel, norm, kept),
+            SIZES[k],
+            in_specs=[whole(SMEM)]
+            + [group(SLAB, width)] * 3
+            + [group(2, half, LANES)] * 3
+            + [whole(pl.ANY)] * kept,
+            out_specs=[group(SLAB, early)]
+            + [
+                pl.BlockSpec((1, SLAB, w), lambda n, k=k: (first_group[k] + n, 0, 0))
+                for w in late_widths
+            ],
+            out_shape=[sds((SIZES[k], SLAB, early), bf16)]
+            + [sds((groups, SLAB, w), bf16) for w in late_widths],
+            input_output_aliases={7 + q: 1 + q for q in range(kept)},
             compiler_params=PARAMS,
-            cost_estimate=cost(4 * per * SLAB * SLAB * width, 4 * slab_bytes),
             name="update",
-        )(step, rows[k], downs[k], others[k], wins[k], mine, far, *swaps[k - 1 : k], *lates[:kept])
+        )(step, rows[k], downs[k], others[k], wins[k], mine, far, *lates[:kept])
         if k:
-            packed[k], mids[k - 1], lates[0] = tie(packed[k], mids[k - 1], lates[0])
+            earlies[k], mids[k - 1], crosses[k - 1] = tie(
+                earlies[k], mids[k - 1], crosses[k - 1]
+            )
+        if k:
+            earlies[k], near_out[k - 1] = tie(earlies[k], near_out[k - 1])
         if k >= 2:
-            packed[k], forwards[k - 1] = tie(packed[k], forwards[k - 1])
-        swaps[k] = send(packed[k][:per], PAIR)
-        mids[k] = send(packed[k], MIDDLE)
+            earlies[k], far_out[k - 2] = tie(earlies[k], far_out[k - 2])
+        swaps[k] = send(earlies[k], PAIR)
+        mids[k] = send(earlies[k], MIDDLE)
         if k:
-            forwards[k] = send(cut(mids[k - 1]), OUTWARD)
-
-    def time_call(sources, plan, specs, table_rows, out, first, grid, name):
-        span = grid * TILE * OCT
-        own_block = pl.BlockSpec((n_time, OCT, TILE), lambda c: (0, 0, first + c))
+            far_out[k - 1] = send(cut(crosses[k - 1]), OUTWARD)
+        beside = [swaps[k], mids[k], lates[0]]
+        if k == 0:
+            beside += [rows[2], models[2], wins[2]]
+        swaps[k], mids[k], lates[0], *beside = tie(*beside)
+        if k == 0:
+            rows[2], models[2], wins[2] = beside
+        crosses[k] = send(swaps[k], MIDDLE)
+        near_out[k] = send(cut(mids[k]), OUTWARD)
+
+    def time_call(sources, plan, specs, table_rows, out, first, grid, name, wide=TILE):
+        own_block = pl.BlockSpec((n_time, OCT, wide), lambda c: (0, 0, first // wide + c))
         own_shape = sds((n_time, OCT, width), bf16)
         blocks = table_rows // n_time
         aliased = 0 if out is None else 1
@@ -404,106 +432,82 @@
             in_specs=[whole(SMEM), pl.BlockSpec((table_rows, 2 * NF), lambda c: (0, 0))]
             + specs
             + [pl.BlockSpec(memory_space=pl.ANY)] * aliased,
-            out_specs=[own_block] + [still((n_time, OCT, TILE))] * (blocks - 1),
-            out_shape=[own_shape] + [sds((n_time, OCT, TILE), bf16)] * (blocks - 1),
+            out_specs=[own_block] + [still((n_time, OCT, wide))] * (blocks - 1),
+            out_shape=[own_shape] + [sds((n_time, OCT, wide), bf16)] * (blocks - 1),
             input_output_aliases={2 + len(specs): 0} if aliased else {},
-            scratch_shapes=[VMEM((blocks, TILE // LANES, n_time * OCT, LANES), f32)],
-            compiler_params=TIME_PARAMS,
-            cost_estimate=cost(2 * table_rows * 2 * NF * span, (2 * NF + table_rows) * span * 2),
+            scratch_shapes=[VMEM((blocks, wide // LANES, n_time * OCT, LANES), f32)],
+            compiler_params=WIDE_PARAMS,
+            cost_estimate=cost(0, 0),
             name=name,
         )(level, table, *sources, *([out] * aliased))
 
-    def part(n, c0, grid):
-        return pl.BlockSpec((per, SLAB, TILE), lambda c: (n, 0, c0 + c if grid else c0))
-
-    last = CHUNKS - 1
+    def part(k, n, c0, grid):
+        return pl.BlockSpec((SIZES[k], SLAB, TILE), lambda c: (n, 0, c0 + c if grid else c0))
 
     def chunk_sources(c0, grid):
-        own = [(packed[k], part(0, c0, grid)) for k in range(CHUNKS)]
-        swap = [(swaps[k], part(0, c0, grid)) for k in range(CHUNKS)]
-        mid = [(mids[k], part(0, c0, grid)) for k in range(CHUNKS)]
-        cross = [(mids[k + 1], part(1, c0, grid)) for k in range(last)]
-        cross.append((cross_last, part(0, c0, grid)))
-        return own, swap, mid, cross
+        ways = (earlies, swaps, mids, crosses)
+        return [[(way[k], part(k, 0, c0, grid)) for k in range(CHUNKS)] for way in ways]
 
     def early_time(out):
-        sources = sum(chunk_sources(RAW_TILES, False), [])
-        arrays, specs = zip(*sources)
+        arrays, specs = zip(*sum(chunk_sources(RAW_TILES, False), []))
         plan = [1] * len(arrays)
         return time_call(
-            arrays, plan, list(specs), 2 * n_time, out, RAW_TILES, 1, "time_early"
+            arrays, plan, list(specs), 2 * n_time, out, raw, 1, "time_early"
         )
 
     def late_time(q, out):
         sources = [lates[q], swaps_in[q], mids_in[q]]
         specs = [still(a.shape) for a in sources]
+        wide = late_widths[q]
         return time_call(
-            sources, [1] * 3, specs, 2 * n_time, out, RAW_TILES + 1 + q, 1, "time_late"
+            sources, [1] * 3, specs, 2 * n_time, out, late_first[q], 1, "time_late", wide
         )
 
     def raw_time(out):
         own, swap, mid, cross = chunk_sources(0, True)
-        mid_far = [(forwards[k + 1], part(0, 0, True)) for k in range(CHUNKS)]
-        cross_far = [(forwards[k + 2], part(1 if k < last else 0, 0, True)) for k in range(CHUNKS)]
         sources = own + swap
-        for near, far in zip(mid + cross, mid_far + cross_far):
-            sources = sources + [near, far]
+        for way, relayed in ((mid, near_out), (cross, far_out)):
+            for k in range(CHUNKS):
+                sources = sources + [way[k], (relayed[k], part(k, 0, 0, True))]
         arrays, specs = zip(*sources)
         plan = [1] * (2 * CHUNKS) + [2] * (2 * CHUNKS)
         return time_call(arrays, plan, list(specs), n_time, out, 0, RAW_TILES, "time_raw")[0]
 
     def place(j, got, out):
         return pl.pallas_call(
-            partial(place_kernel, (RAW_TILES + j) * TILE),
+            partial(place_kernel, late_first[j - 1] if j else raw),
             in_specs=[whole(SMEM), whole(pl.ANY), whole(pl.ANY)],
             out_specs=whole(pl.ANY),
             out_shape=sds((n_time, OCT, width), bf16),
             input_output_aliases={2: 0},
-            scratch_shapes=[VMEM((n_time, OCT, TILE), bf16), pltpu.SemaphoreType.DMA(())],
+            scratch_shapes=[VMEM(got.shape, bf16), pltpu.SemaphoreType.DMA(())],
             compiler_params=PARAMS,
             cost_estimate=cost(0, 3 * n_time * OCT * TILE * 2),
             name="place",
         )(outer, got, out)
 
-    def pack(a, b):
-        n = a.shape[0]
-        return pl.pallas_call(
-            pack_kernel,
-            grid=(1,),
-            in_specs=[still(a.shape)] * 2,
-            out_specs=still((2 * n,) + a.shape[1:]),
-            out_shape=sds((2 * n,) + a.shape[1:], bf16),
-            compiler_params=PARAMS,
-            cost_estimate=cost(0, 0),
-            name="pack",
-        )(a, b)
-
     ends = [None] * (late + 1)
     swaps_in, mids_in = ([None] * late for _ in range(2))
     swaps_in[0] = send(lates[0], INWARD)
-    cross_last = send(swaps[last], MIDDLE)
-    mids[last], swaps_in[0], forwards[last], lates[1] = tie(
-        mids[last], swaps_in[0], forwards[last], lates[1]
-    )
-    forwards[CHUNKS] = send(cut(mids[last]), OUTWARD)
-    mids_in[0] = send(pack(lates[0], swaps_in[0]), MIDDLE)
+    crosses[last], far_out[last - 1], lates[1] = tie(crosses[last], far_out[last - 1], lates[1])
+    far_out[last] = send(cut(crosses[last]), OUTWARD)
+    out, theirs = early_time(None)
+    theirs, near_out[last], far_out[last] = tie(theirs, near_out[last], far_out[last])
+    ends[0] = send(theirs, OUTWARD)
+    swaps_in[0], out, lates[1] = tie(swaps_in[0], out, lates[1])
+    mids_in[0] = send(pack(lates[0], swaps_in[0], late_widths[0]), MIDDLE)
     swaps_in[1] = send(lates[1], INWARD)
-    cross_last, mids[last] = tie(cross_last, mids[last])
-    out, theirs = early_time(None)
-    ends[0] = send(theirs, OUTWARD)
-    cross_last, out, forwards[CHUNKS] = tie(cross_last, out, forwards[CHUNKS])
-    forwards[CHUNKS + 1] = send(cut(cross_last), OUTWARD)
     for q in range(late):
+        if q:
+            ends[q - 1], out = tie(ends[q - 1], out)
+            out = place(q - 1, ends[q - 1], out)
         if q + 1 < late:
             swaps_in[q + 1], out = tie(swaps_in[q + 1], out)
-            mids_in[q + 1] = send(pack(lates[q + 1], swaps_in[q + 1]), MIDDLE)
-            if q + 2 < late:
-                lates[q + 2], swaps_in[q + 1] = tie(lates[q + 2], swaps_in[q + 1])
-                swaps_in[q + 2] = send(lates[q + 2], INWARD)
-            mids_in[q], swaps_in[q + 1] = tie(mids_in[q], swaps_in[q + 1])
-        if q:
-            ends[q - 1], mids_in[q] = tie(ends[q - 1], mids_in[q])
-            out = place(q - 1, ends[q - 1], out)
+            mids_in[q + 1] = send(pack(lates[q + 1], swaps_in[q + 1], late_widths[q + 1]), MIDDLE)
+        if q + 2 < late:
+            lates[q + 2], swaps_in[q + 1] = tie(lates[q + 2], swaps_in[q + 1])
+            swaps_in[q + 2] = send(lates[q + 2], INWARD)
+            mids_in[q], swaps_in[q + 2] = tie(mids_in[q], swaps_in[q + 2])
         if q == 1:
             out = raw_time(out)
         out, theirs = late_time(q, out)

time: 308 us -> 300 us (0.974)
  waiting for transfers between devices: 124 us -> 112 us
  Pallas kernels: 71.1 us -> 82.8 us
  starting transfers between devices: 81.4 us -> 76 us
  local copies, waits for them, and re-layouts: 23.5 us -> 18.1 us
    ppermute x4 -> x3, waiting for transfers between devices: 27.8 us -> 14 us  [line_body(): others = [lax.ppermute(a, 'shot', ((0, 1), (1, 0))) for a in downs]]
    pallas_call x27 -> x25, Pallas kernels: 38.9 us -> 47.5 us  [the longest x3 12.1 us: line_body(): kernel(rows_kernel, SIZES[k], in_specs=[whole(SMEM), pl.BlockSpec((2, OCT...]
    mul x1, other arithmetic: 0.86 us -> 5.62 us  [line_body(): table = (table * math.sqrt(RCV / NF)).astype(bf16)]
    unnamed x89 -> x93, local copies, waits for them, and re-layouts: 19 us -> 14.7 us
    ppermute x30 -> x34, starting transfers between devices: 75.2 us -> 71.3 us  [line_body(): send = lambda a, pairs: lax.ppermute(a, 'freq', pairs)]
    pallas_call x7 -> x8, Pallas kernels: 32.2 us -> 35.4 us  [time_call(): pl.pallas_call(partial(time_kernel, plan, blocks, aliased), grid=(grid,),...]
    ppermute x30 -> x34, waiting for transfers between devices: 91.5 us -> 94.3 us  [line_body(): send = lambda a, pairs: lax.ppermute(a, 'freq', pairs)]
  transfers between devices with their start and end apart: 38 -> 40, of which waited for: 19 -> 21; matrix products, arithmetic and copies ran while one was open for 3% -> 3% of each run, Pallas kernels for 22% -> 27%
where the time goes in v2:
time: 300 us; the launch traced here: 298 us
  waiting for transfers between devices  112 us (37%)
  Pallas kernels  82.8 us (28%)
  starting transfers between devices  76 us (25%)
  local copies, waits for them, and re-layouts  18.1 us (6%)
  other arithmetic  6.89 us (2%)
    ppermute x34, waiting for transfers between devices, line_body(): send = lambda a, pairs: lax.ppermute(a, 'freq', pairs)  94.3 us
    ppermute x34, starting transfers between devices, line_body(): send = lambda a, pairs: lax.ppermute(a, 'freq', pairs)  71.3 us
    pallas_call x8, Pallas kernels, time_call(): pl.pallas_call(partial(time_kernel, plan, blocks, aliased), grid=(grid,),...  35.4 us
    unnamed x93, local copies, waits for them, and re-layouts  14.7 us
    ppermute x3, waiting for transfers between devices, line_body(): others = [lax.ppermute(a, 'shot', ((0, 1), (1, 0))) for a in downs]  14 us
    pallas_call x3, Pallas kernels, line_body(): kernel(rows_kernel, SIZES[k], in_specs=[whole(SMEM), pl.BlockSpec((2, OCT...  12.1 us
    pallas_call x3, Pallas kernels, line_body(): kernel(partial(down_kernel, first_group[k] * OCT), SIZES[k], in_specs=[pl...  9.27 us
    pallas_call x7, Pallas kernels, place(): pl.pallas_call(partial(place_kernel, late_first[j - 1] if j else raw), in...  9.27 us
  transfers between devices with their start and end apart: 40, of which 21 were waited for; matrix products, arithmetic and copies ran while one was open for 3% of the time, Pallas kernels for 27%

profile of v2, /device:TPU:0, one launch (start us, length us, event | category | flops | bytes accessed | tf_op | source)
XLA Modules:
  0.0 297.9 jit_solution(4137287136929142617)
XLA Ops:
  10.7 4.4 %rows.4 = (bf16[3,128,2048]{2,1,0:T(8,128)(2,1)}, f32[3,128,128]{2,1,0:T(8,128)}, f32[3,2,64,128]{3,2,1,0:T(8,128)}) custom-call(s32[1]{0:T(128)} %bitcast.6.side_ref, bf16[2,64,8,2048]{3,2,1,0:T(8,128)(2,1)} %est_ref.5, bf16[2,64,8,16]{3,2,1,0:T(8,128)(2,1)} %copy.35.win_ref, bf16[3,128,2048]{2,1,0:T(8,128)(2,1)} %down.4.down_ref.own_ref), custom_call_target="tpu_custom_call" | custom-call | tf_op jit(solution)/shard_map/rows/pallas_call | solution.py:328
  19.3 5.6 %fusion.3.table_ref = bf16[512,512]{1,0:T(8,128)(2,1)} fusion(s32[512]{0:T(512)S(1)} %mul.40, s32[512]{0:T(512)S(1)} %pad_add_fusion, pred[512]{0:T(512)(128)(4,1)S(1)} %fusion.5), kind=kLoop, calls=%fused_computation.10 | loop fusion | flops 5505024 | bytes 528896 | tf_op jit(solution)/shard_map/mul | solution.py:296
  24.9 5.5 %collective-permute-done.other_ref = bf16[2,128,2048]{2,1,0:T(8,128)(2,1)S(1)} collective-permute-done((bf16[2,128,2048]{2,1,0:T(8,128)(2,1)}, bf16[2,128,2048]{2,1,0:T(8,128)(2,1)S(1)}, u32[]{:S(2)}, u32[]{:S(2)}) %collective-permute-start) | collective-permute-done | bytes 1048608 | tf_op jit(solution)/shard_map/ppermute | solution.py:325
  48.2 4.4 %rows.5 = (bf16[3,128,2048]{2,1,0:T(8,128)(2,1)}, f32[3,128,128]{2,1,0:T(8,128)}, f32[3,2,64,128]{3,2,1,0:T(8,128)}) custom-call(s32[1]{0:T(128)} %bitcast.6.side_ref, bf16[2,64,8,2048]{3,2,1,0:T(8,128)(2,1)} %est_ref.5, bf16[2,64,8,16]{3,2,1,0:T(8,128)(2,1)} %copy.35.win_ref, bf16[3,128,2048]{2,1,0:T(8,128)(2,1)} %down.5.down_ref.own_ref), custom_call_target="tpu_custom_call" | custom-call | tf_op jit(solution)/shard_map/rows/pallas_call | solution.py:328
  55.8 8.5 %collective-permute-done.5.other_ref = bf16[3,128,2048]{2,1,0:T(8,128)(2,1)} collective-permute-done((bf16[3,128,2048]{2,1,0:T(8,128)(2,1)}, bf16[3,128,2048]{2,1,0:T(8,128)(2,1)}, u32[]{:S(2)}, u32[]{:S(2)}) %collective-permute-start.5) | collective-permute-done | bytes 1572896 | tf_op jit(solution)/shard_map/ppermute | solution.py:325
  77.6 5.0 %collective-permute-start.9 = (bf16[3,128,768]{2,1,0:T(8,128)(2,1)S(1)}, bf16[3,128,768]{2,1,0:T(8,128)(2,1)S(1)}, u32[]{:S(2)}, u32[]{:S(2)}) collective-permute-start(bf16[3,128,768]{2,1,0:T(8,128)(2,1)S(1)} %get-tuple-element.161.rest_1_), channel_id=1, source_target_pairs={{0,4},{4,0},{8,12},{12,8},{1,5},{5,1},{9,13},{13,9},{2,6},{6,2},{1... | collective-permute-start | bytes 1769480 | tf_op jit(solution)/shard_map/ppermute | solution.py:352
  82.6 13.3 %collective-permute-done.9.rest_4_ = bf16[3,128,768]{2,1,0:T(8,128)(2,1)S(1)} collective-permute-done((bf16[3,128,768]{2,1,0:T(8,128)(2,1)S(1)}, bf16[3,128,768]{2,1,0:T(8,128)(2,1)S(1)}, u32[]{:S(2)}, u32[]{:S(2)}) %collective-permute-start.9) | collective-permute-done | bytes 589856 | tf_op jit(solution)/shard_map/ppermute | solution.py:352
  115.9 12.8 %collective-permute-done.15.rest_5_ = bf16[3,128,768]{2,1,0:T(8,128)(2,1)S(1)} collective-permute-done((bf16[3,128,768]{2,1,0:T(8,128)(2,1)S(1)}, bf16[3,128,768]{2,1,0:T(8,128)(2,1)S(1)}, u32[]{:S(2)}, u32[]{:S(2)}) %collective-permute-start.15) | collective-permute-done | bytes 589856 | tf_op jit(solution)/shard_map/ppermute | solution.py:352
  130.7 8.2 %collective-permute-start.17 = (bf16[8,128,256]{2,1,0:T(8,128)(2,1)S(1)}, bf16[8,128,256]{2,1,0:T(8,128)(2,1)S(1)}, u32[]{:S(2)}, u32[]{:S(2)}) collective-permute-start(bf16[8,128,256]{2,1,0:T(8,128)(2,1)S(1)} %get-tuple-element.182.a_ref.rest_0_), channel_id=1, source_target_pairs={{0,4},{12,8},{1,5},{13,9},{2,6},{14,10},{3,7},{15,11},{16,20},{28,... | collective-permute-start | bytes 1572872 | tf_op jit(solution)/shard_map/ppermute | solution.py:352
  148.6 4.7 %time_early.1 = (bf16[256,8,2048]{2,1,0:T(8,128)(2,1)}, bf16[256,8,256]{2,1,0:T(8,128)(2,1)}) custom-call(f32[1]{0:T(128)S(6)} %div.11.level_ref, bf16[512,512]{1,0:T(8,128)(2,1)} %fusion.3.table_ref, bf16[2,128,768]{2,1,0:T(8,128)(2,1)} %get-tuple-element.141.rest_0_, bf16[3,128,768]{2,1,0:T(8,128)(2,1)} %copy-done.17, bf16[3,128,768]{2,1,0:T(8,128)(2,1)} %copy-done.18, ...), custom_call_target="tpu_custom_call" | custom-call | tf_op jit(solution)/shard_map/time_early/pallas_call | solution.py:429
  153.3 5.3 %collective-permute-start.20 = (bf16[8,128,256]{2,1,0:T(8,128)(2,1)S(1)}, bf16[8,128,256]{2,1,0:T(8,128)(2,1)S(1)}, u32[]{:S(2)}, u32[]{:S(2)}) collective-permute-start(bf16[8,128,256]{2,1,0:T(8,128)(2,1)S(1)} %get-tuple-element.194.a_ref.rest_0_), channel_id=1, source_target_pairs={{0,4},{12,8},{1,5},{13,9},{2,6},{14,10},{3,7},{15,11},{16,20},{28,... | collective-permute-start | bytes 1572872 | tf_op jit(solution)/shard_map/ppermute | solution.py:352
  161.6 4.8 %collective-permute-done.20.b_ref.rest_1_ = bf16[8,128,256]{2,1,0:T(8,128)(2,1)S(1)} collective-permute-done((bf16[8,128,256]{2,1,0:T(8,128)(2,1)S(1)}, bf16[8,128,256]{2,1,0:T(8,128)(2,1)S(1)}, u32[]{:S(2)}, u32[]{:S(2)}) %collective-permute-start.20) | collective-permute-done | bytes 524320 | tf_op jit(solution)/shard_map/ppermute | solution.py:352
  166.4 4.4 %collective-permute-start.22 = (bf16[8,128,256]{2,1,0:T(8,128)(2,1)S(1)}, bf16[8,128,256]{2,1,0:T(8,128)(2,1)S(1)}, u32[]{:S(2)}, u32[]{:S(2)}) collective-permute-start(bf16[8,128,256]{2,1,0:T(8,128)(2,1)S(1)} %get-tuple-element.197.a_ref.rest_0_), channel_id=1, source_target_pairs={{0,4},{12,8},{1,5},{13,9},{2,6},{14,10},{3,7},{15,11},{16,20},{28,... | collective-permute-start | bytes 1572872 | tf_op jit(solution)/shard_map/ppermute | solution.py:352
  177.5 4.7 %time_late.6 = (bf16[256,8,2048]{2,1,0:T(8,128)(2,1)}, bf16[256,8,256]{2,1,0:T(8,128)(2,1)}) custom-call(f32[1]{0:T(128)S(6)} %div.11.level_ref, bf16[512,512]{1,0:T(8,128)(2,1)} %fusion.3.table_ref, bf16[8,128,256]{2,1,0:T(8,128)(2,1)} %copy-done.3, bf16[8,128,256]{2,1,0:T(8,128)(2,1)} %copy-done.22, ...), custom_call_target="tpu_custom_call", output_to_operand_aliasing={{0}: (5, {})} | custom-call | tf_op jit(solution)/shard_map/time_late/pallas_call | solution.py:429
  183.5 4.9 %collective-permute-done.25.got_ref = bf16[256,8,256]{2,1,0:T(8,128)(2,1)} collective-permute-done((bf16[256,8,256]{2,1,0:T(8,128)(2,1)}, bf16[256,8,256]{2,1,0:T(8,128)(2,1)}, u32[]{:S(2)}, u32[]{:S(2)}) %collective-permute-start.25) | collective-permute-done | bytes 1048608 | tf_op jit(solution)/shard_map/ppermute | solution.py:352
  196.1 5.0 %time_raw.1.rest_3_ = bf16[256,8,2048]{2,1,0:T(8,128)(2,1)} custom-call(f32[1]{0:T(128)S(6)} %div.11.level_ref, bf16[512,512]{1,0:T(8,128)(2,1)} %fusion.3.table_ref, bf16[2,128,768]{2,1,0:T(8,128)(2,1)} %get-tuple-element.141.rest_0_, bf16[3,128,768]{2,1,0:T(8,128)(2,1)} %copy-done.17, ...), custom_call_target="tpu_custom_call", output_to_operand_aliasing={{}: (20, {})} | custom-call | tf_op jit(solution)/shard_map/time_raw/pallas_call | solution.py:429
  201.1 4.7 %time_late.7 = (bf16[256,8,2048]{2,1,0:T(8,128)(2,1)}, bf16[256,8,256]{2,1,0:T(8,128)(2,1)}) custom-call(f32[1]{0:T(128)S(6)} %div.11.level_ref, bf16[512,512]{1,0:T(8,128)(2,1)} %fusion.3.table_ref, bf16[8,128,256]{2,1,0:T(8,128)(2,1)} %copy-done.4, bf16[8,128,256]{2,1,0:T(8,128)(2,1)} %copy-done.20, ...), custom_call_target="tpu_custom_call", output_to_operand_aliasing={{0}: (5, {})} | custom-call | tf_op jit(solution)/shard_map/time_late/pallas_call | solution.py:429
  213.3 6.9 %collective-permute-start.30 = (bf16[8,128,128]{2,1,0:T(8,128)(2,1)S(1)}, bf16[8,128,128]{2,1,0:T(8,128)(2,1)S(1)}, u32[]{:S(2)}, u32[]{:S(2)}) collective-permute-start(bf16[8,128,128]{2,1,0:T(8,128)(2,1)S(1)} %get-tuple-element.226.a_ref.rest_0_), channel_id=1, source_target_pairs={{0,4},{12,8},{1,5},{13,9},{2,6},{14,10},{3,7},{15,11},{16,20},{28,... | collective-permute-start | bytes 786440 | tf_op jit(solution)/shard_map/ppermute | solution.py:352
  225.1 4.5 %time_late.8 = (bf16[256,8,2048]{2,1,0:T(8,128)(2,1)}, bf16[256,8,256]{2,1,0:T(8,128)(2,1)}) custom-call(f32[1]{0:T(128)S(6)} %div.11.level_ref, bf16[512,512]{1,0:T(8,128)(2,1)} %fusion.3.table_ref, bf16[8,128,256]{2,1,0:T(8,128)(2,1)} %copy-done.5, bf16[8,128,256]{2,1,0:T(8,128)(2,1)} %copy-done.19, ...), custom_call_target="tpu_custom_call", output_to_operand_aliasing={{0}: (5, {})} | custom-call | tf_op jit(solution)/shard_map/time_late/pallas_call | solution.py:429
  234.6 6.2 %collective-permute-start.33 = (bf16[8,128,128]{2,1,0:T(8,128)(2,1)S(1)}, bf16[8,128,128]{2,1,0:T(8,128)(2,1)S(1)}, u32[]{:S(2)}, u32[]{:S(2)}) collective-permute-start(bf16[8,128,128]{2,1,0:T(8,128)(2,1)S(1)} %copy-done.13), channel_id=1, source_target_pairs={{0,4},{12,8},{1,5},{13,9},{2,6},{14,10},{3,7},{15,11},{16,20},{28,... | collective-permute-start | bytes 786440 | tf_op jit(solution)/shard_map/ppermute | solution.py:352
  244.6 4.6 %time_late.9 = (bf16[256,8,2048]{2,1,0:T(8,128)(2,1)}, bf16[256,8,256]{2,1,0:T(8,128)(2,1)}) custom-call(f32[1]{0:T(128)S(6)} %div.11.level_ref, bf16[512,512]{1,0:T(8,128)(2,1)} %fusion.3.table_ref, bf16[8,128,256]{2,1,0:T(8,128)(2,1)} %copy-done.6, bf16[8,128,256]{2,1,0:T(8,128)(2,1)} %copy-done.21, ...), custom_call_target="tpu_custom_call", output_to_operand_aliasing={{0}: (5, {})} | custom-call | tf_op jit(solution)/shard_map/time_late/pallas_call | solution.py:429
  262.2 15.8 %collective-permute-done.36.got_ref = bf16[256,8,256]{2,1,0:T(8,128)(2,1)S(1)} collective-permute-done((bf16[256,8,256]{2,1,0:T(8,128)(2,1)}, bf16[256,8,256]{2,1,0:T(8,128)(2,1)S(1)}, u32[]{:S(2)}, u32[]{:S(2)}) %collective-permute-start.36) | collective-permute-done | bytes 1048608 | tf_op jit(solution)/shard_map/ppermute | solution.py:352
  284.8 4.5 %collective-permute-done.39.got_ref = bf16[256,8,128]{2,1,0:T(8,128)(2,1)S(1)} collective-permute-done((bf16[256,8,128]{2,1,0:T(8,128)(2,1)}, bf16[256,8,128]{2,1,0:T(8,128)(2,1)S(1)}, u32[]{:S(2)}, u32[]{:S(2)}) %collective-permute-start.39) | collective-permute-done | bytes 524320 | tf_op jit(solution)/shard_map/ppermute | solution.py:352
  290.1 6.8 %collective-permute-done.38.got_ref = bf16[256,8,128]{2,1,0:T(8,128)(2,1)S(1)} collective-permute-done((bf16[256,8,128]{2,1,0:T(8,128)(2,1)}, bf16[256,8,128]{2,1,0:T(8,128)(2,1)S(1)}, u32[]{:S(2)}, u32[]{:S(2)}) %collective-permute-start.38) | collective-permute-done | bytes 524320 | tf_op jit(solution)/shard_map/ppermute | solution.py:352
  (199 shorter events, 140.1 us)
Async XLA Ops:
  3.3 27.1 %collective-permute-start = (bf16[2,128,2048]{2,1,0:T(8,128)(2,1)}, bf16[2,128,2048]{2,1,0:T(8,128)(2,1)S(1)}, u32[]{:S(2)}, u32[]{:S(2)}) collective-permute-start(bf16[2,128,2048]{2,1,0:T(8,128)(2,1)} %down.3.down_ref.own_ref), channel_id=1, source_target_pairs={{0,2},{2,0},{1,3},{3,1},{4,6},{6,4},{5,7},{7,5},{8,10},{10,8},{9,1... | collective-permute-start | bytes 3145736 | tf_op jit(solution)/shard_map/ppermute | solution.py:325
  9.8 54.4 %collective-permute-start.5 = (bf16[3,128,2048]{2,1,0:T(8,128)(2,1)}, bf16[3,128,2048]{2,1,0:T(8,128)(2,1)}, u32[]{:S(2)}, u32[]{:S(2)}) collective-permute-start(bf16[3,128,2048]{2,1,0:T(8,128)(2,1)} %down.4.down_ref.own_ref), channel_id=1, source_target_pairs={{0,2},{2,0},{1,3},{3,1},{4,6},{6,4},{5,7},{7,5},{8,10},{10,8},{9,1... | collective-permute-start | bytes 4718600 | tf_op jit(solution)/shard_map/ppermute | solution.py:325
  46.7 52.6 %collective-permute-start.4 = (bf16[3,128,2048]{2,1,0:T(8,128)(2,1)}, bf16[3,128,2048]{2,1,0:T(8,128)(2,1)}, u32[]{:S(2)}, u32[]{:S(2)}) collective-permute-start(bf16[3,128,2048]{2,1,0:T(8,128)(2,1)} %down.5.down_ref.own_ref), channel_id=1, source_target_pairs={{0,2},{2,0},{1,3},{3,1},{4,6},{6,4},{5,7},{7,5},{8,10},{10,8},{9,1... | collective-permute-start | bytes 4718600 | tf_op jit(solution)/shard_map/ppermute | solution.py:325
  52.7 23.5 %collective-permute-start.7 = (bf16[2,128,768]{2,1,0:T(8,128)(2,1)}, bf16[2,128,768]{2,1,0:T(8,128)(2,1)S(1)}, u32[]{:S(2)}, u32[]{:S(2)}) collective-permute-start(bf16[2,128,768]{2,1,0:T(8,128)(2,1)} %collective-permute-done.2.rest_3_), channel_id=1, source_target_pairs={{4,8},{8,4},{5,9},{9,5},{6,10},{10,6},{7,11},{11,7},{20,24},{24,20... | collective-permute-start | bytes 1179656 | tf_op jit(solution)/shard_map/ppermute | solution.py:352
  54.5 21.7 %collective-permute-start.8 = (bf16[2,128,512]{2,1,0:T(8,128)(2,1)S(1)}, bf16[2,128,512]{2,1,0:T(8,128)(2,1)S(1)}, u32[]{:S(2)}, u32[]{:S(2)}) collective-permute-start(bf16[2,128,512]{2,1,0:T(8,128)(2,1)S(1)} %slice.18), channel_id=1, source_target_pairs={{4,0},{8,12},{5,1},{9,13},{6,2},{10,14},{7,3},{11,15},{20,16},{24,... | collective-permute-start | bytes 786440 | tf_op jit(solution)/shard_map/ppermute | solution.py:352
  77.6 18.4 %collective-permute-start.9 = (bf16[3,128,768]{2,1,0:T(8,128)(2,1)S(1)}, bf16[3,128,768]{2,1,0:T(8,128)(2,1)S(1)}, u32[]{:S(2)}, u32[]{:S(2)}) collective-permute-start(bf16[3,128,768]{2,1,0:T(8,128)(2,1)S(1)} %get-tuple-element.161.rest_1_), channel_id=1, source_target_pairs={{0,4},{4,0},{8,12},{12,8},{1,5},{5,1},{9,13},{13,9},{2,6},{6,2},{1... | collective-permute-start | bytes 1769480 | tf_op jit(solution)/shard_map/ppermute | solution.py:352
  96.7 14.7 %collective-permute-start.13 = (bf16[3,128,512]{2,1,0:T(8,128)(2,1)S(1)}, bf16[3,128,512]{2,1,0:T(8,128)(2,1)S(1)}, u32[]{:S(2)}, u32[]{:S(2)}) collective-permute-start(bf16[3,128,512]{2,1,0:T(8,128)(2,1)S(1)} %slice.19), channel_id=1, source_target_pairs={{4,0},{8,12},{5,1},{9,13},{6,2},{10,14},{7,3},{11,15},{20,16},{24,... | collective-permute-start | bytes 1179656 | tf_op jit(solution)/shard_map/ppermute | solution.py:352
  98.0 17.1 %collective-permute-start.14 = (bf16[2,128,512]{2,1,0:T(8,128)(2,1)S(1)}, bf16[2,128,512]{2,1,0:T(8,128)(2,1)S(1)}, u32[]{:S(2)}, u32[]{:S(2)}) collective-permute-start(bf16[2,128,512]{2,1,0:T(8,128)(2,1)S(1)} %slice.20), channel_id=1, source_target_pairs={{4,0},{8,12},{5,1},{9,13},{6,2},{10,14},{7,3},{11,15},{20,16},{24,... | collective-permute-start | bytes 786440 | tf_op jit(solution)/shard_map/ppermute | solution.py:352
  128.6 16.3 %collective-permute-start.18 = (bf16[3,128,768]{2,1,0:T(8,128)(2,1)S(1)}, bf16[3,128,768]{2,1,0:T(8,128)(2,1)S(1)}, u32[]{:S(2)}, u32[]{:S(2)}) collective-permute-start(bf16[3,128,768]{2,1,0:T(8,128)(2,1)S(1)} %collective-permute-done.15.rest_5_), channel_id=1, source_target_pairs={{4,8},{8,4},{5,9},{9,5},{6,10},{10,6},{7,11},{11,7},{20,24},{24,20... | collective-permute-start | bytes 1769480 | tf_op jit(solution)/shard_map/ppermute | solution.py:352
  129.4 15.5 %collective-permute-start.19 = (bf16[3,128,512]{2,1,0:T(8,128)(2,1)S(1)}, bf16[3,128,512]{2,1,0:T(8,128)(2,1)S(1)}, u32[]{:S(2)}, u32[]{:S(2)}) collective-permute-start(bf16[3,128,512]{2,1,0:T(8,128)(2,1)S(1)} %slice.21), channel_id=1, source_target_pairs={{4,0},{8,12},{5,1},{9,13},{6,2},{10,14},{7,3},{11,15},{20,16},{24,... | collective-permute-start | bytes 1179656 | tf_op jit(solution)/shard_map/ppermute | solution.py:352
  130.7 22.6 %collective-permute-start.17 = (bf16[8,128,256]{2,1,0:T(8,128)(2,1)S(1)}, bf16[8,128,256]{2,1,0:T(8,128)(2,1)S(1)}, u32[]{:S(2)}, u32[]{:S(2)}) collective-permute-start(bf16[8,128,256]{2,1,0:T(8,128)(2,1)S(1)} %get-tuple-element.182.a_ref.rest_0_), channel_id=1, source_target_pairs={{0,4},{12,8},{1,5},{13,9},{2,6},{14,10},{3,7},{15,11},{16,20},{28,... | collective-permute-start | bytes 1572872 | tf_op jit(solution)/shard_map/ppermute | solution.py:352
  139.7 20.6 %collective-permute-start.23 = (bf16[3,128,512]{2,1,0:T(8,128)(2,1)}, bf16[3,128,512]{2,1,0:T(8,128)(2,1)}, u32[]{:S(2)}, u32[]{:S(2)}) collective-permute-start(bf16[3,128,512]{2,1,0:T(8,128)(2,1)} %slice.22), channel_id=1, source_target_pairs={{4,0},{8,12},{5,1},{9,13},{6,2},{10,14},{7,3},{11,15},{20,16},{24,... | collective-permute-start | bytes 1179656 | tf_op jit(solution)/shard_map/ppermute | solution.py:352
  146.6 13.7 %collective-permute-start.24 = (bf16[3,128,512]{2,1,0:T(8,128)(2,1)}, bf16[3,128,512]{2,1,0:T(8,128)(2,1)}, u32[]{:S(2)}, u32[]{:S(2)}) collective-permute-start(bf16[3,128,512]{2,1,0:T(8,128)(2,1)} %slice.23), channel_id=1, source_target_pairs={{4,0},{8,12},{5,1},{9,13},{6,2},{10,14},{7,3},{11,15},{20,16},{24,... | collective-permute-start | bytes 1179656 | tf_op jit(solution)/shard_map/ppermute | solution.py:352
  158.7 18.8 %collective-permute-start.21 = (bf16[16,128,256]{2,1,0:T(8,128)(2,1)S(1)}, bf16[16,128,256]{2,1,0:T(8,128)(2,1)}, u32[]{:S(2)}, u32[]{:S(2)}) collective-permute-start(bf16[16,128,256]{2,1,0:T(8,128)(2,1)S(1)} %pack.6), channel_id=1, source_target_pairs={{4,8},{8,4},{5,9},{9,5},{6,10},{10,6},{7,11},{11,7},{20,24},{24,20... | collective-permute-start | bytes 3145736 | tf_op jit(solution)/shard_map/ppermute | solution.py:352
  160.3 28.0 %collective-permute-start.25 = (bf16[256,8,256]{2,1,0:T(8,128)(2,1)}, bf16[256,8,256]{2,1,0:T(8,128)(2,1)}, u32[]{:S(2)}, u32[]{:S(2)}) collective-permute-start(bf16[256,8,256]{2,1,0:T(8,128)(2,1)} %get-tuple-element.201), channel_id=1, source_target_pairs={{4,0},{8,12},{5,1},{9,13},{6,2},{10,14},{7,3},{11,15},{20,16},{24,... | collective-permute-start | bytes 3145736 | tf_op jit(solution)/shard_map/ppermute | solution.py:352
  171.8 29.2 %collective-permute-start.27 = (bf16[16,128,256]{2,1,0:T(8,128)(2,1)}, bf16[16,128,256]{2,1,0:T(8,128)(2,1)}, u32[]{:S(2)}, u32[]{:S(2)}) collective-permute-start(bf16[16,128,256]{2,1,0:T(8,128)(2,1)} %pack.8), channel_id=1, source_target_pairs={{4,8},{8,4},{5,9},{9,5},{6,10},{10,6},{7,11},{11,7},{20,24},{24,20... | collective-permute-start | bytes 3145736 | tf_op jit(solution)/shard_map/ppermute | solution.py:352
  182.2 28.3 %collective-permute-start.29 = (bf16[256,8,256]{2,1,0:T(8,128)(2,1)}, bf16[256,8,256]{2,1,0:T(8,128)(2,1)S(1)}, u32[]{:S(2)}, u32[]{:S(2)}) collective-permute-start(bf16[256,8,256]{2,1,0:T(8,128)(2,1)} %get-tuple-element.212), channel_id=1, source_target_pairs={{4,0},{8,12},{5,1},{9,13},{6,2},{10,14},{7,3},{11,15},{20,16},{24,... | collective-permute-start | bytes 3145736 | tf_op jit(solution)/shard_map/ppermute | solution.py:352
  195.2 28.9 %collective-permute-start.26 = (bf16[16,128,256]{2,1,0:T(8,128)(2,1)}, bf16[16,128,256]{2,1,0:T(8,128)(2,1)S(1)}, u32[]{:S(2)}, u32[]{:S(2)}) collective-permute-start(bf16[16,128,256]{2,1,0:T(8,128)(2,1)} %pack.7), channel_id=1, source_target_pairs={{4,8},{8,4},{5,9},{9,5},{6,10},{10,6},{7,11},{11,7},{20,24},{24,20... | collective-permute-start | bytes 3145736 | tf_op jit(solution)/shard_map/ppermute | solution.py:352
  205.8 26.5 %collective-permute-start.31 = (bf16[256,8,256]{2,1,0:T(8,128)(2,1)}, bf16[256,8,256]{2,1,0:T(8,128)(2,1)}, u32[]{:S(2)}, u32[]{:S(2)}) collective-permute-start(bf16[256,8,256]{2,1,0:T(8,128)(2,1)} %get-tuple-element.228), channel_id=1, source_target_pairs={{4,0},{8,12},{5,1},{9,13},{6,2},{10,14},{7,3},{11,15},{20,16},{24,... | collective-permute-start | bytes 3145736 | tf_op jit(solution)/shard_map/ppermute | solution.py:352
  211.7 29.1 %collective-permute-start.32 = (bf16[16,128,256]{2,1,0:T(8,128)(2,1)S(1)}, bf16[16,128,256]{2,1,0:T(8,128)(2,1)}, u32[]{:S(2)}, u32[]{:S(2)}) collective-permute-start(bf16[16,128,256]{2,1,0:T(8,128)(2,1)S(1)} %pack.9), channel_id=1, source_target_pairs={{4,8},{8,4},{5,9},{9,5},{6,10},{10,6},{7,11},{11,7},{20,24},{24,20... | collective-permute-start | bytes 3145736 | tf_op jit(solution)/shard_map/ppermute | solution.py:352
  229.7 25.9 %collective-permute-start.34 = (bf16[256,8,256]{2,1,0:T(8,128)(2,1)}, bf16[256,8,256]{2,1,0:T(8,128)(2,1)S(1)}, u32[]{:S(2)}, u32[]{:S(2)}) collective-permute-start(bf16[256,8,256]{2,1,0:T(8,128)(2,1)} %get-tuple-element.238), channel_id=1, source_target_pairs={{4,0},{8,12},{5,1},{9,13},{6,2},{10,14},{7,3},{11,15},{20,16},{24,... | collective-permute-start | bytes 3145736 | tf_op jit(solution)/shard_map/ppermute | solution.py:352
  249.2 28.8 %collective-permute-start.36 = (bf16[256,8,256]{2,1,0:T(8,128)(2,1)}, bf16[256,8,256]{2,1,0:T(8,128)(2,1)S(1)}, u32[]{:S(2)}, u32[]{:S(2)}) collective-permute-start(bf16[256,8,256]{2,1,0:T(8,128)(2,1)} %get-tuple-element.246), channel_id=1, source_target_pairs={{4,0},{8,12},{5,1},{9,13},{6,2},{10,14},{7,3},{11,15},{20,16},{24,... | collective-permute-start | bytes 3145736 | tf_op jit(solution)/shard_map/ppermute | solution.py:352
  256.7 22.4 %collective-permute-start.35 = (bf16[16,128,128]{2,1,0:T(8,128)(2,1)S(1)}, bf16[16,128,128]{2,1,0:T(8,128)(2,1)S(1)}, u32[]{:S(2)}, u32[]{:S(2)}) collective-permute-start(bf16[16,128,128]{2,1,0:T(8,128)(2,1)S(1)} %pack.10), channel_id=1, source_target_pairs={{4,8},{8,4},{5,9},{9,5},{6,10},{10,6},{7,11},{11,7},{20,24},{24,20... | collective-permute-start | bytes 1572872 | tf_op jit(solution)/shard_map/ppermute | solution.py:352
  260.9 28.3 %collective-permute-start.39 = (bf16[256,8,128]{2,1,0:T(8,128)(2,1)}, bf16[256,8,128]{2,1,0:T(8,128)(2,1)S(1)}, u32[]{:S(2)}, u32[]{:S(2)}) collective-permute-start(bf16[256,8,128]{2,1,0:T(8,128)(2,1)} %get-tuple-element.253), channel_id=1, source_target_pairs={{4,0},{8,12},{5,1},{9,13},{6,2},{10,14},{7,3},{11,15},{20,16},{24,... | collective-permute-start | bytes 1572872 | tf_op jit(solution)/shard_map/ppermute | solution.py:352
  (62 other events, 1315.5 us)

commit v3 on v2

--- a/solution.py
+++ b/solution.py
@@ -412,10 +412,10 @@
         mids[k] = send(earlies[k], MIDDLE)
         if k:
             far_out[k - 1] = send(cut(crosses[k - 1]), OUTWARD)
-        beside = [swaps[k], mids[k], lates[0]]
+        beside = [swaps[k], lates[0]]
         if k == 0:
             beside += [rows[2], models[2], wins[2]]
-        swaps[k], mids[k], lates[0], *beside = tie(*beside)
+        swaps[k], lates[0], *beside = tie(*beside)
         if k == 0:
             rows[2], models[2], wins[2] = beside
         crosses[k] = send(swaps[k], MIDDLE)

time: 300 us -> 298 us (level)
    unnamed x93 -> x91, local copies, waits for them, and re-layouts: 14.7 us -> 14 us
where the time goes in v3:
time: 298 us; the launch traced here: 296 us
  waiting for transfers between devices  114 us (38%)
  Pallas kernels  82.9 us (28%)
  starting transfers between devices  73.1 us (25%)
  local copies, waits for them, and re-layouts  17.4 us (6%)
  other arithmetic  6.97 us (2%)
    ppermute x34, waiting for transfers between devices, line_body(): send = lambda a, pairs: lax.ppermute(a, 'freq', pairs)  94.3 us
    ppermute x34, starting transfers between devices, line_body(): send = lambda a, pairs: lax.ppermute(a, 'freq', pairs)  68.5 us
    pallas_call x8, Pallas kernels, time_call(): pl.pallas_call(partial(time_kernel, plan, blocks, aliased), grid=(grid,),...  35.4 us
    ppermute x3, waiting for transfers between devices, line_body(): others = [lax.ppermute(a, 'shot', ((0, 1), (1, 0))) for a in downs]  15.8 us
    unnamed x91, local copies, waits for them, and re-layouts  14 us
    pallas_call x3, Pallas kernels, line_body(): kernel(rows_kernel, SIZES[k], in_specs=[whole(SMEM), pl.BlockSpec((2, OCT...  12.1 us
    pallas_call x7, Pallas kernels, place(): pl.pallas_call(partial(place_kernel, late_first[j - 1] if j else raw), in...  9.27 us
    pallas_call x3, Pallas kernels, line_body(): kernel(partial(down_kernel, first_group[k] * OCT), SIZES[k], in_specs=[pl...  9.26 us
  transfers between devices with their start and end apart: 40, of which 21 were waited for; matrix products, arithmetic and copies ran while one was open for 3% of the time, Pallas kernels for 27%

profile of v3, /device:TPU:0, one launch (start us, length us, event | category | flops | bytes accessed | tf_op | source)
XLA Modules:
  0.0 296.3 jit_solution(12582935348240901908)
XLA Ops:
  10.8 4.4 %rows.4 = (bf16[3,128,2048]{2,1,0:T(8,128)(2,1)}, f32[3,128,128]{2,1,0:T(8,128)}, f32[3,2,64,128]{3,2,1,0:T(8,128)}) custom-call(s32[1]{0:T(128)} %bitcast.6.side_ref, bf16[2,64,8,2048]{3,2,1,0:T(8,128)(2,1)} %est_ref.5, bf16[2,64,8,16]{3,2,1,0:T(8,128)(2,1)} %copy.35.win_ref, bf16[3,128,2048]{2,1,0:T(8,128)(2,1)} %down.4.down_ref.own_ref), custom_call_target="tpu_custom_call" | custom-call | tf_op jit(solution)/shard_map/rows/pallas_call | solution.py:328
  19.4 5.6 %fusion.3.table_ref = bf16[512,512]{1,0:T(8,128)(2,1)} fusion(s32[512]{0:T(512)S(1)} %mul.40, s32[512]{0:T(512)S(1)} %pad_add_fusion, pred[512]{0:T(512)(128)(4,1)S(1)} %fusion.5), kind=kLoop, calls=%fused_computation.10 | loop fusion | flops 5505024 | bytes 528896 | tf_op jit(solution)/shard_map/mul | solution.py:296
  25.0 5.5 %collective-permute-done.other_ref = bf16[2,128,2048]{2,1,0:T(8,128)(2,1)S(1)} collective-permute-done((bf16[2,128,2048]{2,1,0:T(8,128)(2,1)}, bf16[2,128,2048]{2,1,0:T(8,128)(2,1)S(1)}, u32[]{:S(2)}, u32[]{:S(2)}) %collective-permute-start) | collective-permute-done | bytes 1048608 | tf_op jit(solution)/shard_map/ppermute | solution.py:325
  48.3 4.4 %rows.5 = (bf16[3,128,2048]{2,1,0:T(8,128)(2,1)}, f32[3,128,128]{2,1,0:T(8,128)}, f32[3,2,64,128]{3,2,1,0:T(8,128)}) custom-call(s32[1]{0:T(128)} %bitcast.6.side_ref, bf16[2,64,8,2048]{3,2,1,0:T(8,128)(2,1)} %est_ref.5, bf16[2,64,8,16]{3,2,1,0:T(8,128)(2,1)} %copy.35.win_ref, bf16[3,128,2048]{2,1,0:T(8,128)(2,1)} %down.5.down_ref.own_ref), custom_call_target="tpu_custom_call" | custom-call | tf_op jit(solution)/shard_map/rows/pallas_call | solution.py:328
  55.8 8.5 %collective-permute-done.4.other_ref = bf16[3,128,2048]{2,1,0:T(8,128)(2,1)} collective-permute-done((bf16[3,128,2048]{2,1,0:T(8,128)(2,1)}, bf16[3,128,2048]{2,1,0:T(8,128)(2,1)}, u32[]{:S(2)}, u32[]{:S(2)}) %collective-permute-start.4) | collective-permute-done | bytes 1572896 | tf_op jit(solution)/shard_map/ppermute | solution.py:325
  79.1 12.9 %collective-permute-done.9.rest_4_ = bf16[3,128,768]{2,1,0:T(8,128)(2,1)S(1)} collective-permute-done((bf16[3,128,768]{2,1,0:T(8,128)(2,1)S(1)}, bf16[3,128,768]{2,1,0:T(8,128)(2,1)S(1)}, u32[]{:S(2)}, u32[]{:S(2)}) %collective-permute-start.9) | collective-permute-done | bytes 589856 | tf_op jit(solution)/shard_map/ppermute | solution.py:352
  113.4 13.0 %collective-permute-done.15.rest_5_ = bf16[3,128,768]{2,1,0:T(8,128)(2,1)S(1)} collective-permute-done((bf16[3,128,768]{2,1,0:T(8,128)(2,1)S(1)}, bf16[3,128,768]{2,1,0:T(8,128)(2,1)S(1)}, u32[]{:S(2)}, u32[]{:S(2)}) %collective-permute-start.15) | collective-permute-done | bytes 589856 | tf_op jit(solution)/shard_map/ppermute | solution.py:352
  128.4 4.6 %collective-permute-start.16 = (bf16[8,128,256]{2,1,0:T(8,128)(2,1)S(1)}, bf16[8,128,256]{2,1,0:T(8,128)(2,1)S(1)}, u32[]{:S(2)}, u32[]{:S(2)}) collective-permute-start(bf16[8,128,256]{2,1,0:T(8,128)(2,1)S(1)} %get-tuple-element.177.a_ref.rest_0_), channel_id=1, source_target_pairs={{0,4},{12,8},{1,5},{13,9},{2,6},{14,10},{3,7},{15,11},{16,20},{28,... | collective-permute-start | bytes 1572872 | tf_op jit(solution)/shard_map/ppermute | solution.py:352
  135.2 4.5 %collective-permute-done.19.rest_15_ = bf16[3,128,512]{2,1,0:T(8,128)(2,1)S(1)} collective-permute-done((bf16[3,128,512]{2,1,0:T(8,128)(2,1)S(1)}, bf16[3,128,512]{2,1,0:T(8,128)(2,1)S(1)}, u32[]{:S(2)}, u32[]{:S(2)}) %collective-permute-start.19) | collective-permute-done | bytes 393248 | tf_op jit(solution)/shard_map/ppermute | solution.py:352
  143.4 4.7 %time_early.1 = (bf16[256,8,2048]{2,1,0:T(8,128)(2,1)}, bf16[256,8,256]{2,1,0:T(8,128)(2,1)}) custom-call(f32[1]{0:T(128)S(6)} %div.11.level_ref, bf16[512,512]{1,0:T(8,128)(2,1)} %fusion.3.table_ref, bf16[2,128,768]{2,1,0:T(8,128)(2,1)} %get-tuple-element.138.rest_0_, bf16[3,128,768]{2,1,0:T(8,128)(2,1)} %copy-done.17, bf16[3,128,768]{2,1,0:T(8,128)(2,1)} %copy-done.18, ...), custom_call_target="tpu_custom_call" | custom-call | tf_op jit(solution)/shard_map/time_early/pallas_call | solution.py:429
  148.1 5.6 %collective-permute-start.20 = (bf16[8,128,256]{2,1,0:T(8,128)(2,1)S(1)}, bf16[8,128,256]{2,1,0:T(8,128)(2,1)S(1)}, u32[]{:S(2)}, u32[]{:S(2)}) collective-permute-start(bf16[8,128,256]{2,1,0:T(8,128)(2,1)S(1)} %get-tuple-element.188.a_ref.rest_0_), channel_id=1, source_target_pairs={{0,4},{12,8},{1,5},{13,9},{2,6},{14,10},{3,7},{15,11},{16,20},{28,... | collective-permute-start | bytes 1572872 | tf_op jit(solution)/shard_map/ppermute | solution.py:352
  156.7 6.2 %collective-permute-done.20.b_ref.rest_1_ = bf16[8,128,256]{2,1,0:T(8,128)(2,1)S(1)} collective-permute-done((bf16[8,128,256]{2,1,0:T(8,128)(2,1)S(1)}, bf16[8,128,256]{2,1,0:T(8,128)(2,1)S(1)}, u32[]{:S(2)}, u32[]{:S(2)}) %collective-permute-start.20) | collective-permute-done | bytes 524320 | tf_op jit(solution)/shard_map/ppermute | solution.py:352
  170.0 5.7 %collective-permute-done.22.b_ref.rest_1_ = bf16[8,128,256]{2,1,0:T(8,128)(2,1)S(1)} collective-permute-done((bf16[8,128,256]{2,1,0:T(8,128)(2,1)S(1)}, bf16[8,128,256]{2,1,0:T(8,128)(2,1)S(1)}, u32[]{:S(2)}, u32[]{:S(2)}) %collective-permute-start.22) | collective-permute-done | bytes 524320 | tf_op jit(solution)/shard_map/ppermute | solution.py:352
  175.7 4.7 %time_late.6 = (bf16[256,8,2048]{2,1,0:T(8,128)(2,1)}, bf16[256,8,256]{2,1,0:T(8,128)(2,1)}) custom-call(f32[1]{0:T(128)S(6)} %div.11.level_ref, bf16[512,512]{1,0:T(8,128)(2,1)} %fusion.3.table_ref, bf16[8,128,256]{2,1,0:T(8,128)(2,1)} %copy-done.3, bf16[8,128,256]{2,1,0:T(8,128)(2,1)} %copy-done.22, ...), custom_call_target="tpu_custom_call", output_to_operand_aliasing={{0}: (5, {})} | custom-call | tf_op jit(solution)/shard_map/time_late/pallas_call | solution.py:429
  184.0 5.1 %collective-permute-start.28 = (bf16[8,128,256]{2,1,0:T(8,128)(2,1)S(1)}, bf16[8,128,256]{2,1,0:T(8,128)(2,1)S(1)}, u32[]{:S(2)}, u32[]{:S(2)}) collective-permute-start(bf16[8,128,256]{2,1,0:T(8,128)(2,1)S(1)} %get-tuple-element.204.a_ref.rest_0_), channel_id=1, source_target_pairs={{0,4},{12,8},{1,5},{13,9},{2,6},{14,10},{3,7},{15,11},{16,20},{28,... | collective-permute-start | bytes 1572872 | tf_op jit(solution)/shard_map/ppermute | solution.py:352
  191.1 5.0 %time_raw.1.rest_3_ = bf16[256,8,2048]{2,1,0:T(8,128)(2,1)} custom-call(f32[1]{0:T(128)S(6)} %div.11.level_ref, bf16[512,512]{1,0:T(8,128)(2,1)} %fusion.3.table_ref, bf16[2,128,768]{2,1,0:T(8,128)(2,1)} %get-tuple-element.138.rest_0_, bf16[3,128,768]{2,1,0:T(8,128)(2,1)} %copy-done.17, ...), custom_call_target="tpu_custom_call", output_to_operand_aliasing={{}: (20, {})} | custom-call | tf_op jit(solution)/shard_map/time_raw/pallas_call | solution.py:429
  196.2 4.7 %time_late.7 = (bf16[256,8,2048]{2,1,0:T(8,128)(2,1)}, bf16[256,8,256]{2,1,0:T(8,128)(2,1)}) custom-call(f32[1]{0:T(128)S(6)} %div.11.level_ref, bf16[512,512]{1,0:T(8,128)(2,1)} %fusion.3.table_ref, bf16[8,128,256]{2,1,0:T(8,128)(2,1)} %copy-done.4, bf16[8,128,256]{2,1,0:T(8,128)(2,1)} %copy-done.20, ...), custom_call_target="tpu_custom_call", output_to_operand_aliasing={{0}: (5, {})} | custom-call | tf_op jit(solution)/shard_map/time_late/pallas_call | solution.py:429
  207.3 8.5 %collective-permute-start.30 = (bf16[8,128,128]{2,1,0:T(8,128)(2,1)S(1)}, bf16[8,128,128]{2,1,0:T(8,128)(2,1)S(1)}, u32[]{:S(2)}, u32[]{:S(2)}) collective-permute-start(bf16[8,128,128]{2,1,0:T(8,128)(2,1)S(1)} %get-tuple-element.220.a_ref.rest_0_), channel_id=1, source_target_pairs={{0,4},{12,8},{1,5},{13,9},{2,6},{14,10},{3,7},{15,11},{16,20},{28,... | collective-permute-start | bytes 786440 | tf_op jit(solution)/shard_map/ppermute | solution.py:352
  220.7 4.5 %time_late.8 = (bf16[256,8,2048]{2,1,0:T(8,128)(2,1)}, bf16[256,8,256]{2,1,0:T(8,128)(2,1)}) custom-call(f32[1]{0:T(128)S(6)} %div.11.level_ref, bf16[512,512]{1,0:T(8,128)(2,1)} %fusion.3.table_ref, bf16[8,128,256]{2,1,0:T(8,128)(2,1)} %copy-done.5, bf16[8,128,256]{2,1,0:T(8,128)(2,1)} %copy-done.19, ...), custom_call_target="tpu_custom_call", output_to_operand_aliasing={{0}: (5, {})} | custom-call | tf_op jit(solution)/shard_map/time_late/pallas_call | solution.py:429
  229.5 6.4 %collective-permute-start.33 = (bf16[8,128,128]{2,1,0:T(8,128)(2,1)S(1)}, bf16[8,128,128]{2,1,0:T(8,128)(2,1)S(1)}, u32[]{:S(2)}, u32[]{:S(2)}) collective-permute-start(bf16[8,128,128]{2,1,0:T(8,128)(2,1)S(1)} %copy-done.13), channel_id=1, source_target_pairs={{0,4},{12,8},{1,5},{13,9},{2,6},{14,10},{3,7},{15,11},{16,20},{28,... | collective-permute-start | bytes 786440 | tf_op jit(solution)/shard_map/ppermute | solution.py:352
  239.7 4.6 %time_late.9 = (bf16[256,8,2048]{2,1,0:T(8,128)(2,1)}, bf16[256,8,256]{2,1,0:T(8,128)(2,1)}) custom-call(f32[1]{0:T(128)S(6)} %div.11.level_ref, bf16[512,512]{1,0:T(8,128)(2,1)} %fusion.3.table_ref, bf16[8,128,256]{2,1,0:T(8,128)(2,1)} %copy-done.6, bf16[8,128,256]{2,1,0:T(8,128)(2,1)} %copy-done.21, ...), custom_call_target="tpu_custom_call", output_to_operand_aliasing={{0}: (5, {})} | custom-call | tf_op jit(solution)/shard_map/time_late/pallas_call | solution.py:429
  257.8 17.9 %collective-permute-done.36.got_ref = bf16[256,8,256]{2,1,0:T(8,128)(2,1)S(1)} collective-permute-done((bf16[256,8,256]{2,1,0:T(8,128)(2,1)}, bf16[256,8,256]{2,1,0:T(8,128)(2,1)S(1)}, u32[]{:S(2)}, u32[]{:S(2)}) %collective-permute-start.36) | collective-permute-done | bytes 1048608 | tf_op jit(solution)/shard_map/ppermute | solution.py:352
  282.4 4.5 %collective-permute-done.39.got_ref = bf16[256,8,128]{2,1,0:T(8,128)(2,1)S(1)} collective-permute-done((bf16[256,8,128]{2,1,0:T(8,128)(2,1)}, bf16[256,8,128]{2,1,0:T(8,128)(2,1)S(1)}, u32[]{:S(2)}, u32[]{:S(2)}) %collective-permute-start.39) | collective-permute-done | bytes 524320 | tf_op jit(solution)/shard_map/ppermute | solution.py:352
  287.8 7.5 %collective-permute-done.38.got_ref = bf16[256,8,128]{2,1,0:T(8,128)(2,1)S(1)} collective-permute-done((bf16[256,8,128]{2,1,0:T(8,128)(2,1)}, bf16[256,8,128]{2,1,0:T(8,128)(2,1)S(1)}, u32[]{:S(2)}, u32[]{:S(2)}) %collective-permute-start.38) | collective-permute-done | bytes 524320 | tf_op jit(solution)/shard_map/ppermute | solution.py:352
  (197 shorter events, 134.7 us)
Async XLA Ops:
  3.4 27.1 %collective-permute-start = (bf16[2,128,2048]{2,1,0:T(8,128)(2,1)}, bf16[2,128,2048]{2,1,0:T(8,128)(2,1)S(1)}, u32[]{:S(2)}, u32[]{:S(2)}) collective-permute-start(bf16[2,128,2048]{2,1,0:T(8,128)(2,1)} %down.3.down_ref.own_ref), channel_id=1, source_target_pairs={{0,2},{2,0},{1,3},{3,1},{4,6},{6,4},{5,7},{7,5},{8,10},{10,8},{9,1... | collective-permute-start | bytes 3145736 | tf_op jit(solution)/shard_map/ppermute | solution.py:325
  9.9 54.5 %collective-permute-start.4 = (bf16[3,128,2048]{2,1,0:T(8,128)(2,1)}, bf16[3,128,2048]{2,1,0:T(8,128)(2,1)}, u32[]{:S(2)}, u32[]{:S(2)}) collective-permute-start(bf16[3,128,2048]{2,1,0:T(8,128)(2,1)} %down.4.down_ref.own_ref), channel_id=1, source_target_pairs={{0,2},{2,0},{1,3},{3,1},{4,6},{6,4},{5,7},{7,5},{8,10},{10,8},{9,1... | collective-permute-start | bytes 4718600 | tf_op jit(solution)/shard_map/ppermute | solution.py:325
  46.8 50.4 %collective-permute-start.3 = (bf16[3,128,2048]{2,1,0:T(8,128)(2,1)}, bf16[3,128,2048]{2,1,0:T(8,128)(2,1)}, u32[]{:S(2)}, u32[]{:S(2)}) collective-permute-start(bf16[3,128,2048]{2,1,0:T(8,128)(2,1)} %down.5.down_ref.own_ref), channel_id=1, source_target_pairs={{0,2},{2,0},{1,3},{3,1},{4,6},{6,4},{5,7},{7,5},{8,10},{10,8},{9,1... | collective-permute-start | bytes 4718600 | tf_op jit(solution)/shard_map/ppermute | solution.py:325
  52.7 23.5 %collective-permute-start.7 = (bf16[2,128,768]{2,1,0:T(8,128)(2,1)}, bf16[2,128,768]{2,1,0:T(8,128)(2,1)S(1)}, u32[]{:S(2)}, u32[]{:S(2)}) collective-permute-start(bf16[2,128,768]{2,1,0:T(8,128)(2,1)} %collective-permute-done.2.rest_3_), channel_id=1, source_target_pairs={{4,8},{8,4},{5,9},{9,5},{6,10},{10,6},{7,11},{11,7},{20,24},{24,20... | collective-permute-start | bytes 1179656 | tf_op jit(solution)/shard_map/ppermute | solution.py:352
  54.5 21.7 %collective-permute-start.8 = (bf16[2,128,512]{2,1,0:T(8,128)(2,1)S(1)}, bf16[2,128,512]{2,1,0:T(8,128)(2,1)}, u32[]{:S(2)}, u32[]{:S(2)}) collective-permute-start(bf16[2,128,512]{2,1,0:T(8,128)(2,1)S(1)} %slice.26), channel_id=1, source_target_pairs={{4,0},{8,12},{5,1},{9,13},{6,2},{10,14},{7,3},{11,15},{20,16},{24,... | collective-permute-start | bytes 786440 | tf_op jit(solution)/shard_map/ppermute | solution.py:352
  76.2 15.8 %collective-permute-start.9 = (bf16[3,128,768]{2,1,0:T(8,128)(2,1)S(1)}, bf16[3,128,768]{2,1,0:T(8,128)(2,1)S(1)}, u32[]{:S(2)}, u32[]{:S(2)}) collective-permute-start(bf16[3,128,768]{2,1,0:T(8,128)(2,1)S(1)} %get-tuple-element.157.rest_1_), channel_id=1, source_target_pairs={{0,4},{4,0},{8,12},{12,8},{1,5},{5,1},{9,13},{13,9},{2,6},{6,2},{1... | collective-permute-start | bytes 1769480 | tf_op jit(solution)/shard_map/ppermute | solution.py:352
  78.4 14.3 %collective-permute-start.11 = (bf16[3,128,768]{2,1,0:T(8,128)(2,1)S(1)}, bf16[3,128,768]{2,1,0:T(8,128)(2,1)S(1)}, u32[]{:S(2)}, u32[]{:S(2)}) collective-permute-start(bf16[3,128,768]{2,1,0:T(8,128)(2,1)S(1)} %get-tuple-element.157.rest_1_), channel_id=1, source_target_pairs={{4,8},{8,4},{5,9},{9,5},{6,10},{10,6},{7,11},{11,7},{20,24},{24,20... | collective-permute-start | bytes 1769480 | tf_op jit(solution)/shard_map/ppermute | solution.py:352
  92.8 15.8 %collective-permute-start.13 = (bf16[3,128,512]{2,1,0:T(8,128)(2,1)S(1)}, bf16[3,128,512]{2,1,0:T(8,128)(2,1)S(1)}, u32[]{:S(2)}, u32[]{:S(2)}) collective-permute-start(bf16[3,128,512]{2,1,0:T(8,128)(2,1)S(1)} %slice.27), channel_id=1, source_target_pairs={{4,0},{8,12},{5,1},{9,13},{6,2},{10,14},{7,3},{11,15},{20,16},{24,... | collective-permute-start | bytes 1179656 | tf_op jit(solution)/shard_map/ppermute | solution.py:352
  94.2 18.5 %collective-permute-start.14 = (bf16[2,128,512]{2,1,0:T(8,128)(2,1)S(1)}, bf16[2,128,512]{2,1,0:T(8,128)(2,1)S(1)}, u32[]{:S(2)}, u32[]{:S(2)}) collective-permute-start(bf16[2,128,512]{2,1,0:T(8,128)(2,1)S(1)} %slice.20), channel_id=1, source_target_pairs={{4,0},{8,12},{5,1},{9,13},{6,2},{10,14},{7,3},{11,15},{20,16},{24,... | collective-permute-start | bytes 786440 | tf_op jit(solution)/shard_map/ppermute | solution.py:352
  112.7 20.4 %collective-permute-start.17 = (bf16[3,128,768]{2,1,0:T(8,128)(2,1)S(1)}, bf16[3,128,768]{2,1,0:T(8,128)(2,1)S(1)}, u32[]{:S(2)}, u32[]{:S(2)}) collective-permute-start(bf16[3,128,768]{2,1,0:T(8,128)(2,1)S(1)} %get-tuple-element.175.rest_2_), channel_id=1, source_target_pairs={{4,8},{8,4},{5,9},{9,5},{6,10},{10,6},{7,11},{11,7},{20,24},{24,20... | collective-permute-start | bytes 1769480 | tf_op jit(solution)/shard_map/ppermute | solution.py:352
  128.4 19.7 %collective-permute-start.16 = (bf16[8,128,256]{2,1,0:T(8,128)(2,1)S(1)}, bf16[8,128,256]{2,1,0:T(8,128)(2,1)S(1)}, u32[]{:S(2)}, u32[]{:S(2)}) collective-permute-start(bf16[8,128,256]{2,1,0:T(8,128)(2,1)S(1)} %get-tuple-element.177.a_ref.rest_0_), channel_id=1, source_target_pairs={{0,4},{12,8},{1,5},{13,9},{2,6},{14,10},{3,7},{15,11},{16,20},{28,... | collective-permute-start | bytes 1572872 | tf_op jit(solution)/shard_map/ppermute | solution.py:352
  133.9 21.4 %collective-permute-start.23 = (bf16[3,128,512]{2,1,0:T(8,128)(2,1)}, bf16[3,128,512]{2,1,0:T(8,128)(2,1)}, u32[]{:S(2)}, u32[]{:S(2)}) collective-permute-start(bf16[3,128,512]{2,1,0:T(8,128)(2,1)} %slice.28), channel_id=1, source_target_pairs={{4,0},{8,12},{5,1},{9,13},{6,2},{10,14},{7,3},{11,15},{20,16},{24,... | collective-permute-start | bytes 1179656 | tf_op jit(solution)/shard_map/ppermute | solution.py:352
  148.1 14.8 %collective-permute-start.20 = (bf16[8,128,256]{2,1,0:T(8,128)(2,1)S(1)}, bf16[8,128,256]{2,1,0:T(8,128)(2,1)S(1)}, u32[]{:S(2)}, u32[]{:S(2)}) collective-permute-start(bf16[8,128,256]{2,1,0:T(8,128)(2,1)S(1)} %get-tuple-element.188.a_ref.rest_0_), channel_id=1, source_target_pairs={{0,4},{12,8},{1,5},{13,9},{2,6},{14,10},{3,7},{15,11},{16,20},{28,... | collective-permute-start | bytes 1572872 | tf_op jit(solution)/shard_map/ppermute | solution.py:352
  153.7 22.0 %collective-permute-start.21 = (bf16[16,128,256]{2,1,0:T(8,128)(2,1)S(1)}, bf16[16,128,256]{2,1,0:T(8,128)(2,1)}, u32[]{:S(2)}, u32[]{:S(2)}) collective-permute-start(bf16[16,128,256]{2,1,0:T(8,128)(2,1)S(1)} %pack.6), channel_id=1, source_target_pairs={{4,8},{8,4},{5,9},{9,5},{6,10},{10,6},{7,11},{11,7},{20,24},{24,20... | collective-permute-start | bytes 3145736 | tf_op jit(solution)/shard_map/ppermute | solution.py:352
  155.4 26.4 %collective-permute-start.25 = (bf16[256,8,256]{2,1,0:T(8,128)(2,1)}, bf16[256,8,256]{2,1,0:T(8,128)(2,1)}, u32[]{:S(2)}, u32[]{:S(2)}) collective-permute-start(bf16[256,8,256]{2,1,0:T(8,128)(2,1)} %get-tuple-element.195), channel_id=1, source_target_pairs={{4,0},{8,12},{5,1},{9,13},{6,2},{10,14},{7,3},{11,15},{20,16},{24,... | collective-permute-start | bytes 3145736 | tf_op jit(solution)/shard_map/ppermute | solution.py:352
  168.4 27.8 %collective-permute-start.27 = (bf16[16,128,256]{2,1,0:T(8,128)(2,1)}, bf16[16,128,256]{2,1,0:T(8,128)(2,1)}, u32[]{:S(2)}, u32[]{:S(2)}) collective-permute-start(bf16[16,128,256]{2,1,0:T(8,128)(2,1)} %pack.8), channel_id=1, source_target_pairs={{4,8},{8,4},{5,9},{9,5},{6,10},{10,6},{7,11},{11,7},{20,24},{24,20... | collective-permute-start | bytes 3145736 | tf_op jit(solution)/shard_map/ppermute | solution.py:352
  180.5 24.0 %collective-permute-start.29 = (bf16[256,8,256]{2,1,0:T(8,128)(2,1)}, bf16[256,8,256]{2,1,0:T(8,128)(2,1)S(1)}, u32[]{:S(2)}, u32[]{:S(2)}) collective-permute-start(bf16[256,8,256]{2,1,0:T(8,128)(2,1)} %get-tuple-element.206), channel_id=1, source_target_pairs={{4,0},{8,12},{5,1},{9,13},{6,2},{10,14},{7,3},{11,15},{20,16},{24,... | collective-permute-start | bytes 3145736 | tf_op jit(solution)/shard_map/ppermute | solution.py:352
  190.2 29.4 %collective-permute-start.26 = (bf16[16,128,256]{2,1,0:T(8,128)(2,1)}, bf16[16,128,256]{2,1,0:T(8,128)(2,1)S(1)}, u32[]{:S(2)}, u32[]{:S(2)}) collective-permute-start(bf16[16,128,256]{2,1,0:T(8,128)(2,1)} %pack.7), channel_id=1, source_target_pairs={{4,8},{8,4},{5,9},{9,5},{6,10},{10,6},{7,11},{11,7},{20,24},{24,20... | collective-permute-start | bytes 3145736 | tf_op jit(solution)/shard_map/ppermute | solution.py:352
  200.9 26.3 %collective-permute-start.31 = (bf16[256,8,256]{2,1,0:T(8,128)(2,1)}, bf16[256,8,256]{2,1,0:T(8,128)(2,1)}, u32[]{:S(2)}, u32[]{:S(2)}) collective-permute-start(bf16[256,8,256]{2,1,0:T(8,128)(2,1)} %get-tuple-element.222), channel_id=1, source_target_pairs={{4,0},{8,12},{5,1},{9,13},{6,2},{10,14},{7,3},{11,15},{20,16},{24,... | collective-permute-start | bytes 3145736 | tf_op jit(solution)/shard_map/ppermute | solution.py:352
  205.6 30.2 %collective-permute-start.32 = (bf16[16,128,256]{2,1,0:T(8,128)(2,1)S(1)}, bf16[16,128,256]{2,1,0:T(8,128)(2,1)}, u32[]{:S(2)}, u32[]{:S(2)}) collective-permute-start(bf16[16,128,256]{2,1,0:T(8,128)(2,1)S(1)} %pack.9), channel_id=1, source_target_pairs={{4,8},{8,4},{5,9},{9,5},{6,10},{10,6},{7,11},{11,7},{20,24},{24,20... | collective-permute-start | bytes 3145736 | tf_op jit(solution)/shard_map/ppermute | solution.py:352
  225.2 25.9 %collective-permute-start.34 = (bf16[256,8,256]{2,1,0:T(8,128)(2,1)}, bf16[256,8,256]{2,1,0:T(8,128)(2,1)S(1)}, u32[]{:S(2)}, u32[]{:S(2)}) collective-permute-start(bf16[256,8,256]{2,1,0:T(8,128)(2,1)} %get-tuple-element.232), channel_id=1, source_target_pairs={{4,0},{8,12},{5,1},{9,13},{6,2},{10,14},{7,3},{11,15},{20,16},{24,... | collective-permute-start | bytes 3145736 | tf_op jit(solution)/shard_map/ppermute | solution.py:352
  244.3 31.4 %collective-permute-start.36 = (bf16[256,8,256]{2,1,0:T(8,128)(2,1)}, bf16[256,8,256]{2,1,0:T(8,128)(2,1)S(1)}, u32[]{:S(2)}, u32[]{:S(2)}) collective-permute-start(bf16[256,8,256]{2,1,0:T(8,128)(2,1)} %get-tuple-element.240), channel_id=1, source_target_pairs={{4,0},{8,12},{5,1},{9,13},{6,2},{10,14},{7,3},{11,15},{20,16},{24,... | collective-permute-start | bytes 3145736 | tf_op jit(solution)/shard_map/ppermute | solution.py:352
  252.2 24.5 %collective-permute-start.35 = (bf16[16,128,128]{2,1,0:T(8,128)(2,1)S(1)}, bf16[16,128,128]{2,1,0:T(8,128)(2,1)S(1)}, u32[]{:S(2)}, u32[]{:S(2)}) collective-permute-start(bf16[16,128,128]{2,1,0:T(8,128)(2,1)S(1)} %pack.10), channel_id=1, source_target_pairs={{4,8},{8,4},{5,9},{9,5},{6,10},{10,6},{7,11},{11,7},{20,24},{24,20... | collective-permute-start | bytes 1572872 | tf_op jit(solution)/shard_map/ppermute | solution.py:352
  256.5 30.4 %collective-permute-start.39 = (bf16[256,8,128]{2,1,0:T(8,128)(2,1)}, bf16[256,8,128]{2,1,0:T(8,128)(2,1)S(1)}, u32[]{:S(2)}, u32[]{:S(2)}) collective-permute-start(bf16[256,8,128]{2,1,0:T(8,128)(2,1)} %get-tuple-element.247), channel_id=1, source_target_pairs={{4,0},{8,12},{5,1},{9,13},{6,2},{10,14},{7,3},{11,15},{20,16},{24,... | collective-permute-start | bytes 1572872 | tf_op jit(solution)/shard_map/ppermute | solution.py:352
  (61 other events, 1287.1 us)

commit v4 on v3

--- a/solution.py
+++ b/solution.py
@@ -451,9 +451,19 @@
     def early_time(out):
         arrays, specs = zip(*sum(chunk_sources(RAW_TILES, False), []))
         plan = [1] * len(arrays)
-        return time_call(
-            arrays, plan, list(specs), 2 * n_time, out, raw, 1, "time_early"
-        )
+        theirs = pl.pallas_call(
+            partial(time_kernel, plan, 1, 0),
+            grid=(1,),
+            in_specs=[whole(SMEM), pl.BlockSpec((n_time, 2 * NF), lambda c: (1, 0))] + list(specs),
+            out_specs=[still((n_time, OCT, TILE))],
+            out_shape=[sds((n_time, OCT, TILE), bf16)],
+            scratch_shapes=[VMEM((1, TILE // LANES, n_time * OCT, LANES), f32)],
+            compiler_params=WIDE_PARAMS,
+            cost_estimate=cost(0, 0),
+            name="time_theirs",
+        )(level, table, *arrays)[0]
+        own = time_call(arrays, plan, list(specs), n_time, out, raw, 1, "time_own")[0]
+        return own, theirs
 
     def late_time(q, out):
         sources = [lates[q], swaps_in[q], mids_in[q]]
@@ -492,9 +502,9 @@
     crosses[last], far_out[last - 1], lates[1] = tie(crosses[last], far_out[last - 1], lates[1])
     far_out[last] = send(cut(crosses[last]), OUTWARD)
     out, theirs = early_time(None)
+    swaps_in[0], theirs, lates[1] = tie(swaps_in[0], theirs, lates[1])
     theirs, near_out[last], far_out[last] = tie(theirs, near_out[last], far_out[last])
     ends[0] = send(theirs, OUTWARD)
-    swaps_in[0], out, lates[1] = tie(swaps_in[0], out, lates[1])
     mids_in[0] = send(pack(lates[0], swaps_in[0], late_widths[0]), MIDDLE)
     swaps_in[1] = send(lates[1], INWARD)
     for q in range(late):

time: 298 us -> 297 us (level)
  waiting for transfers between devices: 114 us -> 105 us
  starting transfers between devices: 73.1 us -> 77.3 us
  Pallas kernels: 82.9 us -> 86.5 us
    ppermute x34, waiting for transfers between devices: 94.3 us -> 86.8 us  [line_body(): send = lambda a, pairs: lax.ppermute(a, 'freq', pairs)]
    ppermute x34, starting transfers between devices: 68.5 us -> 72.7 us  [line_body(): send = lambda a, pairs: lax.ppermute(a, 'freq', pairs)]
    pallas_call x0 -> x1, Pallas kernels: none -> 3.63 us  [early_time(): pl.pallas_call(partial(time_kernel, plan, 1, 0), grid=(1,), in_specs=[who...]
    unnamed x91 -> x93, local copies, waits for them, and re-layouts: 14 us -> 14.4 us
  transfers between devices with their start and end apart: 40 -> 40, of which waited for: 21 -> 20; matrix products, arithmetic and copies ran while one was open for 3% -> 3% of each run, Pallas kernels for 27% -> 28%
where the time goes in v4:
time: 297 us; the launch traced here: 295 us
  waiting for transfers between devices  105 us (35%)
  Pallas kernels  86.5 us (29%)
  starting transfers between devices  77.3 us (26%)
  local copies, waits for them, and re-layouts  17 us (6%)
  other arithmetic  6.95 us (2%)
    ppermute x34, waiting for transfers between devices, line_body(): send = lambda a, pairs: lax.ppermute(a, 'freq', pairs)  86.8 us
    ppermute x34, starting transfers between devices, line_body(): send = lambda a, pairs: lax.ppermute(a, 'freq', pairs)  72.7 us
    pallas_call x8, Pallas kernels, time_call(): pl.pallas_call(partial(time_kernel, plan, blocks, aliased), grid=(grid,),...  34.4 us
    ppermute x3, waiting for transfers between devices, line_body(): others = [lax.ppermute(a, 'shot', ((0, 1), (1, 0))) for a in downs]  15.1 us
    unnamed x93, local copies, waits for them, and re-layouts  14.4 us
    pallas_call x3, Pallas kernels, line_body(): kernel(rows_kernel, SIZES[k], in_specs=[whole(SMEM), pl.BlockSpec((2, OCT...  12.1 us
    pallas_call x7, Pallas kernels, place(): pl.pallas_call(partial(place_kernel, late_first[j - 1] if j else raw), in...  9.27 us
    pallas_call x3, Pallas kernels, line_body(): kernel(partial(down_kernel, first_group[k] * OCT), SIZES[k], in_specs=[pl...  9.26 us
  transfers between devices with their start and end apart: 40, of which 20 were waited for; matrix products, arithmetic and copies ran while one was open for 3% of the time, Pallas kernels for 28%

profile of v4, /device:TPU:0, one launch (start us, length us, event | category | flops | bytes accessed | tf_op | source)
XLA Modules:
  0.0 295.5 jit_solution(9818083612159474243)
XLA Ops:
  10.8 4.4 %rows.4 = (bf16[3,128,2048]{2,1,0:T(8,128)(2,1)}, f32[3,128,128]{2,1,0:T(8,128)}, f32[3,2,64,128]{3,2,1,0:T(8,128)}) custom-call(s32[1]{0:T(128)} %bitcast.6.side_ref, bf16[2,64,8,2048]{3,2,1,0:T(8,128)(2,1)} %est_ref.5, bf16[2,64,8,16]{3,2,1,0:T(8,128)(2,1)} %copy.35.win_ref, bf16[3,128,2048]{2,1,0:T(8,128)(2,1)} %down.4.down_ref.own_ref), custom_call_target="tpu_custom_call" | custom-call | tf_op jit(solution)/shard_map/rows/pallas_call | solution.py:328
  19.4 5.6 %fusion.3.table_ref = bf16[512,512]{1,0:T(8,128)(2,1)} fusion(s32[512]{0:T(512)S(1)} %mul.40, s32[512]{0:T(512)S(1)} %pad_add_fusion, pred[512]{0:T(512)(128)(4,1)S(1)} %fusion.5), kind=kLoop, calls=%fused_computation.10 | loop fusion | flops 5505024 | bytes 528896 | tf_op jit(solution)/shard_map/mul | solution.py:296
  25.0 5.5 %collective-permute-done.other_ref = bf16[2,128,2048]{2,1,0:T(8,128)(2,1)S(1)} collective-permute-done((bf16[2,128,2048]{2,1,0:T(8,128)(2,1)}, bf16[2,128,2048]{2,1,0:T(8,128)(2,1)S(1)}, u32[]{:S(2)}, u32[]{:S(2)}) %collective-permute-start) | collective-permute-done | bytes 1048608 | tf_op jit(solution)/shard_map/ppermute | solution.py:325
  48.2 4.4 %rows.5 = (bf16[3,128,2048]{2,1,0:T(8,128)(2,1)}, f32[3,128,128]{2,1,0:T(8,128)}, f32[3,2,64,128]{3,2,1,0:T(8,128)}) custom-call(s32[1]{0:T(128)} %bitcast.6.side_ref, bf16[2,64,8,2048]{3,2,1,0:T(8,128)(2,1)} %est_ref.5, bf16[2,64,8,16]{3,2,1,0:T(8,128)(2,1)} %copy.35.win_ref, bf16[3,128,2048]{2,1,0:T(8,128)(2,1)} %down.5.down_ref.own_ref), custom_call_target="tpu_custom_call" | custom-call | tf_op jit(solution)/shard_map/rows/pallas_call | solution.py:328
  55.8 8.5 %collective-permute-done.4.other_ref = bf16[3,128,2048]{2,1,0:T(8,128)(2,1)} collective-permute-done((bf16[3,128,2048]{2,1,0:T(8,128)(2,1)}, bf16[3,128,2048]{2,1,0:T(8,128)(2,1)}, u32[]{:S(2)}, u32[]{:S(2)}) %collective-permute-start.4) | collective-permute-done | bytes 1572896 | tf_op jit(solution)/shard_map/ppermute | solution.py:325
  79.8 12.9 %collective-permute-done.9.rest_4_ = bf16[3,128,768]{2,1,0:T(8,128)(2,1)S(1)} collective-permute-done((bf16[3,128,768]{2,1,0:T(8,128)(2,1)S(1)}, bf16[3,128,768]{2,1,0:T(8,128)(2,1)S(1)}, u32[]{:S(2)}, u32[]{:S(2)}) %collective-permute-start.9) | collective-permute-done | bytes 589856 | tf_op jit(solution)/shard_map/ppermute | solution.py:352
  109.3 4.0 %collective-permute-done.14.rest_13_ = bf16[2,128,512]{2,1,0:T(8,128)(2,1)S(1)} collective-permute-done((bf16[2,128,512]{2,1,0:T(8,128)(2,1)S(1)}, bf16[2,128,512]{2,1,0:T(8,128)(2,1)S(1)}, u32[]{:S(2)}, u32[]{:S(2)}) %collective-permute-start.14) | collective-permute-done | bytes 262176 | tf_op jit(solution)/shard_map/ppermute | solution.py:352
  114.0 13.0 %collective-permute-done.15.rest_5_ = bf16[3,128,768]{2,1,0:T(8,128)(2,1)S(1)} collective-permute-done((bf16[3,128,768]{2,1,0:T(8,128)(2,1)S(1)}, bf16[3,128,768]{2,1,0:T(8,128)(2,1)S(1)}, u32[]{:S(2)}, u32[]{:S(2)}) %collective-permute-start.15) | collective-permute-done | bytes 589856 | tf_op jit(solution)/shard_map/ppermute | solution.py:352
  129.1 4.6 %collective-permute-start.16 = (bf16[8,128,256]{2,1,0:T(8,128)(2,1)S(1)}, bf16[8,128,256]{2,1,0:T(8,128)(2,1)S(1)}, u32[]{:S(2)}, u32[]{:S(2)}) collective-permute-start(bf16[8,128,256]{2,1,0:T(8,128)(2,1)S(1)} %get-tuple-element.175.a_ref.rest_0_), channel_id=1, source_target_pairs={{0,4},{12,8},{1,5},{13,9},{2,6},{14,10},{3,7},{15,11},{16,20},{28,... | collective-permute-start | bytes 1572872 | tf_op jit(solution)/shard_map/ppermute | solution.py:352
  135.1 6.4 %collective-permute-done.19.rest_15_ = bf16[3,128,512]{2,1,0:T(8,128)(2,1)S(1)} collective-permute-done((bf16[3,128,512]{2,1,0:T(8,128)(2,1)S(1)}, bf16[3,128,512]{2,1,0:T(8,128)(2,1)S(1)}, u32[]{:S(2)}, u32[]{:S(2)}) %collective-permute-start.19) | collective-permute-done | bytes 393248 | tf_op jit(solution)/shard_map/ppermute | solution.py:352
  148.7 5.3 %collective-permute-start.20 = (bf16[8,128,256]{2,1,0:T(8,128)(2,1)S(1)}, bf16[8,128,256]{2,1,0:T(8,128)(2,1)S(1)}, u32[]{:S(2)}, u32[]{:S(2)}) collective-permute-start(bf16[8,128,256]{2,1,0:T(8,128)(2,1)S(1)} %get-tuple-element.185.a_ref.rest_0_), channel_id=1, source_target_pairs={{0,4},{12,8},{1,5},{13,9},{2,6},{14,10},{3,7},{15,11},{16,20},{28,... | collective-permute-start | bytes 1572872 | tf_op jit(solution)/shard_map/ppermute | solution.py:352
  162.5 4.8 %collective-permute-start.22 = (bf16[8,128,256]{2,1,0:T(8,128)(2,1)S(1)}, bf16[8,128,256]{2,1,0:T(8,128)(2,1)S(1)}, u32[]{:S(2)}, u32[]{:S(2)}) collective-permute-start(bf16[8,128,256]{2,1,0:T(8,128)(2,1)S(1)} %get-tuple-element.187.a_ref.rest_0_), channel_id=1, source_target_pairs={{0,4},{12,8},{1,5},{13,9},{2,6},{14,10},{3,7},{15,11},{16,20},{28,... | collective-permute-start | bytes 1572872 | tf_op jit(solution)/shard_map/ppermute | solution.py:352
  170.0 5.2 %collective-permute-done.22.b_ref.rest_1_ = bf16[8,128,256]{2,1,0:T(8,128)(2,1)S(1)} collective-permute-done((bf16[8,128,256]{2,1,0:T(8,128)(2,1)S(1)}, bf16[8,128,256]{2,1,0:T(8,128)(2,1)S(1)}, u32[]{:S(2)}, u32[]{:S(2)}) %collective-permute-start.22) | collective-permute-done | bytes 524320 | tf_op jit(solution)/shard_map/ppermute | solution.py:352
  175.3 4.7 %time_late.6 = (bf16[256,8,2048]{2,1,0:T(8,128)(2,1)}, bf16[256,8,256]{2,1,0:T(8,128)(2,1)}) custom-call(f32[1]{0:T(128)S(6)} %div.11.level_ref, bf16[512,512]{1,0:T(8,128)(2,1)} %fusion.3.table_ref, bf16[8,128,256]{2,1,0:T(8,128)(2,1)} %copy-done.3, bf16[8,128,256]{2,1,0:T(8,128)(2,1)} %copy-done.22, ...), custom_call_target="tpu_custom_call", output_to_operand_aliasing={{0}: (5, {})} | custom-call | tf_op jit(solution)/shard_map/time_late/pallas_call | solution.py:429
  183.5 7.2 %collective-permute-start.28 = (bf16[8,128,256]{2,1,0:T(8,128)(2,1)S(1)}, bf16[8,128,256]{2,1,0:T(8,128)(2,1)S(1)}, u32[]{:S(2)}, u32[]{:S(2)}) collective-permute-start(bf16[8,128,256]{2,1,0:T(8,128)(2,1)S(1)} %get-tuple-element.200.a_ref.rest_0_), channel_id=1, source_target_pairs={{0,4},{12,8},{1,5},{13,9},{2,6},{14,10},{3,7},{15,11},{16,20},{28,... | collective-permute-start | bytes 1572872 | tf_op jit(solution)/shard_map/ppermute | solution.py:352
  193.4 5.0 %time_raw.1.rest_3_ = bf16[256,8,2048]{2,1,0:T(8,128)(2,1)} custom-call(f32[1]{0:T(128)S(6)} %div.11.level_ref, bf16[512,512]{1,0:T(8,128)(2,1)} %fusion.3.table_ref, bf16[2,128,768]{2,1,0:T(8,128)(2,1)} %get-tuple-element.136.rest_0_, bf16[3,128,768]{2,1,0:T(8,128)(2,1)} %copy-done.9, ...), custom_call_target="tpu_custom_call", output_to_operand_aliasing={{}: (20, {})} | custom-call | tf_op jit(solution)/shard_map/time_raw/pallas_call | solution.py:429
  198.4 4.7 %time_late.7 = (bf16[256,8,2048]{2,1,0:T(8,128)(2,1)}, bf16[256,8,256]{2,1,0:T(8,128)(2,1)}) custom-call(f32[1]{0:T(128)S(6)} %div.11.level_ref, bf16[512,512]{1,0:T(8,128)(2,1)} %fusion.3.table_ref, bf16[8,128,256]{2,1,0:T(8,128)(2,1)} %copy-done.4, bf16[8,128,256]{2,1,0:T(8,128)(2,1)} %copy-done.20, ...), custom_call_target="tpu_custom_call", output_to_operand_aliasing={{0}: (5, {})} | custom-call | tf_op jit(solution)/shard_map/time_late/pallas_call | solution.py:429
  207.3 9.8 %collective-permute-start.30 = (bf16[8,128,128]{2,1,0:T(8,128)(2,1)S(1)}, bf16[8,128,128]{2,1,0:T(8,128)(2,1)S(1)}, u32[]{:S(2)}, u32[]{:S(2)}) collective-permute-start(bf16[8,128,128]{2,1,0:T(8,128)(2,1)S(1)} %get-tuple-element.216.a_ref.rest_0_), channel_id=1, source_target_pairs={{0,4},{12,8},{1,5},{13,9},{2,6},{14,10},{3,7},{15,11},{16,20},{28,... | collective-permute-start | bytes 786440 | tf_op jit(solution)/shard_map/ppermute | solution.py:352
  220.9 4.6 %time_late.8 = (bf16[256,8,2048]{2,1,0:T(8,128)(2,1)}, bf16[256,8,256]{2,1,0:T(8,128)(2,1)}) custom-call(f32[1]{0:T(128)S(6)} %div.11.level_ref, bf16[512,512]{1,0:T(8,128)(2,1)} %fusion.3.table_ref, bf16[8,128,256]{2,1,0:T(8,128)(2,1)} %copy-done.5, bf16[8,128,256]{2,1,0:T(8,128)(2,1)} %copy-done.19, ...), custom_call_target="tpu_custom_call", output_to_operand_aliasing={{0}: (5, {})} | custom-call | tf_op jit(solution)/shard_map/time_late/pallas_call | solution.py:429
  229.5 7.0 %collective-permute-start.33 = (bf16[8,128,128]{2,1,0:T(8,128)(2,1)S(1)}, bf16[8,128,128]{2,1,0:T(8,128)(2,1)S(1)}, u32[]{:S(2)}, u32[]{:S(2)}) collective-permute-start(bf16[8,128,128]{2,1,0:T(8,128)(2,1)S(1)} %copy-done.15), channel_id=1, source_target_pairs={{0,4},{12,8},{1,5},{13,9},{2,6},{14,10},{3,7},{15,11},{16,20},{28,... | collective-permute-start | bytes 786440 | tf_op jit(solution)/shard_map/ppermute | solution.py:352
  240.4 4.6 %time_late.9 = (bf16[256,8,2048]{2,1,0:T(8,128)(2,1)}, bf16[256,8,256]{2,1,0:T(8,128)(2,1)}) custom-call(f32[1]{0:T(128)S(6)} %div.11.level_ref, bf16[512,512]{1,0:T(8,128)(2,1)} %fusion.3.table_ref, bf16[8,128,256]{2,1,0:T(8,128)(2,1)} %copy-done.6, bf16[8,128,256]{2,1,0:T(8,128)(2,1)} %copy-done.21, ...), custom_call_target="tpu_custom_call", output_to_operand_aliasing={{0}: (5, {})} | custom-call | tf_op jit(solution)/shard_map/time_late/pallas_call | solution.py:429
  257.0 19.5 %collective-permute-done.36.got_ref = bf16[256,8,256]{2,1,0:T(8,128)(2,1)S(1)} collective-permute-done((bf16[256,8,256]{2,1,0:T(8,128)(2,1)}, bf16[256,8,256]{2,1,0:T(8,128)(2,1)S(1)}, u32[]{:S(2)}, u32[]{:S(2)}) %collective-permute-start.36) | collective-permute-done | bytes 1048608 | tf_op jit(solution)/shard_map/ppermute | solution.py:352
  283.2 4.6 %collective-permute-done.39.got_ref = bf16[256,8,128]{2,1,0:T(8,128)(2,1)S(1)} collective-permute-done((bf16[256,8,128]{2,1,0:T(8,128)(2,1)}, bf16[256,8,128]{2,1,0:T(8,128)(2,1)S(1)}, u32[]{:S(2)}, u32[]{:S(2)}) %collective-permute-start.39) | collective-permute-done | bytes 524320 | tf_op jit(solution)/shard_map/ppermute | solution.py:352
  288.6 5.8 %collective-permute-done.38.got_ref = bf16[256,8,128]{2,1,0:T(8,128)(2,1)S(1)} collective-permute-done((bf16[256,8,128]{2,1,0:T(8,128)(2,1)}, bf16[256,8,128]{2,1,0:T(8,128)(2,1)S(1)}, u32[]{:S(2)}, u32[]{:S(2)}) %collective-permute-start.38) | collective-permute-done | bytes 524320 | tf_op jit(solution)/shard_map/ppermute | solution.py:352
  (200 shorter events, 130.9 us)
Async XLA Ops:
  3.4 27.1 %collective-permute-start = (bf16[2,128,2048]{2,1,0:T(8,128)(2,1)}, bf16[2,128,2048]{2,1,0:T(8,128)(2,1)S(1)}, u32[]{:S(2)}, u32[]{:S(2)}) collective-permute-start(bf16[2,128,2048]{2,1,0:T(8,128)(2,1)} %down.3.down_ref.own_ref), channel_id=1, source_target_pairs={{0,2},{2,0},{1,3},{3,1},{4,6},{6,4},{5,7},{7,5},{8,10},{10,8},{9,1... | collective-permute-start | bytes 3145736 | tf_op jit(solution)/shard_map/ppermute | solution.py:325
  9.9 54.5 %collective-permute-start.4 = (bf16[3,128,2048]{2,1,0:T(8,128)(2,1)}, bf16[3,128,2048]{2,1,0:T(8,128)(2,1)}, u32[]{:S(2)}, u32[]{:S(2)}) collective-permute-start(bf16[3,128,2048]{2,1,0:T(8,128)(2,1)} %down.4.down_ref.own_ref), channel_id=1, source_target_pairs={{0,2},{2,0},{1,3},{3,1},{4,6},{6,4},{5,7},{7,5},{8,10},{10,8},{9,1... | collective-permute-start | bytes 4718600 | tf_op jit(solution)/shard_map/ppermute | solution.py:325
  46.8 50.4 %collective-permute-start.3 = (bf16[3,128,2048]{2,1,0:T(8,128)(2,1)}, bf16[3,128,2048]{2,1,0:T(8,128)(2,1)}, u32[]{:S(2)}, u32[]{:S(2)}) collective-permute-start(bf16[3,128,2048]{2,1,0:T(8,128)(2,1)} %down.5.down_ref.own_ref), channel_id=1, source_target_pairs={{0,2},{2,0},{1,3},{3,1},{4,6},{6,4},{5,7},{7,5},{8,10},{10,8},{9,1... | collective-permute-start | bytes 4718600 | tf_op jit(solution)/shard_map/ppermute | solution.py:325
  52.7 23.5 %collective-permute-start.7 = (bf16[2,128,768]{2,1,0:T(8,128)(2,1)}, bf16[2,128,768]{2,1,0:T(8,128)(2,1)S(1)}, u32[]{:S(2)}, u32[]{:S(2)}) collective-permute-start(bf16[2,128,768]{2,1,0:T(8,128)(2,1)} %collective-permute-done.2.rest_3_), channel_id=1, source_target_pairs={{4,8},{8,4},{5,9},{9,5},{6,10},{10,6},{7,11},{11,7},{20,24},{24,20... | collective-permute-start | bytes 1179656 | tf_op jit(solution)/shard_map/ppermute | solution.py:352
  54.5 21.7 %collective-permute-start.8 = (bf16[2,128,512]{2,1,0:T(8,128)(2,1)S(1)}, bf16[2,128,512]{2,1,0:T(8,128)(2,1)S(1)}, u32[]{:S(2)}, u32[]{:S(2)}) collective-permute-start(bf16[2,128,512]{2,1,0:T(8,128)(2,1)S(1)} %slice.26), channel_id=1, source_target_pairs={{4,0},{8,12},{5,1},{9,13},{6,2},{10,14},{7,3},{11,15},{20,16},{24,... | collective-permute-start | bytes 786440 | tf_op jit(solution)/shard_map/ppermute | solution.py:352
  77.0 15.8 %collective-permute-start.9 = (bf16[3,128,768]{2,1,0:T(8,128)(2,1)S(1)}, bf16[3,128,768]{2,1,0:T(8,128)(2,1)S(1)}, u32[]{:S(2)}, u32[]{:S(2)}) collective-permute-start(bf16[3,128,768]{2,1,0:T(8,128)(2,1)S(1)} %get-tuple-element.155.rest_1_), channel_id=1, source_target_pairs={{0,4},{4,0},{8,12},{12,8},{1,5},{5,1},{9,13},{13,9},{2,6},{6,2},{1... | collective-permute-start | bytes 1769480 | tf_op jit(solution)/shard_map/ppermute | solution.py:352
  93.5 15.8 %collective-permute-start.13 = (bf16[3,128,512]{2,1,0:T(8,128)(2,1)S(1)}, bf16[3,128,512]{2,1,0:T(8,128)(2,1)S(1)}, u32[]{:S(2)}, u32[]{:S(2)}) collective-permute-start(bf16[3,128,512]{2,1,0:T(8,128)(2,1)S(1)} %slice.27), channel_id=1, source_target_pairs={{4,0},{8,12},{5,1},{9,13},{6,2},{10,14},{7,3},{11,15},{20,16},{24,... | collective-permute-start | bytes 1179656 | tf_op jit(solution)/shard_map/ppermute | solution.py:352
  94.8 18.5 %collective-permute-start.14 = (bf16[2,128,512]{2,1,0:T(8,128)(2,1)S(1)}, bf16[2,128,512]{2,1,0:T(8,128)(2,1)S(1)}, u32[]{:S(2)}, u32[]{:S(2)}) collective-permute-start(bf16[2,128,512]{2,1,0:T(8,128)(2,1)S(1)} %slice.20), channel_id=1, source_target_pairs={{4,0},{8,12},{5,1},{9,13},{6,2},{10,14},{7,3},{11,15},{20,16},{24,... | collective-permute-start | bytes 786440 | tf_op jit(solution)/shard_map/ppermute | solution.py:352
  113.3 20.4 %collective-permute-start.17 = (bf16[3,128,768]{2,1,0:T(8,128)(2,1)S(1)}, bf16[3,128,768]{2,1,0:T(8,128)(2,1)S(1)}, u32[]{:S(2)}, u32[]{:S(2)}) collective-permute-start(bf16[3,128,768]{2,1,0:T(8,128)(2,1)S(1)} %get-tuple-element.173.rest_2_), channel_id=1, source_target_pairs={{4,8},{8,4},{5,9},{9,5},{6,10},{10,6},{7,11},{11,7},{20,24},{24,20... | collective-permute-start | bytes 1769480 | tf_op jit(solution)/shard_map/ppermute | solution.py:352
  127.0 14.4 %collective-permute-start.18 = (bf16[3,128,768]{2,1,0:T(8,128)(2,1)S(1)}, bf16[3,128,768]{2,1,0:T(8,128)(2,1)S(1)}, u32[]{:S(2)}, u32[]{:S(2)}) collective-permute-start(bf16[3,128,768]{2,1,0:T(8,128)(2,1)S(1)} %collective-permute-done.15.rest_5_), channel_id=1, source_target_pairs={{4,8},{8,4},{5,9},{9,5},{6,10},{10,6},{7,11},{11,7},{20,24},{24,20... | collective-permute-start | bytes 1769480 | tf_op jit(solution)/shard_map/ppermute | solution.py:352
  129.1 19.7 %collective-permute-start.16 = (bf16[8,128,256]{2,1,0:T(8,128)(2,1)S(1)}, bf16[8,128,256]{2,1,0:T(8,128)(2,1)S(1)}, u32[]{:S(2)}, u32[]{:S(2)}) collective-permute-start(bf16[8,128,256]{2,1,0:T(8,128)(2,1)S(1)} %get-tuple-element.175.a_ref.rest_0_), channel_id=1, source_target_pairs={{0,4},{12,8},{1,5},{13,9},{2,6},{14,10},{3,7},{15,11},{16,20},{28,... | collective-permute-start | bytes 1572872 | tf_op jit(solution)/shard_map/ppermute | solution.py:352
  133.8 23.0 %collective-permute-start.23 = (bf16[3,128,512]{2,1,0:T(8,128)(2,1)S(1)}, bf16[3,128,512]{2,1,0:T(8,128)(2,1)}, u32[]{:S(2)}, u32[]{:S(2)}) collective-permute-start(bf16[3,128,512]{2,1,0:T(8,128)(2,1)S(1)} %slice.28), channel_id=1, source_target_pairs={{4,0},{8,12},{5,1},{9,13},{6,2},{10,14},{7,3},{11,15},{20,16},{24,... | collective-permute-start | bytes 1179656 | tf_op jit(solution)/shard_map/ppermute | solution.py:352
  155.2 20.1 %collective-permute-start.21 = (bf16[16,128,256]{2,1,0:T(8,128)(2,1)}, bf16[16,128,256]{2,1,0:T(8,128)(2,1)}, u32[]{:S(2)}, u32[]{:S(2)}) collective-permute-start(bf16[16,128,256]{2,1,0:T(8,128)(2,1)} %pack.6), channel_id=1, source_target_pairs={{4,8},{8,4},{5,9},{9,5},{6,10},{10,6},{7,11},{11,7},{20,24},{24,20... | collective-permute-start | bytes 3145736 | tf_op jit(solution)/shard_map/ppermute | solution.py:352
  156.8 24.5 %collective-permute-start.25 = (bf16[256,8,256]{2,1,0:T(8,128)(2,1)}, bf16[256,8,256]{2,1,0:T(8,128)(2,1)}, u32[]{:S(2)}, u32[]{:S(2)}) collective-permute-start(bf16[256,8,256]{2,1,0:T(8,128)(2,1)} %time_theirs.1), channel_id=1, source_target_pairs={{4,0},{8,12},{5,1},{9,13},{6,2},{10,14},{7,3},{11,15},{20,16},{24,... | collective-permute-start | bytes 3145736 | tf_op jit(solution)/shard_map/ppermute | solution.py:352
  168.4 30.0 %collective-permute-start.27 = (bf16[16,128,256]{2,1,0:T(8,128)(2,1)}, bf16[16,128,256]{2,1,0:T(8,128)(2,1)}, u32[]{:S(2)}, u32[]{:S(2)}) collective-permute-start(bf16[16,128,256]{2,1,0:T(8,128)(2,1)} %pack.8), channel_id=1, source_target_pairs={{4,8},{8,4},{5,9},{9,5},{6,10},{10,6},{7,11},{11,7},{20,24},{24,20... | collective-permute-start | bytes 3145736 | tf_op jit(solution)/shard_map/ppermute | solution.py:352
  180.0 24.4 %collective-permute-start.29 = (bf16[256,8,256]{2,1,0:T(8,128)(2,1)}, bf16[256,8,256]{2,1,0:T(8,128)(2,1)S(1)}, u32[]{:S(2)}, u32[]{:S(2)}) collective-permute-start(bf16[256,8,256]{2,1,0:T(8,128)(2,1)} %get-tuple-element.202), channel_id=1, source_target_pairs={{4,0},{8,12},{5,1},{9,13},{6,2},{10,14},{7,3},{11,15},{20,16},{24,... | collective-permute-start | bytes 3145736 | tf_op jit(solution)/shard_map/ppermute | solution.py:352
  183.5 14.9 %collective-permute-start.28 = (bf16[8,128,256]{2,1,0:T(8,128)(2,1)S(1)}, bf16[8,128,256]{2,1,0:T(8,128)(2,1)S(1)}, u32[]{:S(2)}, u32[]{:S(2)}) collective-permute-start(bf16[8,128,256]{2,1,0:T(8,128)(2,1)S(1)} %get-tuple-element.200.a_ref.rest_0_), channel_id=1, source_target_pairs={{0,4},{12,8},{1,5},{13,9},{2,6},{14,10},{3,7},{15,11},{16,20},{28,... | collective-permute-start | bytes 1572872 | tf_op jit(solution)/shard_map/ppermute | solution.py:352
  191.8 29.1 %collective-permute-start.26 = (bf16[16,128,256]{2,1,0:T(8,128)(2,1)}, bf16[16,128,256]{2,1,0:T(8,128)(2,1)}, u32[]{:S(2)}, u32[]{:S(2)}) collective-permute-start(bf16[16,128,256]{2,1,0:T(8,128)(2,1)} %pack.7), channel_id=1, source_target_pairs={{4,8},{8,4},{5,9},{9,5},{6,10},{10,6},{7,11},{11,7},{20,24},{24,20... | collective-permute-start | bytes 3145736 | tf_op jit(solution)/shard_map/ppermute | solution.py:352
  203.1 24.1 %collective-permute-start.31 = (bf16[256,8,256]{2,1,0:T(8,128)(2,1)}, bf16[256,8,256]{2,1,0:T(8,128)(2,1)}, u32[]{:S(2)}, u32[]{:S(2)}) collective-permute-start(bf16[256,8,256]{2,1,0:T(8,128)(2,1)} %get-tuple-element.218), channel_id=1, source_target_pairs={{4,0},{8,12},{5,1},{9,13},{6,2},{10,14},{7,3},{11,15},{20,16},{24,... | collective-permute-start | bytes 3145736 | tf_op jit(solution)/shard_map/ppermute | solution.py:352
  205.6 30.9 %collective-permute-start.32 = (bf16[16,128,256]{2,1,0:T(8,128)(2,1)S(1)}, bf16[16,128,256]{2,1,0:T(8,128)(2,1)}, u32[]{:S(2)}, u32[]{:S(2)}) collective-permute-start(bf16[16,128,256]{2,1,0:T(8,128)(2,1)S(1)} %pack.9), channel_id=1, source_target_pairs={{4,8},{8,4},{5,9},{9,5},{6,10},{10,6},{7,11},{11,7},{20,24},{24,20... | collective-permute-start | bytes 3145736 | tf_op jit(solution)/shard_map/ppermute | solution.py:352
  225.6 24.0 %collective-permute-start.34 = (bf16[256,8,256]{2,1,0:T(8,128)(2,1)}, bf16[256,8,256]{2,1,0:T(8,128)(2,1)S(1)}, u32[]{:S(2)}, u32[]{:S(2)}) collective-permute-start(bf16[256,8,256]{2,1,0:T(8,128)(2,1)} %get-tuple-element.228), channel_id=1, source_target_pairs={{4,0},{8,12},{5,1},{9,13},{6,2},{10,14},{7,3},{11,15},{20,16},{24,... | collective-permute-start | bytes 3145736 | tf_op jit(solution)/shard_map/ppermute | solution.py:352
  245.0 31.5 %collective-permute-start.36 = (bf16[256,8,256]{2,1,0:T(8,128)(2,1)}, bf16[256,8,256]{2,1,0:T(8,128)(2,1)S(1)}, u32[]{:S(2)}, u32[]{:S(2)}) collective-permute-start(bf16[256,8,256]{2,1,0:T(8,128)(2,1)} %get-tuple-element.236), channel_id=1, source_target_pairs={{4,0},{8,12},{5,1},{9,13},{6,2},{10,14},{7,3},{11,15},{20,16},{24,... | collective-permute-start | bytes 3145736 | tf_op jit(solution)/shard_map/ppermute | solution.py:352
  250.6 26.9 %collective-permute-start.35 = (bf16[16,128,128]{2,1,0:T(8,128)(2,1)S(1)}, bf16[16,128,128]{2,1,0:T(8,128)(2,1)S(1)}, u32[]{:S(2)}, u32[]{:S(2)}) collective-permute-start(bf16[16,128,128]{2,1,0:T(8,128)(2,1)S(1)} %pack.10), channel_id=1, source_target_pairs={{4,8},{8,4},{5,9},{9,5},{6,10},{10,6},{7,11},{11,7},{20,24},{24,20... | collective-permute-start | bytes 1572872 | tf_op jit(solution)/shard_map/ppermute | solution.py:352
  255.7 32.0 %collective-permute-start.39 = (bf16[256,8,128]{2,1,0:T(8,128)(2,1)}, bf16[256,8,128]{2,1,0:T(8,128)(2,1)S(1)}, u32[]{:S(2)}, u32[]{:S(2)}) collective-permute-start(bf16[256,8,128]{2,1,0:T(8,128)(2,1)} %get-tuple-element.243), channel_id=1, source_target_pairs={{4,0},{8,12},{5,1},{9,13},{6,2},{10,14},{7,3},{11,15},{20,16},{24,... | collective-permute-start | bytes 1572872 | tf_op jit(solution)/shard_map/ppermute | solution.py:352
  (62 other events, 1269.2 us)

commit v5 on v4

--- a/solution.py
+++ b/solution.py
@@ -272,7 +272,7 @@
     tiles = width // TILE
     raw = RAW_TILES * TILE
     early = raw + TILE
-    late_widths = [TILE] * (tiles - RAW_TILES - 2) + [TILE // 2] * 2
+    late_widths = [TILE] * (tiles - RAW_TILES - 1)
     late = len(late_widths)
     late_first = [early + sum(late_widths[:q]) for q in range(late)]
     z = lax.axis_index("freq")

time: 297 us -> 297 us (level)
  waiting for transfers between devices: 105 us -> 118 us
  starting transfers between devices: 77.3 us -> 69.1 us
  Pallas kernels: 86.5 us -> 83.5 us
    ppermute x34 -> x31, waiting for transfers between devices: 86.8 us -> 98.6 us  [line_body(): send = lambda a, pairs: lax.ppermute(a, 'freq', pairs)]
    ppermute x34 -> x31, starting transfers between devices: 72.7 us -> 64.4 us  [line_body(): send = lambda a, pairs: lax.ppermute(a, 'freq', pairs)]
    pallas_call x8 -> x7, Pallas kernels: 34.4 us -> 31.8 us  [time_call(): pl.pallas_call(partial(time_kernel, plan, blocks, aliased), grid=(grid,),...]
    unnamed x93 -> x87, local copies, waits for them, and re-layouts: 14.4 us -> 12.5 us
    pallas_call x7 -> x6, Pallas kernels: 9.27 us -> 8.61 us  [place(): pl.pallas_call(partial(place_kernel, late_first[j - 1] if j else raw), in...]
  transfers between devices with their start and end apart: 40 -> 37, of which waited for: 20 -> 17; matrix products, arithmetic and copies ran while one was open for 3% -> 3% of each run, Pallas kernels for 28% -> 27%
where the time goes in v5:
time: 297 us; the launch traced here: 295 us
  waiting for transfers between devices  118 us (40%)
  Pallas kernels  83.5 us (28%)
  starting transfers between devices  69.1 us (23%)
  local copies, waits for them, and re-layouts  15.1 us (5%)
  other arithmetic  6.93 us (2%)
    ppermute x31, waiting for transfers between devices, line_body(): send = lambda a, pairs: lax.ppermute(a, 'freq', pairs)  98.6 us
    ppermute x31, starting transfers between devices, line_body(): send = lambda a, pairs: lax.ppermute(a, 'freq', pairs)  64.4 us
    pallas_call x7, Pallas kernels, time_call(): pl.pallas_call(partial(time_kernel, plan, blocks, aliased), grid=(grid,),...  31.8 us
    ppermute x3, waiting for transfers between devices, line_body(): others = [lax.ppermute(a, 'shot', ((0, 1), (1, 0))) for a in downs]  16.2 us
    unnamed x87, local copies, waits for them, and re-layouts  12.5 us
    pallas_call x3, Pallas kernels, line_body(): kernel(rows_kernel, SIZES[k], in_specs=[whole(SMEM), pl.BlockSpec((2, OCT...  12.1 us
    pallas_call x3, Pallas kernels, line_body(): kernel(partial(down_kernel, first_group[k] * OCT), SIZES[k], in_specs=[pl...  9.26 us
    pallas_call x6, Pallas kernels, place(): pl.pallas_call(partial(place_kernel, late_first[j - 1] if j else raw), in...  8.61 us
  transfers between devices with their start and end apart: 37, of which 17 were waited for; matrix products, arithmetic and copies ran while one was open for 3% of the time, Pallas kernels for 27%

profile of v5, /device:TPU:0, one launch (start us, length us, event | category | flops | bytes accessed | tf_op | source)
XLA Modules:
  0.0 295.0 jit_solution(6603555489337362678)
XLA Ops:
  10.8 4.4 %rows.4 = (bf16[3,128,2048]{2,1,0:T(8,128)(2,1)}, f32[3,128,128]{2,1,0:T(8,128)}, f32[3,2,64,128]{3,2,1,0:T(8,128)}) custom-call(s32[1]{0:T(128)} %bitcast.6.side_ref, bf16[2,64,8,2048]{3,2,1,0:T(8,128)(2,1)} %est_ref.5, bf16[2,64,8,16]{3,2,1,0:T(8,128)(2,1)} %copy.31.win_ref, bf16[3,128,2048]{2,1,0:T(8,128)(2,1)} %down.4.down_ref.own_ref), custom_call_target="tpu_custom_call" | custom-call | tf_op jit(solution)/shard_map/rows/pallas_call | solution.py:328
  19.4 5.6 %fusion.3.table_ref = bf16[512,512]{1,0:T(8,128)(2,1)} fusion(s32[512]{0:T(512)S(1)} %mul.40, s32[512]{0:T(512)S(1)} %pad_add_fusion, pred[512]{0:T(512)(128)(4,1)S(1)} %fusion.5), kind=kLoop, calls=%fused_computation.10 | loop fusion | flops 5505024 | bytes 528896 | tf_op jit(solution)/shard_map/mul | solution.py:296
  25.0 5.5 %collective-permute-done.other_ref = bf16[2,128,2048]{2,1,0:T(8,128)(2,1)S(1)} collective-permute-done((bf16[2,128,2048]{2,1,0:T(8,128)(2,1)}, bf16[2,128,2048]{2,1,0:T(8,128)(2,1)S(1)}, u32[]{:S(2)}, u32[]{:S(2)}) %collective-permute-start) | collective-permute-done | bytes 1048608 | tf_op jit(solution)/shard_map/ppermute | solution.py:325
  47.7 4.4 %rows.5 = (bf16[3,128,2048]{2,1,0:T(8,128)(2,1)}, f32[3,128,128]{2,1,0:T(8,128)}, f32[3,2,64,128]{3,2,1,0:T(8,128)}) custom-call(s32[1]{0:T(128)} %bitcast.6.side_ref, bf16[2,64,8,2048]{3,2,1,0:T(8,128)(2,1)} %est_ref.5, bf16[2,64,8,16]{3,2,1,0:T(8,128)(2,1)} %copy.31.win_ref, bf16[3,128,2048]{2,1,0:T(8,128)(2,1)} %down.5.down_ref.own_ref), custom_call_target="tpu_custom_call" | custom-call | tf_op jit(solution)/shard_map/rows/pallas_call | solution.py:328
  55.3 9.0 %collective-permute-done.4.other_ref = bf16[3,128,2048]{2,1,0:T(8,128)(2,1)} collective-permute-done((bf16[3,128,2048]{2,1,0:T(8,128)(2,1)}, bf16[3,128,2048]{2,1,0:T(8,128)(2,1)}, u32[]{:S(2)}, u32[]{:S(2)}) %collective-permute-start.4) | collective-permute-done | bytes 1572896 | tf_op jit(solution)/shard_map/ppermute | solution.py:325
  79.2 12.9 %collective-permute-done.9.rest_4_ = bf16[3,128,768]{2,1,0:T(8,128)(2,1)S(1)} collective-permute-done((bf16[3,128,768]{2,1,0:T(8,128)(2,1)S(1)}, bf16[3,128,768]{2,1,0:T(8,128)(2,1)S(1)}, u32[]{:S(2)}, u32[]{:S(2)}) %collective-permute-start.9) | collective-permute-done | bytes 589856 | tf_op jit(solution)/shard_map/ppermute | solution.py:352
  113.4 13.0 %collective-permute-done.15.rest_5_ = bf16[3,128,768]{2,1,0:T(8,128)(2,1)S(1)} collective-permute-done((bf16[3,128,768]{2,1,0:T(8,128)(2,1)S(1)}, bf16[3,128,768]{2,1,0:T(8,128)(2,1)S(1)}, u32[]{:S(2)}, u32[]{:S(2)}) %collective-permute-start.15) | collective-permute-done | bytes 589856 | tf_op jit(solution)/shard_map/ppermute | solution.py:352
  128.5 4.6 %collective-permute-start.16 = (bf16[8,128,256]{2,1,0:T(8,128)(2,1)S(1)}, bf16[8,128,256]{2,1,0:T(8,128)(2,1)S(1)}, u32[]{:S(2)}, u32[]{:S(2)}) collective-permute-start(bf16[8,128,256]{2,1,0:T(8,128)(2,1)S(1)} %get-tuple-element.159.a_ref.rest_0_), channel_id=1, source_target_pairs={{0,4},{12,8},{1,5},{13,9},{2,6},{14,10},{3,7},{15,11},{16,20},{28,... | collective-permute-start | bytes 1572872 | tf_op jit(solution)/shard_map/ppermute | solution.py:352
  134.5 6.4 %collective-permute-done.19.rest_15_ = bf16[3,128,512]{2,1,0:T(8,128)(2,1)S(1)} collective-permute-done((bf16[3,128,512]{2,1,0:T(8,128)(2,1)S(1)}, bf16[3,128,512]{2,1,0:T(8,128)(2,1)S(1)}, u32[]{:S(2)}, u32[]{:S(2)}) %collective-permute-start.19) | collective-permute-done | bytes 393248 | tf_op jit(solution)/shard_map/ppermute | solution.py:352
  148.2 5.3 %collective-permute-start.20 = (bf16[8,128,256]{2,1,0:T(8,128)(2,1)S(1)}, bf16[8,128,256]{2,1,0:T(8,128)(2,1)S(1)}, u32[]{:S(2)}, u32[]{:S(2)}) collective-permute-start(bf16[8,128,256]{2,1,0:T(8,128)(2,1)S(1)} %get-tuple-element.169.a_ref.rest_0_), channel_id=1, source_target_pairs={{0,4},{12,8},{1,5},{13,9},{2,6},{14,10},{3,7},{15,11},{16,20},{28,... | collective-permute-start | bytes 1572872 | tf_op jit(solution)/shard_map/ppermute | solution.py:352
  161.9 4.8 %collective-permute-start.23 = (bf16[8,128,256]{2,1,0:T(8,128)(2,1)S(1)}, bf16[8,128,256]{2,1,0:T(8,128)(2,1)S(1)}, u32[]{:S(2)}, u32[]{:S(2)}) collective-permute-start(bf16[8,128,256]{2,1,0:T(8,128)(2,1)S(1)} %get-tuple-element.174.a_ref.rest_0_), channel_id=1, source_target_pairs={{0,4},{12,8},{1,5},{13,9},{2,6},{14,10},{3,7},{15,11},{16,20},{28,... | collective-permute-start | bytes 1572872 | tf_op jit(solution)/shard_map/ppermute | solution.py:352
  169.4 5.3 %collective-permute-done.23.b_ref.rest_1_ = bf16[8,128,256]{2,1,0:T(8,128)(2,1)S(1)} collective-permute-done((bf16[8,128,256]{2,1,0:T(8,128)(2,1)S(1)}, bf16[8,128,256]{2,1,0:T(8,128)(2,1)S(1)}, u32[]{:S(2)}, u32[]{:S(2)}) %collective-permute-start.23) | collective-permute-done | bytes 524320 | tf_op jit(solution)/shard_map/ppermute | solution.py:352
  174.7 4.7 %time_late.5 = (bf16[256,8,2048]{2,1,0:T(8,128)(2,1)}, bf16[256,8,256]{2,1,0:T(8,128)(2,1)}) custom-call(f32[1]{0:T(128)S(6)} %div.11.level_ref, bf16[512,512]{1,0:T(8,128)(2,1)} %fusion.3.table_ref, bf16[8,128,256]{2,1,0:T(8,128)(2,1)} %copy-done.3, bf16[8,128,256]{2,1,0:T(8,128)(2,1)} %copy-done.22, ...), custom_call_target="tpu_custom_call", output_to_operand_aliasing={{0}: (5, {})} | custom-call | tf_op jit(solution)/shard_map/time_late/pallas_call | solution.py:429
  182.9 7.2 %collective-permute-start.27 = (bf16[8,128,256]{2,1,0:T(8,128)(2,1)S(1)}, bf16[8,128,256]{2,1,0:T(8,128)(2,1)S(1)}, u32[]{:S(2)}, u32[]{:S(2)}) collective-permute-start(bf16[8,128,256]{2,1,0:T(8,128)(2,1)S(1)} %get-tuple-element.184.a_ref.rest_0_), channel_id=1, source_target_pairs={{0,4},{12,8},{1,5},{13,9},{2,6},{14,10},{3,7},{15,11},{16,20},{28,... | collective-permute-start | bytes 1572872 | tf_op jit(solution)/shard_map/ppermute | solution.py:352
  192.8 5.0 %time_raw.1.rest_3_ = bf16[256,8,2048]{2,1,0:T(8,128)(2,1)} custom-call(f32[1]{0:T(128)S(6)} %div.11.level_ref, bf16[512,512]{1,0:T(8,128)(2,1)} %fusion.3.table_ref, bf16[2,128,768]{2,1,0:T(8,128)(2,1)} %copy-done.18, bf16[3,128,768]{2,1,0:T(8,128)(2,1)} %copy-done.13, bf16[3,128,768]{2,1,0:T(8,128)(2,1)} %copy-done.14, ...), custom_call_target="tpu_custom_call", output_to_operand_aliasing={{}: (20, {})} | custom-call | tf_op jit(solution)/shard_map/time_raw/pallas_call | solution.py:429
  197.8 4.7 %time_late.6 = (bf16[256,8,2048]{2,1,0:T(8,128)(2,1)}, bf16[256,8,256]{2,1,0:T(8,128)(2,1)}) custom-call(f32[1]{0:T(128)S(6)} %div.11.level_ref, bf16[512,512]{1,0:T(8,128)(2,1)} %fusion.3.table_ref, bf16[8,128,256]{2,1,0:T(8,128)(2,1)} %copy-done.4, bf16[8,128,256]{2,1,0:T(8,128)(2,1)} %copy-done.20, ...), custom_call_target="tpu_custom_call", output_to_operand_aliasing={{0}: (5, {})} | custom-call | tf_op jit(solution)/shard_map/time_late/pallas_call | solution.py:429
  205.0 9.6 %collective-permute-start.30 = (bf16[8,128,256]{2,1,0:T(8,128)(2,1)S(1)}, bf16[8,128,256]{2,1,0:T(8,128)(2,1)S(1)}, u32[]{:S(2)}, u32[]{:S(2)}) collective-permute-start(bf16[8,128,256]{2,1,0:T(8,128)(2,1)S(1)} %copy-done.10), channel_id=1, source_target_pairs={{0,4},{12,8},{1,5},{13,9},{2,6},{14,10},{3,7},{15,11},{16,20},{28,... | collective-permute-start | bytes 1572872 | tf_op jit(solution)/shard_map/ppermute | solution.py:352
  216.3 4.9 %collective-permute-done.30.b_ref.rest_1_ = bf16[8,128,256]{2,1,0:T(8,128)(2,1)S(1)} collective-permute-done((bf16[8,128,256]{2,1,0:T(8,128)(2,1)S(1)}, bf16[8,128,256]{2,1,0:T(8,128)(2,1)S(1)}, u32[]{:S(2)}, u32[]{:S(2)}) %collective-permute-start.30) | collective-permute-done | bytes 524320 | tf_op jit(solution)/shard_map/ppermute | solution.py:352
  221.2 4.7 %time_late.7 = (bf16[256,8,2048]{2,1,0:T(8,128)(2,1)}, bf16[256,8,256]{2,1,0:T(8,128)(2,1)}) custom-call(f32[1]{0:T(128)S(6)} %div.11.level_ref, bf16[512,512]{1,0:T(8,128)(2,1)} %fusion.3.table_ref, bf16[8,128,256]{2,1,0:T(8,128)(2,1)} %copy-done.5, bf16[8,128,256]{2,1,0:T(8,128)(2,1)} %copy-done.19, ...), custom_call_target="tpu_custom_call", output_to_operand_aliasing={{0}: (5, {})} | custom-call | tf_op jit(solution)/shard_map/time_late/pallas_call | solution.py:429
  232.1 4.5 %time_late.8 = (bf16[256,8,2048]{2,1,0:T(8,128)(2,1)}, bf16[256,8,256]{2,1,0:T(8,128)(2,1)}) custom-call(f32[1]{0:T(128)S(6)} %div.11.level_ref, bf16[512,512]{1,0:T(8,128)(2,1)} %fusion.3.table_ref, bf16[8,128,256]{2,1,0:T(8,128)(2,1)} %copy-done.6, bf16[8,128,256]{2,1,0:T(8,128)(2,1)} %copy-done.21, ...), custom_call_target="tpu_custom_call", output_to_operand_aliasing={{0}: (5, {})} | custom-call | tf_op jit(solution)/shard_map/time_late/pallas_call | solution.py:429
  237.9 11.1 %collective-permute-done.33.got_ref = bf16[256,8,256]{2,1,0:T(8,128)(2,1)S(1)} collective-permute-done((bf16[256,8,256]{2,1,0:T(8,128)(2,1)}, bf16[256,8,256]{2,1,0:T(8,128)(2,1)S(1)}, u32[]{:S(2)}, u32[]{:S(2)}) %collective-permute-start.33) | collective-permute-done | bytes 1048608 | tf_op jit(solution)/shard_map/ppermute | solution.py:352
  250.0 4.5 %time_late.9 = (bf16[256,8,2048]{2,1,0:T(8,128)(2,1)}, bf16[256,8,256]{2,1,0:T(8,128)(2,1)}) custom-call(f32[1]{0:T(128)S(6)} %div.11.level_ref, bf16[512,512]{1,0:T(8,128)(2,1)} %fusion.3.table_ref, bf16[8,128,256]{2,1,0:T(8,128)(2,1)} %copy-done.9, bf16[8,128,256]{2,1,0:T(8,128)(2,1)} %copy-done.23, ...), custom_call_target="tpu_custom_call", output_to_operand_aliasing={{0}: (5, {})} | custom-call | tf_op jit(solution)/shard_map/time_late/pallas_call | solution.py:429
  255.8 15.6 %collective-permute-done.36.got_ref = bf16[256,8,256]{2,1,0:T(8,128)(2,1)S(1)} collective-permute-done((bf16[256,8,256]{2,1,0:T(8,128)(2,1)}, bf16[256,8,256]{2,1,0:T(8,128)(2,1)S(1)}, u32[]{:S(2)}, u32[]{:S(2)}) %collective-permute-start.36) | collective-permute-done | bytes 1048608 | tf_op jit(solution)/shard_map/ppermute | solution.py:352
  272.5 21.3 %collective-permute-done.35.got_ref = bf16[256,8,256]{2,1,0:T(8,128)(2,1)S(1)} collective-permute-done((bf16[256,8,256]{2,1,0:T(8,128)(2,1)}, bf16[256,8,256]{2,1,0:T(8,128)(2,1)S(1)}, u32[]{:S(2)}, u32[]{:S(2)}) %collective-permute-start.35) | collective-permute-done | bytes 1048608 | tf_op jit(solution)/shard_map/ppermute | solution.py:352
  (185 shorter events, 113.7 us)
Async XLA Ops:
  3.4 27.1 %collective-permute-start = (bf16[2,128,2048]{2,1,0:T(8,128)(2,1)}, bf16[2,128,2048]{2,1,0:T(8,128)(2,1)S(1)}, u32[]{:S(2)}, u32[]{:S(2)}) collective-permute-start(bf16[2,128,2048]{2,1,0:T(8,128)(2,1)} %down.3.down_ref.own_ref), channel_id=1, source_target_pairs={{0,2},{2,0},{1,3},{3,1},{4,6},{6,4},{5,7},{7,5},{8,10},{10,8},{9,1... | collective-permute-start | bytes 3145736 | tf_op jit(solution)/shard_map/ppermute | solution.py:325
  9.9 54.5 %collective-permute-start.4 = (bf16[3,128,2048]{2,1,0:T(8,128)(2,1)}, bf16[3,128,2048]{2,1,0:T(8,128)(2,1)}, u32[]{:S(2)}, u32[]{:S(2)}) collective-permute-start(bf16[3,128,2048]{2,1,0:T(8,128)(2,1)} %down.4.down_ref.own_ref), channel_id=1, source_target_pairs={{0,2},{2,0},{1,3},{3,1},{4,6},{6,4},{5,7},{7,5},{8,10},{10,8},{9,1... | collective-permute-start | bytes 4718600 | tf_op jit(solution)/shard_map/ppermute | solution.py:325
  46.3 50.9 %collective-permute-start.3 = (bf16[3,128,2048]{2,1,0:T(8,128)(2,1)}, bf16[3,128,2048]{2,1,0:T(8,128)(2,1)}, u32[]{:S(2)}, u32[]{:S(2)}) collective-permute-start(bf16[3,128,2048]{2,1,0:T(8,128)(2,1)} %down.5.down_ref.own_ref), channel_id=1, source_target_pairs={{0,2},{2,0},{1,3},{3,1},{4,6},{6,4},{5,7},{7,5},{8,10},{10,8},{9,1... | collective-permute-start | bytes 4718600 | tf_op jit(solution)/shard_map/ppermute | solution.py:325
  52.2 24.1 %collective-permute-start.7 = (bf16[2,128,768]{2,1,0:T(8,128)(2,1)}, bf16[2,128,768]{2,1,0:T(8,128)(2,1)S(1)}, u32[]{:S(2)}, u32[]{:S(2)}) collective-permute-start(bf16[2,128,768]{2,1,0:T(8,128)(2,1)} %collective-permute-done.2.rest_3_), channel_id=1, source_target_pairs={{4,8},{8,4},{5,9},{9,5},{6,10},{10,6},{7,11},{11,7},{20,24},{24,20... | collective-permute-start | bytes 1179656 | tf_op jit(solution)/shard_map/ppermute | solution.py:352
  54.0 22.3 %collective-permute-start.8 = (bf16[2,128,512]{2,1,0:T(8,128)(2,1)S(1)}, bf16[2,128,512]{2,1,0:T(8,128)(2,1)S(1)}, u32[]{:S(2)}, u32[]{:S(2)}) collective-permute-start(bf16[2,128,512]{2,1,0:T(8,128)(2,1)S(1)} %slice.26), channel_id=1, source_target_pairs={{4,0},{8,12},{5,1},{9,13},{6,2},{10,14},{7,3},{11,15},{20,16},{24,... | collective-permute-start | bytes 786440 | tf_op jit(solution)/shard_map/ppermute | solution.py:352
  76.3 15.8 %collective-permute-start.9 = (bf16[3,128,768]{2,1,0:T(8,128)(2,1)S(1)}, bf16[3,128,768]{2,1,0:T(8,128)(2,1)S(1)}, u32[]{:S(2)}, u32[]{:S(2)}) collective-permute-start(bf16[3,128,768]{2,1,0:T(8,128)(2,1)S(1)} %get-tuple-element.141.rest_1_), channel_id=1, source_target_pairs={{0,4},{4,0},{8,12},{12,8},{1,5},{5,1},{9,13},{13,9},{2,6},{6,2},{1... | collective-permute-start | bytes 1769480 | tf_op jit(solution)/shard_map/ppermute | solution.py:352
  92.9 15.8 %collective-permute-start.13 = (bf16[3,128,512]{2,1,0:T(8,128)(2,1)S(1)}, bf16[3,128,512]{2,1,0:T(8,128)(2,1)S(1)}, u32[]{:S(2)}, u32[]{:S(2)}) collective-permute-start(bf16[3,128,512]{2,1,0:T(8,128)(2,1)S(1)} %slice.27), channel_id=1, source_target_pairs={{4,0},{8,12},{5,1},{9,13},{6,2},{10,14},{7,3},{11,15},{20,16},{24,... | collective-permute-start | bytes 1179656 | tf_op jit(solution)/shard_map/ppermute | solution.py:352
  94.2 18.5 %collective-permute-start.14 = (bf16[2,128,512]{2,1,0:T(8,128)(2,1)S(1)}, bf16[2,128,512]{2,1,0:T(8,128)(2,1)S(1)}, u32[]{:S(2)}, u32[]{:S(2)}) collective-permute-start(bf16[2,128,512]{2,1,0:T(8,128)(2,1)S(1)} %slice.20), channel_id=1, source_target_pairs={{4,0},{8,12},{5,1},{9,13},{6,2},{10,14},{7,3},{11,15},{20,16},{24,... | collective-permute-start | bytes 786440 | tf_op jit(solution)/shard_map/ppermute | solution.py:352
  112.7 20.4 %collective-permute-start.17 = (bf16[3,128,768]{2,1,0:T(8,128)(2,1)S(1)}, bf16[3,128,768]{2,1,0:T(8,128)(2,1)S(1)}, u32[]{:S(2)}, u32[]{:S(2)}) collective-permute-start(bf16[3,128,768]{2,1,0:T(8,128)(2,1)S(1)} %get-tuple-element.157.rest_2_), channel_id=1, source_target_pairs={{4,8},{8,4},{5,9},{9,5},{6,10},{10,6},{7,11},{11,7},{20,24},{24,20... | collective-permute-start | bytes 1769480 | tf_op jit(solution)/shard_map/ppermute | solution.py:352
  128.5 19.7 %collective-permute-start.16 = (bf16[8,128,256]{2,1,0:T(8,128)(2,1)S(1)}, bf16[8,128,256]{2,1,0:T(8,128)(2,1)S(1)}, u32[]{:S(2)}, u32[]{:S(2)}) collective-permute-start(bf16[8,128,256]{2,1,0:T(8,128)(2,1)S(1)} %get-tuple-element.159.a_ref.rest_0_), channel_id=1, source_target_pairs={{0,4},{12,8},{1,5},{13,9},{2,6},{14,10},{3,7},{15,11},{16,20},{28,... | collective-permute-start | bytes 1572872 | tf_op jit(solution)/shard_map/ppermute | solution.py:352
  133.2 23.0 %collective-permute-start.24 = (bf16[3,128,512]{2,1,0:T(8,128)(2,1)S(1)}, bf16[3,128,512]{2,1,0:T(8,128)(2,1)}, u32[]{:S(2)}, u32[]{:S(2)}) collective-permute-start(bf16[3,128,512]{2,1,0:T(8,128)(2,1)S(1)} %slice.28), channel_id=1, source_target_pairs={{4,0},{8,12},{5,1},{9,13},{6,2},{10,14},{7,3},{11,15},{20,16},{24,... | collective-permute-start | bytes 1179656 | tf_op jit(solution)/shard_map/ppermute | solution.py:352
  154.5 20.1 %collective-permute-start.22 = (bf16[16,128,256]{2,1,0:T(8,128)(2,1)}, bf16[16,128,256]{2,1,0:T(8,128)(2,1)}, u32[]{:S(2)}, u32[]{:S(2)}) collective-permute-start(bf16[16,128,256]{2,1,0:T(8,128)(2,1)} %pack.6), channel_id=1, source_target_pairs={{4,8},{8,4},{5,9},{9,5},{6,10},{10,6},{7,11},{11,7},{20,24},{24,20... | collective-permute-start | bytes 3145736 | tf_op jit(solution)/shard_map/ppermute | solution.py:352
  156.2 24.5 %collective-permute-start.26 = (bf16[256,8,256]{2,1,0:T(8,128)(2,1)}, bf16[256,8,256]{2,1,0:T(8,128)(2,1)}, u32[]{:S(2)}, u32[]{:S(2)}) collective-permute-start(bf16[256,8,256]{2,1,0:T(8,128)(2,1)} %time_theirs.1), channel_id=1, source_target_pairs={{4,0},{8,12},{5,1},{9,13},{6,2},{10,14},{7,3},{11,15},{20,16},{24,... | collective-permute-start | bytes 3145736 | tf_op jit(solution)/shard_map/ppermute | solution.py:352
  167.7 30.0 %collective-permute-start.21 = (bf16[16,128,256]{2,1,0:T(8,128)(2,1)}, bf16[16,128,256]{2,1,0:T(8,128)(2,1)}, u32[]{:S(2)}, u32[]{:S(2)}) collective-permute-start(bf16[16,128,256]{2,1,0:T(8,128)(2,1)} %pack.5), channel_id=1, source_target_pairs={{4,8},{8,4},{5,9},{9,5},{6,10},{10,6},{7,11},{11,7},{20,24},{24,20... | collective-permute-start | bytes 3145736 | tf_op jit(solution)/shard_map/ppermute | solution.py:352
  179.4 24.4 %collective-permute-start.28 = (bf16[256,8,256]{2,1,0:T(8,128)(2,1)}, bf16[256,8,256]{2,1,0:T(8,128)(2,1)S(1)}, u32[]{:S(2)}, u32[]{:S(2)}) collective-permute-start(bf16[256,8,256]{2,1,0:T(8,128)(2,1)} %get-tuple-element.186), channel_id=1, source_target_pairs={{4,0},{8,12},{5,1},{9,13},{6,2},{10,14},{7,3},{11,15},{20,16},{24,... | collective-permute-start | bytes 3145736 | tf_op jit(solution)/shard_map/ppermute | solution.py:352
  182.9 14.8 %collective-permute-start.27 = (bf16[8,128,256]{2,1,0:T(8,128)(2,1)S(1)}, bf16[8,128,256]{2,1,0:T(8,128)(2,1)S(1)}, u32[]{:S(2)}, u32[]{:S(2)}) collective-permute-start(bf16[8,128,256]{2,1,0:T(8,128)(2,1)S(1)} %get-tuple-element.184.a_ref.rest_0_), channel_id=1, source_target_pairs={{0,4},{12,8},{1,5},{13,9},{2,6},{14,10},{3,7},{15,11},{16,20},{28,... | collective-permute-start | bytes 1572872 | tf_op jit(solution)/shard_map/ppermute | solution.py:352
  191.1 25.2 %collective-permute-start.29 = (bf16[16,128,256]{2,1,0:T(8,128)(2,1)}, bf16[16,128,256]{2,1,0:T(8,128)(2,1)}, u32[]{:S(2)}, u32[]{:S(2)}) collective-permute-start(bf16[16,128,256]{2,1,0:T(8,128)(2,1)} %pack.7), channel_id=1, source_target_pairs={{4,8},{8,4},{5,9},{9,5},{6,10},{10,6},{7,11},{11,7},{20,24},{24,20... | collective-permute-start | bytes 3145736 | tf_op jit(solution)/shard_map/ppermute | solution.py:352
  202.5 24.8 %collective-permute-start.31 = (bf16[256,8,256]{2,1,0:T(8,128)(2,1)}, bf16[256,8,256]{2,1,0:T(8,128)(2,1)}, u32[]{:S(2)}, u32[]{:S(2)}) collective-permute-start(bf16[256,8,256]{2,1,0:T(8,128)(2,1)} %get-tuple-element.202), channel_id=1, source_target_pairs={{4,0},{8,12},{5,1},{9,13},{6,2},{10,14},{7,3},{11,15},{20,16},{24,... | collective-permute-start | bytes 3145736 | tf_op jit(solution)/shard_map/ppermute | solution.py:352
  205.0 16.3 %collective-permute-start.30 = (bf16[8,128,256]{2,1,0:T(8,128)(2,1)S(1)}, bf16[8,128,256]{2,1,0:T(8,128)(2,1)S(1)}, u32[]{:S(2)}, u32[]{:S(2)}) collective-permute-start(bf16[8,128,256]{2,1,0:T(8,128)(2,1)S(1)} %copy-done.10), channel_id=1, source_target_pairs={{0,4},{12,8},{1,5},{13,9},{2,6},{14,10},{3,7},{15,11},{16,20},{28,... | collective-permute-start | bytes 1572872 | tf_op jit(solution)/shard_map/ppermute | solution.py:352
  214.7 17.4 %collective-permute-start.34 = (bf16[16,128,256]{2,1,0:T(8,128)(2,1)S(1)}, bf16[16,128,256]{2,1,0:T(8,128)(2,1)}, u32[]{:S(2)}, u32[]{:S(2)}) collective-permute-start(bf16[16,128,256]{2,1,0:T(8,128)(2,1)S(1)} %pack.9), channel_id=1, source_target_pairs={{4,8},{8,4},{5,9},{9,5},{6,10},{10,6},{7,11},{11,7},{20,24},{24,20... | collective-permute-start | bytes 3145736 | tf_op jit(solution)/shard_map/ppermute | solution.py:352
  225.9 23.1 %collective-permute-start.33 = (bf16[256,8,256]{2,1,0:T(8,128)(2,1)}, bf16[256,8,256]{2,1,0:T(8,128)(2,1)S(1)}, u32[]{:S(2)}, u32[]{:S(2)}) collective-permute-start(bf16[256,8,256]{2,1,0:T(8,128)(2,1)} %get-tuple-element.210), channel_id=1, source_target_pairs={{4,0},{8,12},{5,1},{9,13},{6,2},{10,14},{7,3},{11,15},{20,16},{24,... | collective-permute-start | bytes 3145736 | tf_op jit(solution)/shard_map/ppermute | solution.py:352
  230.5 19.6 %collective-permute-start.32 = (bf16[16,128,256]{2,1,0:T(8,128)(2,1)}, bf16[16,128,256]{2,1,0:T(8,128)(2,1)}, u32[]{:S(2)}, u32[]{:S(2)}) collective-permute-start(bf16[16,128,256]{2,1,0:T(8,128)(2,1)} %pack.8), channel_id=1, source_target_pairs={{4,8},{8,4},{5,9},{9,5},{6,10},{10,6},{7,11},{11,7},{20,24},{24,20... | collective-permute-start | bytes 3145736 | tf_op jit(solution)/shard_map/ppermute | solution.py:352
  236.6 34.9 %collective-permute-start.36 = (bf16[256,8,256]{2,1,0:T(8,128)(2,1)}, bf16[256,8,256]{2,1,0:T(8,128)(2,1)S(1)}, u32[]{:S(2)}, u32[]{:S(2)}) collective-permute-start(bf16[256,8,256]{2,1,0:T(8,128)(2,1)} %get-tuple-element.217), channel_id=1, source_target_pairs={{4,0},{8,12},{5,1},{9,13},{6,2},{10,14},{7,3},{11,15},{20,16},{24,... | collective-permute-start | bytes 3145736 | tf_op jit(solution)/shard_map/ppermute | solution.py:352
  254.6 39.3 %collective-permute-start.35 = (bf16[256,8,256]{2,1,0:T(8,128)(2,1)}, bf16[256,8,256]{2,1,0:T(8,128)(2,1)S(1)}, u32[]{:S(2)}, u32[]{:S(2)}) collective-permute-start(bf16[256,8,256]{2,1,0:T(8,128)(2,1)} %get-tuple-element.216), channel_id=1, source_target_pairs={{4,0},{8,12},{5,1},{9,13},{6,2},{10,14},{7,3},{11,15},{20,16},{24,... | collective-permute-start | bytes 3145736 | tf_op jit(solution)/shard_map/ppermute | solution.py:352
  (56 other events, 1173.1 us)
